TPU v7x, 32 devices: a whole 2x2x4 slice. The times are simulated.
32 devices in a mesh: groups: 2 (over x), dp: 8 (over z, y), tensor: 2 (over core).
Axes of the slice: x: 2, y: 2, z: 4, core: 2. Of those that a mesh axis runs over, the one named last changes fastest.
Arguments:
- tokens: bfloat16 [16384, 8192], P(('groups', 'dp'), 'tensor'), parts along dimension 0, may hold values from -6 to 6
- base_weight: bfloat16 [8192, 1024], P('tensor', 'dp'), may hold values from -0.0625 to 0.0625
- adapt_a: bfloat16 [64, 32, 8192], P(('groups', 'dp'), None, 'tensor'), parts along dimension 0, may hold values from -0.0625 to 0.0625
- adapt_b: bfloat16 [64, 32, 1024], P(('groups', 'dp')), parts along dimension 0, may hold values from -1 to 1
- cotangent: bfloat16 [16384, 1024], P(('groups', 'dp'), 'tensor'), parts along dimension 0, may hold values from -6 to 6
- row_tenant: int32 [16384], P(('groups', 'dp')), parts along dimension 0, may hold values from 0 to 32, as said below
- adapter_slot: int32 [64], P('groups'), parts along dimension 0, may hold values from 0 to 31, as said below
Outputs:
- proj_out: bfloat16 [16384, 1024], P(('groups', 'dp'), 'tensor'), parts along dimension 0
- grad_a: bfloat16 [64, 32, 8192], P(('groups', 'dp'), None, 'tensor'), parts along dimension 0
- grad_b: bfloat16 [64, 32, 1024], P(('groups', 'dp'), None, 'tensor'), parts along dimension 0
There are 2 independent parts, one for each index of `groups`. A program takes and returns all parts, laid end to end along the dimension named above; an argument that names none is the same for every part. Nothing has to cross between parts.
Inputs may be any that keep to these rules, and one draw needn't show every extreme that they name: `row_tenant`: each block of 128 rows holds one tenant's rows first (the first row always), then padding rows marked 32; the first block of every device uses an adapter on one common device, and the other blocks of a device use adapters on pairwise different devices other than that one. `adapter_slot`: A permutation of the slots.
All inputs are finite; a program needn't handle non-finite values.
Results may differ from a plain program's by a relative error of at most 0.0057.
Values may be sent and summed in bfloat16 or wider, within the bound.
No kernel may reach another device: no remote copies, remote signals or barrier semaphores. Data moves between devices by JAX's collectives and lax.ppermute only.
A program may use at most 128 MiB of HBM per device.

v0:
```python
import jax
import jax.numpy as jnp
from jax import lax
from jax.sharding import PartitionSpec as P

BLOCK = 128


ADAPTER_SCALING = 2.0


def shards(tokens, base_weight, adapt_a, adapt_b, cotangent, row_tenant, adapter_slot):
    rows, half_width = tokens.shape
    ten_dev = adapt_a.shape[0]
    output_columns = cotangent.shape[1]
    tenants_all = adapter_slot.shape[0]
    peers = lax.axis_size("dp")
    blocks = rows // BLOCK
    first = row_tenant.reshape(blocks, BLOCK)[:, 0]
    table_ids = jnp.arange(tenants_all, dtype=jnp.int32)
    block_slot = jnp.sum(
        jnp.where(first[:, None] == table_ids[None, :], adapter_slot[None, :], 0), axis=1
    )
    block_home = block_slot // ten_dev
    block_local = block_slot % ten_dev
    peer_ids = jnp.arange(peers, dtype=jnp.int32)
    local_ids = jnp.arange(ten_dev, dtype=jnp.int32)
    match = block_home[:, None] == peer_ids[None, :]
    wanted = ten_dev + jnp.sum(jnp.where(match, (block_local - ten_dev)[:, None], 0), axis=0)
    asked = lax.all_to_all(wanted.reshape(peers, 1), "dp", split_axis=0, concat_axis=0, tiled=True)
    select = asked == local_ids[None, :]
    select_low = select.astype(jnp.bfloat16)
    pick = match.astype(jnp.bfloat16)
    column = lax.axis_index("tensor") * output_columns
    own_b = lax.dynamic_slice_in_dim(adapt_b, column, output_columns, 2)
    send_a = jnp.einsum(
        "ns,srd->nrd", select_low, adapt_a, preferred_element_type=jnp.float32
    ).astype(jnp.bfloat16)
    send_b = jnp.einsum(
        "ns,sro->nro", select_low, own_b, preferred_element_type=jnp.float32
    ).astype(jnp.bfloat16)
    partial_value = jnp.dot(
        tokens,
        lax.all_gather(base_weight, "dp", axis=1, tiled=True),
        preferred_element_type=jnp.float32,
    )
    got_a, got_b = (
        lax.all_to_all(send_a, "dp", split_axis=0, concat_axis=0, tiled=True),
        lax.all_to_all(send_b, "dp", split_axis=0, concat_axis=0, tiled=True),
    )
    block_down_matrix = jnp.einsum(
        "bn,nrd->brd", pick, got_a, preferred_element_type=jnp.float32
    ).astype(jnp.bfloat16)
    block_b = jnp.einsum("bn,nro->bro", pick, got_b, preferred_element_type=jnp.float32).astype(
        jnp.bfloat16
    )
    alive = (row_tenant != tenants_all).reshape(blocks, BLOCK, 1)
    token_tiles = tokens.reshape(blocks, BLOCK, half_width)
    grad_blocks = cotangent.reshape(blocks, BLOCK, output_columns)
    hidden_fraction = jnp.einsum(
        "nhc,nuc->nhu", token_tiles, block_down_matrix, preferred_element_type=jnp.float32
    )
    back_part = jnp.einsum("bko,bro->bkr", grad_blocks, block_b, preferred_element_type=jnp.float32)
    hidden_sum, back_sum = lax.psum((hidden_fraction, back_part), "tensor")
    hidden = jnp.where(alive, hidden_sum, 0.0).astype(jnp.bfloat16)
    backward_pass = jnp.where(alive, back_sum, 0.0).astype(jnp.bfloat16)
    added = ADAPTER_SCALING * jnp.einsum(
        "bkr,bro->bko", hidden, block_b, preferred_element_type=jnp.float32
    )
    summed = lax.psum_scatter(partial_value, "tensor", scatter_dimension=1, tiled=True)
    proj_out = (summed + added.reshape(rows, output_columns)).astype(jnp.bfloat16)
    part_a = (
        ADAPTER_SCALING
        * jnp.einsum("qxz,qxu->qzu", backward_pass, token_tiles, preferred_element_type=jnp.float32)
    ).astype(jnp.bfloat16)
    part_b = (
        ADAPTER_SCALING
        * jnp.einsum("bkr,bko->bro", hidden, grad_blocks, preferred_element_type=jnp.float32)
    ).astype(jnp.bfloat16)
    home_a = jnp.einsum("bn,brd->nrd", pick, part_a, preferred_element_type=jnp.float32).astype(
        jnp.bfloat16
    )
    home_b = jnp.einsum("bn,bro->nro", pick, part_b, preferred_element_type=jnp.float32).astype(
        jnp.bfloat16
    )
    came_a, came_b = (
        lax.all_to_all(home_a, "dp", split_axis=0, concat_axis=0, tiled=True),
        lax.all_to_all(home_b, "dp", split_axis=0, concat_axis=0, tiled=True),
    )
    total_a = jnp.einsum("ns,nrd->srd", select_low, came_a, preferred_element_type=jnp.float32)
    total_b = jnp.einsum("ns,nro->sro", select_low, came_b, preferred_element_type=jnp.float32)
    return (proj_out, total_a.astype(jnp.bfloat16), total_b.astype(jnp.bfloat16))


def solution(mesh):
    return jax.shard_map(
        shards,
        mesh=mesh,
        in_specs=(
            P(("groups", "dp"), "tensor"),
            P("tensor", "dp"),
            P(("groups", "dp"), None, "tensor"),
            P(("groups", "dp"), None, None),
            P(("groups", "dp"), "tensor"),
            P(("groups", "dp")),
            P("groups"),
        ),
        out_specs=(
            P(("groups", "dp"), "tensor"),
            P(("groups", "dp"), None, "tensor"),
            P(("groups", "dp"), None, "tensor"),
        ),
        check_vma=False,
    )
```

profile of v0, /device:TPU:0, one launch (start us, length us, event | category | flops | bytes accessed | tf_op | source)
XLA Modules:
  0.0 298.2 jit_solution(14797074930432138801)
XLA Ops:
  7.2 0.0 copy-start
  7.2 0.0 all-gather.2.cloned.1.call-start
  7.2 0.7 all-gather.2.cloned.1.call-update
  7.9 0.8 slice_reduce_fusion
  8.7 0.8 select_reduce_fusion.1
  9.6 0.1 select_reduce_fusion
  9.7 0.7 copy.67
  10.4 7.3 %all-to-all-start = ((s32[8,1,1]{2,1,0:T(1,128)}), s32[8,1,1]{2,1,0:T(1,128)S(1)}, u32[]{:S(2)}, u32[]{:S(2)}) async-start(s32[8,1,1]{2,1,0:T(1,128)} %copy.67), calls=%async_computation.1 | async-start | bytes 8192 | tf_op jit(solution)/shard_map/all_to_all | solution.py:30
  17.7 0.9 constant_dynamic-slice_fusion
  18.6 5.5 %all-to-all-done = s32[8,1,1]{2,1,0:T(1,128)S(1)} async-done(((s32[8,1,1]{2,1,0:T(1,128)}), s32[8,1,1]{2,1,0:T(1,128)S(1)}, u32[]{:S(2)}, u32[]{:S(2)}) %all-to-all-start) | async-done | bytes 64 | tf_op jit(solution)/shard_map/all_to_all | solution.py:30
  24.0 0.2 reduce.1
  24.3 0.3 convolution_convert_fusion.6
  24.6 0.8 copy.74
  25.4 3.4 %all-to-all-start.2 = ((bf16[8,32,512]{2,1,0:T(8,128)(2,1)}), bf16[8,32,512]{2,1,0:T(8,128)(2,1)S(1)}, u32[]{:S(2)}, u32[]{:S(2)}) async-start(bf16[8,32,512]{2,1,0:T(8,128)(2,1)} %copy.74), calls=%async_computation.3 | async-start | bytes 524288 | tf_op jit(solution)/shard_map/all_to_all | solution.py:49
  28.8 1.2 convolution_convert_fusion.2
  30.0 2.5 copy.69
  32.5 9.2 %all-to-all-done.2 = bf16[8,32,512]{2,1,0:T(8,128)(2,1)S(1)} async-done(((bf16[8,32,512]{2,1,0:T(8,128)(2,1)}), bf16[8,32,512]{2,1,0:T(8,128)(2,1)S(1)}, u32[]{:S(2)}, u32[]{:S(2)}) %all-to-all-start.2) | async-done | bytes 262176 | tf_op jit(solution)/shard_map/all_to_all | solution.py:49
  41.7 3.6 %all-to-all-start.1 = ((bf16[8,32,4096]{2,1,0:T(8,128)(2,1)}), bf16[8,32,4096]{2,1,0:T(8,128)(2,1)S(1)}, u32[]{:S(2)}, u32[]{:S(2)}) async-start(bf16[8,32,4096]{2,1,0:T(8,128)(2,1)} %copy.69), calls=%async_computation.2 | async-start | bytes 4194304 | tf_op jit(solution)/shard_map/all_to_all | solution.py:48
  45.3 0.0 reduce-scatter.2.cloned.1.call-start
  45.4 134.5 %all-gather.2.cloned.1.call-done = bf16[4096,1024]{1,0:T(8,128)(2,1)} async-done(((bf16[4096,128]{1,0:T(8,128)(2,1)}), bf16[4096,1024]{1,0:T(8,128)(2,1)}) %all-gather.2.cloned.1.call-update) | async-done | bytes 8388624 | tf_op jit(solution)/shard_map/all_gather | solution.py:44
  179.9 15.0 %fusion.38 = f32[1024,1024]{1,0:T(8,128)} fusion(bf16[1024,4096]{1,0:T(8,128)(2,1)} %param.7, bf16[4096,1024]{1,0:T(8,128)(2,1)} %all-gather.2.cloned.1.call-done), kind=kOutput, calls=%fused_computation.57 | convolution fusion | flops 8589934592 | bytes 20971520 | tf_op jit(solution)/shard_map/dot_general | solution.py:42
  194.9 0.0 reduce-scatter.2.cloned.1.call-update
  195.0 0.7 copy-done.7
  195.6 1.2 convolution_convert_fusion.5
  196.9 1.7 convolution_bitcast_fusion
  198.6 1.8 convolution_convert_fusion.1
  200.4 0.0 copy-start.1
  200.4 7.5 %fusion.8 = f32[8,128,32]{1,2,0:T(8,128)S(1)} fusion(bf16[8,128,4096]{2,1,0:T(8,128)(2,1)} %bitcast.35, bf16[8,32,4096]{2,0,1:T(8,128)(2,1)S(1)} %convolution_convert_fusion.1), kind=kOutput, calls=%fused_computation.20 | convolution fusion | flops 268435456 | bytes 10616832 | tf_op jit(solution)/shard_map/nhc,nuc->nhu/dot_general | solution.py:60
  207.9 4.2 %all-reduce.2 = (bf16[8,128,32]{1,2,0:T(8,128)(2,1)S(1)}, bf16[8,128,32]{1,2,0:T(8,128)(2,1)S(1)}) all-reduce(f32[8,128,32]{1,2,0:T(8,128)S(1)} %fusion.8, f32[8,128,32]{1,2,0:T(8,128)S(1)} %convolution_bitcast_fusion), channel_id=1, replica_groups=mesh['groups'=2,'dp'=8,'tensor'=2] {'tensor'}, use_global_device_ids=true, to_apply=%region_3.4 | all-reduce | flops 65536 | bytes 393216 | tf_op jit(solution)/shard_map/psum | solution.py:64
  212.1 0.0 copy-start.5
  212.1 0.3 fusion.7
  212.3 0.3 convolution_convert_fusion.4
  212.6 0.8 copy.83
  213.4 4.8 %all-to-all-start.4 = ((bf16[8,32,512]{2,1,0:T(8,128)(2,1)}), bf16[8,32,512]{2,1,0:T(8,128)(2,1)S(1)}, u32[]{:S(2)}, u32[]{:S(2)}) async-start(bf16[8,32,512]{2,1,0:T(8,128)(2,1)} %copy.83), calls=%async_computation.5 | async-start | bytes 524288 | tf_op jit(solution)/shard_map/all_to_all | solution.py:88
  218.2 4.6 %fusion = bf16[8,32,4096]{2,1,0:T(8,128)(2,1)S(1)} fusion(bf16[8,128,4096]{2,1,0:T(8,128)(2,1)} %bitcast.36, bf16[8,128,32]{1,2,0:T(8,128)(2,1)S(1)} %get-tuple-element.22, pred[8,128]{1,0:T(8,128)(4,1)S(1)} %compare_bitcast_fusion), kind=kOutput, calls=%fused_computation.1 | convolution fusion | flops 270565376 | bytes 10552320 | tf_op jit(solution)/shard_map/qxz,qxu->qzu/dot_general | solution.py:74
  222.8 2.4 convolution_convert_fusion
  225.2 2.5 copy.80
  227.7 0.7 copy-done.3
  228.4 6.0 %all-to-all-start.3 = ((bf16[8,32,4096]{2,1,0:T(8,128)(2,1)}), bf16[8,32,4096]{2,1,0:T(8,128)(2,1)}, u32[]{:S(2)}, u32[]{:S(2)}) async-start(bf16[8,32,4096]{2,1,0:T(8,128)(2,1)} %copy.80), calls=%async_computation.4 | async-start | bytes 4194304 | tf_op jit(solution)/shard_map/all_to_all | solution.py:87
  234.4 0.0 copy-start.4
  234.4 0.5 convolution_multiply_fusion.1
  234.9 0.5 copy-done.4
  235.4 0.3 convolution_convert_fusion.7
  235.6 0.7 copy.86
  236.3 46.4 %all-to-all-done.3 = bf16[8,32,4096]{2,1,0:T(8,128)(2,1)} async-done(((bf16[8,32,4096]{2,1,0:T(8,128)(2,1)}), bf16[8,32,4096]{2,1,0:T(8,128)(2,1)}, u32[]{:S(2)}, u32[]{:S(2)}) %all-to-all-start.3) | async-done | bytes 2097184 | tf_op jit(solution)/shard_map/all_to_all | solution.py:87
  282.7 4.1 %convolution_convert_fusion.3 = bf16[4,32,4096]{2,0,1:T(4,128)(2,1)S(1)} fusion(bf16[8,32,4096]{2,1,0:T(8,128)(2,1)} %all-to-all-done.3, s32[8]{0:T(128)S(1)} %reduce.1), kind=kOutput, calls=%fused_computation.5 | convolution fusion | flops 8912928 | bytes 3145760 | tf_op jit(solution)/shard_map/ns,nrd->srd/dot_general | solution.py:90
  286.8 1.6 copy.85
  288.4 3.0 %fusion.1 = bf16[1024,512]{1,0:T(8,128)(2,1)} fusion(f32[1024,512]{1,0:T(8,128)} %reduce-scatter.2.cloned.1.call-done, f32[8,128,512]{2,1,0:T(8,128)S(1)} %convolution_multiply_fusion.1), kind=kLoop, calls=%fused_computation.7 | loop fusion | flops 1048576 | bytes 5242880 | tf_op jit(solution)/shard_map/convert_element_type | solution.py:71
  (15 shorter events, 0.0 us)
Async XLA Ops:
  7.2 21.6 %copy-start = (bf16[4,32,4096]{2,1,0:T(8,128)(2,1)S(1)}, bf16[4,32,4096]{2,1,0:T(8,128)(2,1)}, u32[]{:S(2)}) copy-start(bf16[4,32,4096]{2,1,0:T(8,128)(2,1)} %param.9) | copy-start | bytes 3145732
  7.2 172.7 %all-gather.2.cloned.1.call-start = ((), (), s32[]{:S(2)}) async-start(), calls=%async_computation.6 | async-start | bytes 9437184 | tf_op jit(solution)/shard_map/all_gather | solution.py:44
  10.4 13.7 %all-to-all-start = ((s32[8,1,1]{2,1,0:T(1,128)}), s32[8,1,1]{2,1,0:T(1,128)S(1)}, u32[]{:S(2)}, u32[]{:S(2)}) async-start(s32[8,1,1]{2,1,0:T(1,128)} %copy.67), calls=%async_computation.1 | async-start | bytes 8192 | tf_op jit(solution)/shard_map/all_to_all | solution.py:30
  25.4 16.4 %all-to-all-start.2 = ((bf16[8,32,512]{2,1,0:T(8,128)(2,1)}), bf16[8,32,512]{2,1,0:T(8,128)(2,1)S(1)}, u32[]{:S(2)}, u32[]{:S(2)}) async-start(bf16[8,32,512]{2,1,0:T(8,128)(2,1)} %copy.74), calls=%async_computation.3 | async-start | bytes 524288 | tf_op jit(solution)/shard_map/all_to_all | solution.py:49
  41.7 153.2 %copy-start.2 = (bf16[8,32,512]{2,1,0:T(8,128)(2,1)}, bf16[8,32,512]{2,1,0:T(8,128)(2,1)S(1)}, u32[]{:S(2)}) copy-start(bf16[8,32,512]{2,1,0:T(8,128)(2,1)S(1)} %all-to-all-done.2) | copy-start | bytes 786436
  41.7 156.8 %all-to-all-start.1 = ((bf16[8,32,4096]{2,1,0:T(8,128)(2,1)}), bf16[8,32,4096]{2,1,0:T(8,128)(2,1)S(1)}, u32[]{:S(2)}, u32[]{:S(2)}) async-start(bf16[8,32,4096]{2,1,0:T(8,128)(2,1)} %copy.69), calls=%async_computation.2 | async-start | bytes 4194304 | tf_op jit(solution)/shard_map/all_to_all | solution.py:48
  45.3 243.0 %reduce-scatter.2.cloned.1.call-start = ((), (), s32[]{:S(2)}) async-start(), calls=%async_computation.7 | async-start | bytes 6291456 | tf_op jit(solution)/shard_map/reduce_scatter | solution.py:70
  194.9 0.7 copy-start.7
  200.4 11.7 %copy-start.1 = (bf16[1024,512]{1,0:T(8,128)(2,1)S(1)}, bf16[1024,512]{1,0:T(8,128)(2,1)}, u32[]{:S(2)}) copy-start(bf16[1024,512]{1,0:T(8,128)(2,1)} %param.11) | copy-start | bytes 3145732
  212.1 10.7 %copy-start.5 = (bf16[8,128,32]{1,2,0:T(8,128)(2,1)}, bf16[8,128,32]{1,2,0:T(8,128)(2,1)S(1)}, u32[]{:S(2)}) copy-start(bf16[8,128,32]{1,2,0:T(8,128)(2,1)S(1)} %get-tuple-element.21) | copy-start | bytes 196612
  213.4 14.3 %all-to-all-start.4 = ((bf16[8,32,512]{2,1,0:T(8,128)(2,1)}), bf16[8,32,512]{2,1,0:T(8,128)(2,1)S(1)}, u32[]{:S(2)}, u32[]{:S(2)}) async-start(bf16[8,32,512]{2,1,0:T(8,128)(2,1)} %copy.83), calls=%async_computation.5 | async-start | bytes 524288 | tf_op jit(solution)/shard_map/all_to_all | solution.py:88
  227.7 6.7 %copy-start.6 = (bf16[8,128,32]{1,2,0:T(8,128)(2,1)S(1)}, bf16[8,128,32]{1,2,0:T(8,128)(2,1)}, u32[]{:S(2)}) copy-start(bf16[8,128,32]{1,2,0:T(8,128)(2,1)} %copy-done.5) | copy-start | bytes 196612
  227.7 0.7 copy-start.3
  228.4 54.3 %all-to-all-start.3 = ((bf16[8,32,4096]{2,1,0:T(8,128)(2,1)}), bf16[8,32,4096]{2,1,0:T(8,128)(2,1)}, u32[]{:S(2)}, u32[]{:S(2)}) async-start(bf16[8,32,4096]{2,1,0:T(8,128)(2,1)} %copy.80), calls=%async_computation.4 | async-start | bytes 4194304 | tf_op jit(solution)/shard_map/all_to_all | solution.py:87
  234.4 1.0 copy-start.4
Sparse Core Ops, SparseCore 0:
  10.1 169.7 all-gather.1
  195.1 12.5 reduce-scatter.1
where the time goes:
time: 299 us; the launch traced here: 298 us
  waiting for transfers between devices  196 us (66%)
  matrix products  41.2 us (14%)
  starting transfers between devices  25.1 us (8%)
  between operations  14.2 us (5%)
  local copies, waits for them, and re-layouts  13 us (4%)
  other arithmetic  4.23 us (1%)
  blocking collectives  4.18 us (1%)
    all_gather x1, waiting for transfers between devices, shards(): lax.all_gather(base_weight, 'dp', axis=1, tiled=True)  135 us
    all_to_all x1, waiting for transfers between devices, shards(): lax.all_to_all(home_a, 'dp', split_axis=0, concat_axis=0, tiled=True)  46.4 us
    dot_general x1, matrix products, shards(): jnp.dot(tokens, lax.all_gather(base_weight, 'dp', axis=1, tiled=True), pr...  15 us
    all_to_all x1, waiting for transfers between devices, shards(): lax.all_to_all(send_b, 'dp', split_axis=0, concat_axis=0, tiled=True)  9.21 us
    dot_general x1, matrix products, shards(): jnp.einsum('nhc,nuc->nhu', token_tiles, block_down_matrix, preferred_elem...  7.49 us
    all_to_all x1, starting transfers between devices, shards(): lax.all_to_all(wanted.reshape(peers, 1), 'dp', split_axis=0, concat_axis=...  7.28 us
    all_to_all x1, starting transfers between devices, shards(): lax.all_to_all(home_a, 'dp', split_axis=0, concat_axis=0, tiled=True)  6 us
  transfers between devices with their start and end apart: 7, of which 4 were waited for; matrix products, arithmetic and copies ran while one was open for 18% of the time, Pallas kernels for 0%

commit v1 on v0

v1 whole, which is shorter than its diff:
```python
import jax
import jax.numpy as jnp
from jax import lax
from jax.sharding import PartitionSpec as P

BLOCK = 128


ADAPTER_SCALING = 2.0
SWAP = [(0, 1), (1, 0)]


def dot(left, right, contract):
    return lax.dot_general(
        left, right, ((contract[0], contract[1]), ((), ())), preferred_element_type=jnp.float32
    )


def partial_base(tokens, base_weight):
    width = base_weight.shape[0]
    peers, core = lax.axis_size("dp"), lax.axis_index("tensor")
    if peers != 8 or lax.axis_size("groups") != 2:
        full = jnp.dot(
            tokens,
            lax.all_gather(base_weight, "dp", axis=1, tiled=True),
            preferred_element_type=jnp.float32,
        )
        mine = full.shape[1] // 2
        return (
            lax.dynamic_slice_in_dim(full, core * mine, mine, 1),
            lax.dynamic_slice_in_dim(full, (1 - core) * mine, mine, 1),
        )
    place, group = lax.axis_index("dp"), lax.axis_index("groups")
    layer, side = place // 2, place % 2
    pair = [(i, i ^ 2) for i in range(8)]
    middle = [(2, 4), (3, 5), (4, 2), (5, 3)]
    outward = [(2, 0), (3, 1), (4, 6), (5, 7)]
    across = [(i, i ^ 1) for i in range(8)]
    half = lax.dynamic_slice_in_dim(base_weight, group * (width // 2), width // 2, 0)
    near = lax.ppermute(half, "dp", pair)
    mid_next = lax.ppermute(half, "dp", middle)
    other_side = lax.ppermute(base_weight, "dp", across)
    mid_far = lax.ppermute(near, "dp", middle)
    end_next = lax.ppermute(mid_next, "dp", outward)
    end_far = lax.ppermute(mid_far, "dp", outward)
    inner = (layer == 1) | (layer == 2)
    halves = [near, jnp.where(inner, mid_next, end_next), jnp.where(inner, mid_far, end_far)]

    def whole(part):
        rest = lax.ppermute(part, "groups", SWAP)
        return jnp.where(
            group == 0, jnp.concatenate([part, rest], 0), jnp.concatenate([rest, part], 0)
        )

    def columns(part, part_across):
        return jnp.where(
            side == 0,
            jnp.concatenate([part, part_across], 1),
            jnp.concatenate([part_across, part], 1),
        )

    own = columns(base_weight, other_side)
    near, following, far = [
        columns(whole(part), whole(lax.ppermute(part, "dp", across))) for part in halves
    ]
    here = jnp.where(
        layer % 2 == 0, jnp.concatenate([own, near], 1), jnp.concatenate([near, own], 1)
    )
    there = jnp.where(
        layer < 2, jnp.concatenate([following, far], 1), jnp.concatenate([far, following], 1)
    )
    product_here = jnp.dot(tokens, here, preferred_element_type=jnp.float32)
    product_there = jnp.dot(tokens, there, preferred_element_type=jnp.float32)
    keep_here = layer // 2 == core
    return (
        jnp.where(keep_here, product_here, product_there),
        jnp.where(keep_here, product_there, product_here),
    )


def shards(tokens, base_weight, adapt_a, adapt_b, cotangent, row_tenant, adapter_slot):
    rows, half_width = tokens.shape
    ten_dev, rank, _ = adapt_a.shape
    output_columns = cotangent.shape[1]
    tenants_all = adapter_slot.shape[0]
    peers = lax.axis_size("dp")
    blocks = rows // BLOCK
    keep, give = partial_base(tokens, base_weight)
    first = row_tenant.reshape(blocks, BLOCK)[:, 0]
    table_ids = jnp.arange(tenants_all, dtype=jnp.int32)
    block_slot = jnp.sum(
        jnp.where(first[:, None] == table_ids[None, :], adapter_slot[None, :], 0), axis=1
    )
    block_home = block_slot // ten_dev
    block_local = block_slot % ten_dev
    peer_ids = jnp.arange(peers, dtype=jnp.int32)
    match = block_home[:, None] == peer_ids[None, :]
    wanted = ten_dev + jnp.sum(jnp.where(match, (block_local - ten_dev)[:, None], 0), axis=0)
    asked = lax.all_to_all(wanted.reshape(peers, 1), "dp", split_axis=0, concat_axis=0, tiled=True)
    asked_rows = jnp.broadcast_to(asked, (peers, rank)).reshape(peers * rank, 1)
    out_row = lax.broadcasted_iota(jnp.int32, (peers * rank, ten_dev * rank), 0)
    slot_row = lax.broadcasted_iota(jnp.int32, (peers * rank, ten_dev * rank), 1)
    select = (
        (asked_rows == slot_row // rank) & (out_row % rank == slot_row % rank)
    ).astype(jnp.bfloat16)
    column = lax.axis_index("tensor") * output_columns
    own_b = lax.dynamic_slice_in_dim(adapt_b, column, output_columns, 2)

    def to_peers(sent):
        return lax.all_to_all(
            sent.reshape(peers, rank, sent.shape[1]), "dp", split_axis=0, concat_axis=0, tiled=True
        ).reshape(sent.shape)

    def chosen(table):
        return dot(select, table.reshape(ten_dev * rank, -1), ((1,), (0,))).astype(jnp.bfloat16)

    got_b = to_peers(chosen(own_b))
    got_a = to_peers(chosen(adapt_a))
    row_home = jnp.broadcast_to(block_home[:, None], (blocks, BLOCK)).reshape(rows, 1)
    home_of = lax.broadcasted_iota(jnp.int32, (rows, peers * rank), 1) // rank
    counted = (row_home == home_of) & (row_tenant != tenants_all)[:, None]

    def rank_space(part):
        total = part + lax.ppermute(part, "tensor", SWAP)
        return jnp.where(counted, total, 0.0).astype(jnp.bfloat16)

    backward_pass = rank_space(dot(cotangent, got_b, ((1,), (1,))))
    home_a = (ADAPTER_SCALING * dot(backward_pass, tokens, ((0,), (0,)))).astype(jnp.bfloat16)
    came_a = to_peers(home_a)
    hidden = rank_space(dot(tokens, got_a, ((1,), (1,))))
    home_b = (ADAPTER_SCALING * dot(hidden, cotangent, ((0,), (0,)))).astype(jnp.bfloat16)
    came_b = to_peers(home_b)
    added = ADAPTER_SCALING * dot(hidden, got_b, ((1,), (0,)))
    base = keep + lax.ppermute(give, "tensor", SWAP)
    proj_out = (base + added).astype(jnp.bfloat16)
    total_a = dot(select, came_a, ((0,), (0,))).astype(jnp.bfloat16)
    total_b = dot(select, came_b, ((0,), (0,))).astype(jnp.bfloat16)
    return (
        proj_out,
        total_a.reshape(ten_dev, rank, half_width),
        total_b.reshape(ten_dev, rank, output_columns),
    )


def solution(mesh):
    return jax.shard_map(
        shards,
        mesh=mesh,
        in_specs=(
            P(("groups", "dp"), "tensor"),
            P("tensor", "dp"),
            P(("groups", "dp"), None, "tensor"),
            P(("groups", "dp"), None, None),
            P(("groups", "dp"), "tensor"),
            P(("groups", "dp")),
            P("groups"),
        ),
        out_specs=(
            P(("groups", "dp"), "tensor"),
            P(("groups", "dp"), None, "tensor"),
            P(("groups", "dp"), None, "tensor"),
        ),
        check_vma=False,
    )
```

time: 299 us -> 236 us (0.79)
  waiting for transfers between devices: 196 us -> 104 us
  starting transfers between devices: 25.1 us -> 63.3 us
  between operations: 14.2 us -> 1.04 us
  other arithmetic: 4.23 us -> 14.4 us
  local copies, waits for them, and re-layouts: 13 us -> 6.87 us
  blocking collectives: 4.18 us -> 0 us
  matrix products: 41.2 us -> 45.2 us
    all_gather x1 -> x0, waiting for transfers between devices: 135 us -> none  [shards(): lax.all_gather(base_weight, 'dp', axis=1, tiled=True)]
    ppermute x0 -> x18, waiting for transfers between devices: none -> 61.1 us  [the longest x3 20.7 us: partial_base(): lax.ppermute(part, 'dp', across)]
    ppermute x0 -> x18, starting transfers between devices: none -> 29.2 us  [the longest x6 8.58 us: whole(): rest = lax.ppermute(part, 'groups', SWAP)]
    all_to_all x4, waiting for transfers between devices: 55.6 us -> 27 us  [to_peers(): lax.all_to_all(sent.reshape(peers, rank, sent.shape[1]), 'dp', split_axis...]
    all_to_all x4, starting transfers between devices: 17.8 us -> 30.8 us  [to_peers(): lax.all_to_all(sent.reshape(peers, rank, sent.shape[1]), 'dp', split_axis...]
    select_n x0 -> x13, other arithmetic: none -> 12.1 us  [the longest x4 5.86 us: columns(): jnp.where(side == 0, jnp.concatenate([part, part_across], 1), jnp.concate...]
    all_to_all x1, waiting for transfers between devices: 5.48 us -> 15.6 us  [shards(): lax.all_to_all(wanted.reshape(peers, 1), 'dp', split_axis=0, concat_axis=...]
    convert_element_type x4 -> x0, local copies, waits for them, and re-layouts: 6.53 us -> none  [the longest x1 2.48 us: shards(): jnp.einsum('bn,brd->nrd', pick, part_a, preferred_element_type=jnp.float32)]
  transfers between devices with their start and end apart: 7 -> 23, of which waited for: 4 -> 9; matrix products, arithmetic and copies ran while one was open for 18% -> 27% of each run, Pallas kernels for 0% -> 0%
where the time goes in v1:
time: 236 us; the launch traced here: 235 us
  waiting for transfers between devices  104 us (44%)
  starting transfers between devices  63.3 us (27%)
  matrix products  45.2 us (19%)
  other arithmetic  14.4 us (6%)
  local copies, waits for them, and re-layouts  6.87 us (3%)
    all_to_all x4, starting transfers between devices, to_peers(): lax.all_to_all(sent.reshape(peers, rank, sent.shape[1]), 'dp', split_axis...  30.8 us
    all_to_all x4, waiting for transfers between devices, to_peers(): lax.all_to_all(sent.reshape(peers, rank, sent.shape[1]), 'dp', split_axis...  27 us
    dot_general x9, matrix products, dot(): lax.dot_general(left, right, ((contract[0], contract[1]), ((), ())), pref...  26.9 us
    ppermute x3, waiting for transfers between devices, partial_base(): lax.ppermute(part, 'dp', across)  20.7 us
    ppermute x1, waiting for transfers between devices, partial_base(): end_far = lax.ppermute(mid_far, 'dp', outward)  19.8 us
    all_to_all x1, waiting for transfers between devices, shards(): lax.all_to_all(wanted.reshape(peers, 1), 'dp', split_axis=0, concat_axis=...  15.6 us
    ppermute x6, waiting for transfers between devices, whole(): rest = lax.ppermute(part, 'groups', SWAP)  13 us
    dot_general x1, matrix products, partial_base(): product_there = jnp.dot(tokens, there, preferred_element_type=jnp.float32)  10.4 us
  transfers between devices with their start and end apart: 23, of which 9 were waited for; matrix products, arithmetic and copies ran while one was open for 27% of the time, Pallas kernels for 0%

profile of v1, /device:TPU:0, one launch (start us, length us, event | category | flops | bytes accessed | tf_op | source)
XLA Modules:
  0.0 234.6 jit_solution(6927894238858921220)
XLA Ops:
  0.7 1.2 constant_dynamic-slice_fusion.1
  1.8 1.5 collective-permute-start.5
  3.3 5.1 %collective-permute-start.1 = (bf16[2048,128]{1,0:T(8,128)(2,1)S(1)}, bf16[2048,128]{1,0:T(8,128)(2,1)}, u32[]{:S(2)}, u32[]{:S(2)}) collective-permute-start(bf16[2048,128]{1,0:T(8,128)(2,1)S(1)} %constant_dynamic-slice_fusion.1), channel_id=1, source_target_pairs={{0,4},{2,6},{4,0},{6,2},{8,12},{10,14},{12,8},{14,10},{1,5},{3,7},... | collective-permute-start | bytes 1572872 | tf_op jit(solution)/shard_map/ppermute | solution.py:40
  8.4 1.5 collective-permute-start
  9.9 0.8 slice_reduce_fusion
  10.7 0.8 select_reduce_fusion.1
  12.4 3.3 %all-to-all-start = ((s32[8,1,1]{2,1,0:T(1,128)}), s32[8,1,1]{2,1,0:T(1,128)S(1)}, u32[]{:S(2)}, u32[]{:S(2)}) async-start(s32[8,1,1]{2,1,0:T(1,128)} %copy.22), calls=%async_computation | async-start | bytes 8192 | tf_op jit(solution)/shard_map/all_to_all | solution.py:99
  16.5 0.9 constant_dynamic-slice_fusion
  17.4 15.6 %all-to-all-done = s32[8,1,1]{2,1,0:T(1,128)S(1)} async-done(((s32[8,1,1]{2,1,0:T(1,128)}), s32[8,1,1]{2,1,0:T(1,128)S(1)}, u32[]{:S(2)}, u32[]{:S(2)}) %all-to-all-start) | async-done | bytes 64 | tf_op jit(solution)/shard_map/all_to_all | solution.py:99
  33.4 1.0 convolution_convert_fusion.2
  34.5 3.6 %all-to-all-start.2 = ((bf16[8,32,512]{2,1,0:T(8,128)(2,1)}), bf16[8,32,512]{2,1,0:T(8,128)(2,1)S(1)}, u32[]{:S(2)}, u32[]{:S(2)}) async-start(bf16[8,32,512]{2,1,0:T(8,128)(2,1)} %bitcast.10), calls=%async_computation.2 | async-start | bytes 524288 | tf_op jit(solution)/shard_map/all_to_all | solution.py:110
  38.2 1.3 collective-permute-start.6
  39.5 2.1 convolution_convert_fusion
  41.6 1.5 collective-permute-start.2
  43.1 3.3 %all-to-all-done.2 = bf16[8,32,512]{2,1,0:T(8,128)(2,1)S(1)} async-done(((bf16[8,32,512]{2,1,0:T(8,128)(2,1)}), bf16[8,32,512]{2,1,0:T(8,128)(2,1)S(1)}, u32[]{:S(2)}, u32[]{:S(2)}) %all-to-all-start.2) | async-done | bytes 262176 | tf_op jit(solution)/shard_map/all_to_all | solution.py:110
  46.3 4.9 %all-to-all-start.1 = ((bf16[8,32,4096]{2,1,0:T(8,128)(2,1)}), bf16[8,32,4096]{2,1,0:T(8,128)(2,1)}, u32[]{:S(2)}, u32[]{:S(2)}) async-start(bf16[8,32,4096]{2,1,0:T(8,128)(2,1)} %bitcast.6), calls=%async_computation.1 | async-start | bytes 4194304 | tf_op jit(solution)/shard_map/all_to_all | solution.py:110
  51.8 0.8 collective-permute-start.10
  52.6 5.3 %collective-permute-done.6 = bf16[2048,128]{1,0:T(8,128)(2,1)} collective-permute-done((bf16[2048,128]{1,0:T(8,128)(2,1)}, bf16[2048,128]{1,0:T(8,128)(2,1)}, u32[]{:S(2)}, u32[]{:S(2)}) %collective-permute-start.6) | collective-permute-done | bytes 524320 | tf_op jit(solution)/shard_map/ppermute | solution.py:44
  57.9 4.5 %collective-permute-start.3 = (bf16[2048,128]{1,0:T(8,128)(2,1)}, bf16[2048,128]{1,0:T(8,128)(2,1)S(1)}, u32[]{:S(2)}, u32[]{:S(2)}) collective-permute-start(bf16[2048,128]{1,0:T(8,128)(2,1)} %collective-permute-done.1), channel_id=1, source_target_pairs={{0,2},{2,0},{4,6},{6,4},{8,10},{10,8},{12,14},{14,12},{1,3},{3,1},... | collective-permute-start | bytes 1572872 | tf_op jit(solution)/shard_map/ppermute | solution.py:64
  62.5 1.1 broadcast_select_fusion.1
  63.7 1.8 maximum_select_fusion.8
  65.5 2.1 collective-permute-start.7
  67.6 20.7 %collective-permute-done.3 = bf16[2048,128]{1,0:T(8,128)(2,1)S(1)} collective-permute-done((bf16[2048,128]{1,0:T(8,128)(2,1)}, bf16[2048,128]{1,0:T(8,128)(2,1)S(1)}, u32[]{:S(2)}, u32[]{:S(2)}) %collective-permute-start.3) | collective-permute-done | bytes 524320 | tf_op jit(solution)/shard_map/ppermute | solution.py:64
  88.2 1.5 collective-permute-start.11
  89.7 1.8 collective-permute-start.4
  92.3 7.3 %fusion = bf16[256,4096]{1,0:T(8,128)(2,1)} fusion(bf16[1024,4096]{1,0:T(8,128)(2,1)} %param.7, f32[1024,256]{0,1:T(8,128)S(1)} %convolution_bitcast_fusion, f32[1024,256]{0,1:T(8,128)S(1)} %collective-permute-done.17, s32[256]{0:T(256)S(1)} %get-tuple-element.31, s32[256]{0:T(256)S(1)} %get-tuple-element.32, s32[1024]{0:T(1024)S(1)} %broadcast_bitcast_fusion, ...), kind=kOutput, calls=%fused_computation.1 | convolution fusion | flops 2151153664 | bytes 12590336 | tf_op jit(solution)/shard_map/dot_general | solution.py:14
  99.5 19.8 %collective-permute-done.11 = bf16[2048,128]{1,0:T(8,128)(2,1)S(1)} collective-permute-done((bf16[2048,128]{1,0:T(8,128)(2,1)S(1)}, bf16[2048,128]{1,0:T(8,128)(2,1)S(1)}, u32[]{:S(2)}, u32[]{:S(2)}) %collective-permute-start.11) | collective-permute-done | bytes 524320 | tf_op jit(solution)/shard_map/ppermute | solution.py:45
  119.4 1.1 collective-permute-start.12
  120.5 3.7 %collective-permute-start.13 = (bf16[2048,128]{1,0:T(8,128)(2,1)S(1)}, bf16[2048,128]{1,0:T(8,128)(2,1)S(1)}, u32[]{:S(2)}, u32[]{:S(2)}) collective-permute-start(bf16[2048,128]{1,0:T(8,128)(2,1)S(1)} %broadcast_select_fusion), channel_id=1, source_target_pairs={{0,2},{2,0},{4,6},{6,4},{8,10},{10,8},{12,14},{14,12},{1,3},{3,1},... | collective-permute-start | bytes 1572872 | tf_op jit(solution)/shard_map/ppermute | solution.py:64
  125.3 1.0 collective-permute-start.9
  126.3 7.9 %fusion.1 = f32[512,1024]{1,0:T(8,128)S(1)} fusion(bf16[1024,4096]{1,0:T(8,128)(2,1)} %param.7, bf16[4096,256]{1,0:T(8,128)(2,1)S(1)} %maximum_select_fusion.5, bf16[4096,256]{1,0:T(8,128)(2,1)S(1)} %maximum_select_fusion.4, pred[]{:T(512)S(6)} %eq.86), kind=kOutput, calls=%fused_computation.5 | convolution fusion | flops 4313841664 | bytes 14680065 | tf_op jit(solution)/shard_map/dot_general | solution.py:72
  134.5 1.1 collective-permute-start.14
  135.7 8.0 %collective-permute-done.9 = bf16[2048,128]{1,0:T(8,128)(2,1)S(1)} collective-permute-done((bf16[2048,128]{1,0:T(8,128)(2,1)S(1)}, bf16[2048,128]{1,0:T(8,128)(2,1)S(1)}, u32[]{:S(2)}, u32[]{:S(2)}) %collective-permute-start.9) | collective-permute-done | bytes 524320 | tf_op jit(solution)/shard_map/ppermute | solution.py:50
  144.2 2.1 maximum_select_fusion.6
  146.4 5.0 %collective-permute-done.14 = bf16[2048,128]{1,0:T(8,128)(2,1)S(1)} collective-permute-done((bf16[2048,128]{1,0:T(8,128)(2,1)S(1)}, bf16[2048,128]{1,0:T(8,128)(2,1)S(1)}, u32[]{:S(2)}, u32[]{:S(2)}) %collective-permute-start.14) | collective-permute-done | bytes 524320 | tf_op jit(solution)/shard_map/ppermute | solution.py:50
  151.6 2.1 maximum_select_fusion.7
  153.8 18.3 %all-to-all-start.3 = ((bf16[8,32,4096]{2,1,0:T(8,128)(2,1)}), bf16[8,32,4096]{2,1,0:T(8,128)(2,1)}, u32[]{:S(2)}, u32[]{:S(2)}) async-start(bf16[8,32,4096]{2,1,0:T(8,128)(2,1)} %bitcast.47), calls=%async_computation.3 | async-start | bytes 4194304 | tf_op jit(solution)/shard_map/all_to_all | solution.py:110
  172.1 10.4 %fusion.7 = f32[512,1024]{1,0:T(8,128)S(1)} fusion(bf16[1024,4096]{1,0:T(8,128)(2,1)} %param.7, bf16[4096,256]{1,0:T(8,128)(2,1)} %maximum_select_fusion.7, bf16[4096,256]{1,0:T(8,128)(2,1)} %maximum_select_fusion.6, pred[]{:T(512)S(6)} %lt.39), kind=kOutput, calls=%fused_computation.12 | convolution fusion | flops 4313841664 | bytes 14680065 | tf_op jit(solution)/shard_map/dot_general | solution.py:73
  182.5 2.0 select_bitcast_fusion
  184.5 6.4 %convolution_bitcast_fusion.1 = f32[1024,256]{0,1:T(8,128)S(1)} fusion(bf16[256,4096]{1,0:T(8,128)(2,1)} %bitcast.7, bf16[1024,4096]{1,0:T(8,128)(2,1)} %param.7), kind=kOutput, calls=%fused_computation.29 | convolution fusion | flops 2147483648 | bytes 11534336 | tf_op jit(solution)/shard_map/dot_general | solution.py:14
  191.4 2.3 collective-permute-done.16
  194.9 1.2 fusion.17
  196.0 23.8 %all-to-all-done.3 = bf16[8,32,4096]{2,1,0:T(8,128)(2,1)} async-done(((bf16[8,32,4096]{2,1,0:T(8,128)(2,1)}), bf16[8,32,4096]{2,1,0:T(8,128)(2,1)}, u32[]{:S(2)}, u32[]{:S(2)}) %all-to-all-start.3) | async-done | bytes 2097184 | tf_op jit(solution)/shard_map/all_to_all | solution.py:110
  219.8 4.1 %all-to-all-start.4 = ((bf16[8,32,512]{2,1,0:T(8,128)(2,1)}), bf16[8,32,512]{2,1,0:T(8,128)(2,1)}, u32[]{:S(2)}, u32[]{:S(2)}) async-start(bf16[8,32,512]{2,1,0:T(8,128)(2,1)} %bitcast.49), calls=%async_computation.4 | async-start | bytes 524288 | tf_op jit(solution)/shard_map/all_to_all | solution.py:110
  223.8 3.3 %fusion.16 = bf16[1024,512]{0,1:T(8,128)(2,1)} fusion(f32[1024,512]{0,1:T(8,128)} %collective-permute-done.15, f32[512,1024]{1,0:T(8,128)S(1)} %fusion.1, f32[512,1024]{1,0:T(8,128)} %copy-done.1, bf16[1024,256]{0,1:T(8,128)(2,1)} %copy-done.3, bf16[256,512]{1,0:T(8,128)(2,1)S(1)} %bitcast.46, pred[]{:T(512)S(6)} %eq.85), kind=kOutput, calls=%fused_computation.26 | convolution fusion | flops 271056896 | bytes 8126465 | tf_op jit(solution)/shard_map/dot_general | solution.py:14
  227.1 2.3 copy.24
  229.4 3.2 %convolution_convert_fusion.1 = bf16[128,4096]{1,0:T(8,128)(2,1)} fusion(bf16[256,4096]{1,0:T(8,128)(2,1)} %bitcast.14, s32[128]{0:T(128)S(1)} %get-tuple-element.28, s32[128]{0:T(128)S(1)} %get-tuple-element.29, s32[256]{0:T(256)S(1)} %get-tuple-element.25, s32[256]{0:T(256)S(1)} %get-tuple-element.26, s32[128]{0:T(128)S(1)} %get-tuple-element.27, ...), kind=kOutput, calls=%fused_computation.3 | convolution fusion | flops 269156352 | bytes 3151360 | tf_op jit(solution)/shard_map/dot_general | solution.py:14
  232.6 2.0 convolution_convert_fusion.3
  (56 shorter events, 7.3 us)
Async XLA Ops:
  0.6 38.8 %copy-start = (bf16[4,32,4096]{2,1,0:T(8,128)(2,1)S(1)}, bf16[4,32,4096]{2,1,0:T(8,128)(2,1)}, u32[]{:S(2)}) copy-start(bf16[4,32,4096]{2,1,0:T(8,128)(2,1)} %param.9) | copy-start | bytes 3145732
  1.8 36.3 %collective-permute-start.5 = (bf16[2048,128]{1,0:T(8,128)(2,1)S(1)}, bf16[2048,128]{1,0:T(8,128)(2,1)}, u32[]{:S(2)}, u32[]{:S(2)}) collective-permute-start(bf16[2048,128]{1,0:T(8,128)(2,1)S(1)} %constant_dynamic-slice_fusion.1), channel_id=1, source_target_pairs={{4,8},{6,10},{8,4},{10,6},{5,9},{7,11},{9,5},{11,7},{20,24},{22,26... | collective-permute-start | bytes 1572872 | tf_op jit(solution)/shard_map/ppermute | solution.py:41
  3.3 38.3 %collective-permute-start.1 = (bf16[2048,128]{1,0:T(8,128)(2,1)S(1)}, bf16[2048,128]{1,0:T(8,128)(2,1)}, u32[]{:S(2)}, u32[]{:S(2)}) collective-permute-start(bf16[2048,128]{1,0:T(8,128)(2,1)S(1)} %constant_dynamic-slice_fusion.1), channel_id=1, source_target_pairs={{0,4},{2,6},{4,0},{6,2},{8,12},{10,14},{12,8},{14,10},{1,5},{3,7},... | collective-permute-start | bytes 1572872 | tf_op jit(solution)/shard_map/ppermute | solution.py:40
  8.4 81.3 %collective-permute-start = (bf16[4096,128]{1,0:T(8,128)(2,1)}, bf16[4096,128]{1,0:T(8,128)(2,1)S(1)}, u32[]{:S(2)}, u32[]{:S(2)}) collective-permute-start(bf16[4096,128]{1,0:T(8,128)(2,1)} %param.8), channel_id=1, source_target_pairs={{0,2},{2,0},{4,6},{6,4},{8,10},{10,8},{12,14},{14,12},{1,3},{3,1},... | collective-permute-start | bytes 3145736 | tf_op jit(solution)/shard_map/ppermute | solution.py:42
  12.4 20.7 %all-to-all-start = ((s32[8,1,1]{2,1,0:T(1,128)}), s32[8,1,1]{2,1,0:T(1,128)S(1)}, u32[]{:S(2)}, u32[]{:S(2)}) async-start(s32[8,1,1]{2,1,0:T(1,128)} %copy.22), calls=%async_computation | async-start | bytes 8192 | tf_op jit(solution)/shard_map/all_to_all | solution.py:99
  34.5 11.8 %all-to-all-start.2 = ((bf16[8,32,512]{2,1,0:T(8,128)(2,1)}), bf16[8,32,512]{2,1,0:T(8,128)(2,1)S(1)}, u32[]{:S(2)}, u32[]{:S(2)}) async-start(bf16[8,32,512]{2,1,0:T(8,128)(2,1)} %bitcast.10), calls=%async_computation.2 | async-start | bytes 524288 | tf_op jit(solution)/shard_map/all_to_all | solution.py:110
  38.2 19.8 %collective-permute-start.6 = (bf16[2048,128]{1,0:T(8,128)(2,1)}, bf16[2048,128]{1,0:T(8,128)(2,1)}, u32[]{:S(2)}, u32[]{:S(2)}) collective-permute-start(bf16[2048,128]{1,0:T(8,128)(2,1)} %collective-permute-done.5), channel_id=1, source_target_pairs={{4,0},{6,2},{8,12},{10,14},{5,1},{7,3},{9,13},{11,15},{20,16},{22,... | collective-permute-start | bytes 1572872 | tf_op jit(solution)/shard_map/ppermute | solution.py:44
  41.6 22.0 %collective-permute-start.2 = (bf16[2048,128]{1,0:T(8,128)(2,1)}, bf16[2048,128]{1,0:T(8,128)(2,1)}, u32[]{:S(2)}, u32[]{:S(2)}) collective-permute-start(bf16[2048,128]{1,0:T(8,128)(2,1)} %collective-permute-done.1), channel_id=1, source_target_pairs={{0,16},{16,0},{1,17},{17,1},{2,18},{18,2},{3,19},{19,3},{4,20},{20... | collective-permute-start | bytes 1572872 | tf_op jit(solution)/shard_map/ppermute | solution.py:50
  46.3 4.9 %copy-start.4 = (bf16[1024,512]{1,0:T(8,128)(2,1)S(1)}, bf16[1024,512]{1,0:T(8,128)(2,1)}, u32[]{:S(2)}) copy-start(bf16[1024,512]{1,0:T(8,128)(2,1)} %param.11) | copy-start | bytes 3145732
  46.3 107.5 %all-to-all-start.1 = ((bf16[8,32,4096]{2,1,0:T(8,128)(2,1)}), bf16[8,32,4096]{2,1,0:T(8,128)(2,1)}, u32[]{:S(2)}, u32[]{:S(2)}) async-start(bf16[8,32,4096]{2,1,0:T(8,128)(2,1)} %bitcast.6), calls=%async_computation.1 | async-start | bytes 4194304 | tf_op jit(solution)/shard_map/all_to_all | solution.py:110
  51.7 39.8 %copy-start.2 = (bf16[4096,128]{1,0:T(8,128)(2,1)S(1)}, bf16[4096,128]{1,0:T(8,128)(2,1)}, u32[]{:S(2)}) copy-start(bf16[4096,128]{1,0:T(8,128)(2,1)} %param.8) | copy-start | bytes 3145732
  51.7 40.6 %collective-permute-start.17 = (f32[1024,256]{0,1:T(8,128)S(1)}, f32[1024,256]{0,1:T(8,128)S(1)}, u32[]{:S(2)}, u32[]{:S(2)}) collective-permute-start(f32[1024,256]{0,1:T(8,128)S(1)} %convolution_bitcast_fusion), channel_id=1, source_target_pairs={{0,1},{1,0},{2,3},{3,2},{4,5},{5,4},{6,7},{7,6},{8,9},{9,8},{10,11... | collective-permute-start | bytes 3145736 | tf_op jit(solution)/shard_map/ppermute | solution.py:124
  51.8 13.7 %collective-permute-start.10 = (bf16[2048,128]{1,0:T(8,128)(2,1)}, bf16[2048,128]{1,0:T(8,128)(2,1)S(1)}, u32[]{:S(2)}, u32[]{:S(2)}) collective-permute-start(bf16[2048,128]{1,0:T(8,128)(2,1)} %collective-permute-done.1), channel_id=1, source_target_pairs={{4,8},{6,10},{8,4},{10,6},{5,9},{7,11},{9,5},{11,7},{20,24},{22,26... | collective-permute-start | bytes 1572872 | tf_op jit(solution)/shard_map/ppermute | solution.py:43
  57.9 30.3 %collective-permute-start.3 = (bf16[2048,128]{1,0:T(8,128)(2,1)}, bf16[2048,128]{1,0:T(8,128)(2,1)S(1)}, u32[]{:S(2)}, u32[]{:S(2)}) collective-permute-start(bf16[2048,128]{1,0:T(8,128)(2,1)} %collective-permute-done.1), channel_id=1, source_target_pairs={{0,2},{2,0},{4,6},{6,4},{8,10},{10,8},{12,14},{14,12},{1,3},{3,1},... | collective-permute-start | bytes 1572872 | tf_op jit(solution)/shard_map/ppermute | solution.py:64
  63.6 61.7 %collective-permute-start.8 = (bf16[2048,128]{1,0:T(8,128)(2,1)S(1)}, bf16[2048,128]{1,0:T(8,128)(2,1)S(1)}, u32[]{:S(2)}, u32[]{:S(2)}) collective-permute-start(bf16[2048,128]{1,0:T(8,128)(2,1)S(1)} %broadcast_select_fusion.1), channel_id=1, source_target_pairs={{0,2},{2,0},{4,6},{6,4},{8,10},{10,8},{12,14},{14,12},{1,3},{3,1},... | collective-permute-start | bytes 1572872 | tf_op jit(solution)/shard_map/ppermute | solution.py:64
  65.5 68.8 %collective-permute-start.7 = (bf16[2048,128]{1,0:T(8,128)(2,1)S(1)}, bf16[2048,128]{1,0:T(8,128)(2,1)S(1)}, u32[]{:S(2)}, u32[]{:S(2)}) collective-permute-start(bf16[2048,128]{1,0:T(8,128)(2,1)S(1)} %broadcast_select_fusion.1), channel_id=1, source_target_pairs={{0,16},{16,0},{1,17},{17,1},{2,18},{18,2},{3,19},{19,3},{4,20},{20... | collective-permute-start | bytes 1572872 | tf_op jit(solution)/shard_map/ppermute | solution.py:50
  88.2 31.1 %collective-permute-start.11 = (bf16[2048,128]{1,0:T(8,128)(2,1)S(1)}, bf16[2048,128]{1,0:T(8,128)(2,1)S(1)}, u32[]{:S(2)}, u32[]{:S(2)}) collective-permute-start(bf16[2048,128]{1,0:T(8,128)(2,1)S(1)} %collective-permute-done.10), channel_id=1, source_target_pairs={{4,0},{6,2},{8,12},{10,14},{5,1},{7,3},{9,13},{11,15},{20,16},{22,... | collective-permute-start | bytes 1572872 | tf_op jit(solution)/shard_map/ppermute | solution.py:45
  89.7 34.5 %collective-permute-start.4 = (bf16[2048,128]{1,0:T(8,128)(2,1)S(1)}, bf16[2048,128]{1,0:T(8,128)(2,1)S(1)}, u32[]{:S(2)}, u32[]{:S(2)}) collective-permute-start(bf16[2048,128]{1,0:T(8,128)(2,1)S(1)} %collective-permute-done.3), channel_id=1, source_target_pairs={{0,16},{16,0},{1,17},{17,1},{2,18},{18,2},{3,19},{19,3},{4,20},{20... | collective-permute-start | bytes 1572872 | tf_op jit(solution)/shard_map/ppermute | solution.py:50
  119.4 24.5 %collective-permute-start.12 = (bf16[2048,128]{1,0:T(8,128)(2,1)S(1)}, bf16[2048,128]{1,0:T(8,128)(2,1)S(1)}, u32[]{:S(2)}, u32[]{:S(2)}) collective-permute-start(bf16[2048,128]{1,0:T(8,128)(2,1)S(1)} %broadcast_select_fusion), channel_id=1, source_target_pairs={{0,16},{16,0},{1,17},{17,1},{2,18},{18,2},{3,19},{19,3},{4,20},{20... | collective-permute-start | bytes 1572872 | tf_op jit(solution)/shard_map/ppermute | solution.py:50
  120.5 14.0 %collective-permute-start.13 = (bf16[2048,128]{1,0:T(8,128)(2,1)S(1)}, bf16[2048,128]{1,0:T(8,128)(2,1)S(1)}, u32[]{:S(2)}, u32[]{:S(2)}) collective-permute-start(bf16[2048,128]{1,0:T(8,128)(2,1)S(1)} %broadcast_select_fusion), channel_id=1, source_target_pairs={{0,2},{2,0},{4,6},{6,4},{8,10},{10,8},{12,14},{14,12},{1,3},{3,1},... | collective-permute-start | bytes 1572872 | tf_op jit(solution)/shard_map/ppermute | solution.py:64
  125.3 18.4 %collective-permute-start.9 = (bf16[2048,128]{1,0:T(8,128)(2,1)S(1)}, bf16[2048,128]{1,0:T(8,128)(2,1)S(1)}, u32[]{:S(2)}, u32[]{:S(2)}) collective-permute-start(bf16[2048,128]{1,0:T(8,128)(2,1)S(1)} %collective-permute-done.8), channel_id=1, source_target_pairs={{0,16},{16,0},{1,17},{17,1},{2,18},{18,2},{3,19},{19,3},{4,20},{20... | collective-permute-start | bytes 1572872 | tf_op jit(solution)/shard_map/ppermute | solution.py:50
  134.5 16.8 %collective-permute-start.14 = (bf16[2048,128]{1,0:T(8,128)(2,1)S(1)}, bf16[2048,128]{1,0:T(8,128)(2,1)S(1)}, u32[]{:S(2)}, u32[]{:S(2)}) collective-permute-start(bf16[2048,128]{1,0:T(8,128)(2,1)S(1)} %collective-permute-done.13), channel_id=1, source_target_pairs={{0,16},{16,0},{1,17},{17,1},{2,18},{18,2},{3,19},{19,3},{4,20},{20... | collective-permute-start | bytes 1572872 | tf_op jit(solution)/shard_map/ppermute | solution.py:50
  153.8 66.0 %all-to-all-start.3 = ((bf16[8,32,4096]{2,1,0:T(8,128)(2,1)}), bf16[8,32,4096]{2,1,0:T(8,128)(2,1)}, u32[]{:S(2)}, u32[]{:S(2)}) async-start(bf16[8,32,4096]{2,1,0:T(8,128)(2,1)} %bitcast.47), calls=%async_computation.3 | async-start | bytes 4194304 | tf_op jit(solution)/shard_map/all_to_all | solution.py:110
  182.5 2.0 copy-start.1
  184.5 39.4 %collective-permute-start.15 = (f32[1024,512]{0,1:T(8,128)}, f32[1024,512]{0,1:T(8,128)}, u32[]{:S(2)}, u32[]{:S(2)}) collective-permute-start(f32[1024,512]{0,1:T(8,128)} %select_bitcast_fusion), channel_id=1, source_target_pairs={{0,1},{1,0},{2,3},{3,2},{4,5},{5,4},{6,7},{7,6},{8,9},{9,8},{10,11... | collective-permute-start | bytes 6291464 | tf_op jit(solution)/shard_map/ppermute | solution.py:134
  190.9 4.0 %copy-start.5 = (bf16[1024,512]{1,0:T(8,128)(2,1)S(1)}, bf16[1024,512]{1,0:T(8,128)(2,1)}, u32[]{:S(2)}) copy-start(bf16[1024,512]{1,0:T(8,128)(2,1)} %param.11) | copy-start | bytes 3145732
  190.9 2.9 %collective-permute-start.16 = (f32[1024,256]{0,1:T(8,128)S(1)}, f32[1024,256]{0,1:T(8,128)S(1)}, u32[]{:S(2)}, u32[]{:S(2)}) collective-permute-start(f32[1024,256]{0,1:T(8,128)S(1)} %convolution_bitcast_fusion.1), channel_id=1, source_target_pairs={{0,1},{1,0},{2,3},{3,2},{4,5},{5,4},{6,7},{7,6},{8,9},{9,8},{10,11... | collective-permute-start | bytes 3145736 | tf_op jit(solution)/shard_map/ppermute | solution.py:124
  194.1 0.8 copy-start.3
  219.8 12.9 %all-to-all-start.4 = ((bf16[8,32,512]{2,1,0:T(8,128)(2,1)}), bf16[8,32,512]{2,1,0:T(8,128)(2,1)}, u32[]{:S(2)}, u32[]{:S(2)}) async-start(bf16[8,32,512]{2,1,0:T(8,128)(2,1)} %bitcast.49), calls=%async_computation.4 | async-start | bytes 524288 | tf_op jit(solution)/shard_map/all_to_all | solution.py:110

commit v2 on v0

v2 whole, which is shorter than its diff:
```python
import jax
import jax.numpy as jnp
from jax import lax
from jax.sharding import PartitionSpec as P

BLOCK = 128


ADAPTER_SCALING = 2.0
SWAP = [(0, 1), (1, 0)]


def dot(left, right, contract):
    return lax.dot_general(
        left, right, ((contract[0], contract[1]), ((), ())), preferred_element_type=jnp.float32
    )


def after(value, *others):
    return lax.optimization_barrier((value, *others))[0]


def in_order(group, part, rest):
    return jnp.where(
        group == 0, jnp.concatenate([part, rest], 0), jnp.concatenate([rest, part], 0)
    )


def beside(side, part, other):
    return jnp.where(
        side == 0, jnp.concatenate([part, other], 1), jnp.concatenate([other, part], 1)
    )


class Adapters:
    def __init__(self, tokens, adapt_a, adapt_b, cotangent, row_tenant, adapter_slot):
        self.tokens, self.cotangent = tokens, cotangent
        self.rows = tokens.shape[0]
        self.ten_dev, self.rank, _ = adapt_a.shape
        self.peers, self.place = lax.axis_size("dp"), lax.axis_index("dp")
        tenants_all, blocks = adapter_slot.shape[0], self.rows // BLOCK
        first = row_tenant.reshape(blocks, BLOCK)[:, 0]
        table_ids = jnp.arange(tenants_all, dtype=jnp.int32)
        block_slot = jnp.sum(
            jnp.where(first[:, None] == table_ids[None, :], adapter_slot[None, :], 0), axis=1
        )
        block_home = block_slot // self.ten_dev
        block_local = block_slot % self.ten_dev
        peer_ids = jnp.arange(self.peers, dtype=jnp.int32)
        match = block_home[:, None] == peer_ids[None, :]
        self.wanted = self.ten_dev + jnp.sum(
            jnp.where(match, (block_local - self.ten_dev)[:, None], 0), axis=0
        )
        columns = self.peers * self.rank
        row_home = jnp.broadcast_to(block_home[:, None], (blocks, BLOCK)).reshape(-1, 1)
        home_of = lax.broadcasted_iota(jnp.int32, (self.rows, columns), 1) // self.rank
        self.counted = (row_home == home_of) & (row_tenant != tenants_all)[:, None]
        output_columns = cotangent.shape[1]
        column = lax.axis_index("tensor") * output_columns
        self.own_a = adapt_a
        self.own_b = lax.dynamic_slice_in_dim(adapt_b, column, output_columns, 2)

    def exchange(self, sent):
        return lax.all_to_all(
            sent.reshape(self.peers, -1, sent.shape[1]), "dp", split_axis=0, concat_axis=0, tiled=True
        ).reshape(sent.shape)

    def choose(self, asked):
        asked_rows = jnp.broadcast_to(asked, (self.peers, self.rank)).reshape(-1, 1)
        shape = (self.peers * self.rank, self.ten_dev * self.rank)
        out_row = lax.broadcasted_iota(jnp.int32, shape, 0)
        slot_row = lax.broadcasted_iota(jnp.int32, shape, 1)
        self.select = (
            (asked_rows == slot_row // self.rank) & (out_row % self.rank == slot_row % self.rank)
        ).astype(jnp.bfloat16)

    def chosen(self, table):
        return dot(
            self.select, table.reshape(self.ten_dev * self.rank, -1), ((1,), (0,))
        ).astype(jnp.bfloat16)

    def rank_space(self, part):
        total = part + lax.ppermute(part, "tensor", SWAP)
        return jnp.where(self.counted, total, 0.0).astype(jnp.bfloat16)

    def term(self, left, right):
        return (ADAPTER_SCALING * dot(left, right, ((0,), (0,)))).astype(jnp.bfloat16)

    def total(self, came):
        return (
            dot(self.select, came, ((0,), (0,)))
            .astype(jnp.bfloat16)
            .reshape(self.ten_dev, self.rank, -1)
        )


def plain(tokens, base_weight, adapters):
    adapters.choose(adapters.exchange(adapters.wanted.reshape(-1, 1)))
    full = jnp.dot(
        tokens,
        lax.all_gather(base_weight, "dp", axis=1, tiled=True),
        preferred_element_type=jnp.float32,
    )
    base = lax.psum_scatter(full, "tensor", scatter_dimension=1, tiled=True)
    got_b = adapters.exchange(adapters.chosen(adapters.own_b))
    got_a = adapters.exchange(adapters.chosen(adapters.own_a))
    backward_pass = adapters.rank_space(dot(adapters.cotangent, got_b, ((1,), (1,))))
    came_a = adapters.exchange(adapters.term(backward_pass, tokens))
    hidden = adapters.rank_space(dot(tokens, got_a, ((1,), (1,))))
    came_b = adapters.exchange(adapters.term(hidden, adapters.cotangent))
    added = ADAPTER_SCALING * dot(hidden, got_b, ((1,), (0,)))
    return (
        (base + added).astype(jnp.bfloat16),
        adapters.total(came_a),
        adapters.total(came_b),
    )


def shards(tokens, base_weight, adapt_a, adapt_b, cotangent, row_tenant, adapter_slot):
    work = Adapters(tokens, adapt_a, adapt_b, cotangent, row_tenant, adapter_slot)
    if lax.axis_size("dp") != 8 or lax.axis_size("groups") != 2:
        return plain(tokens, base_weight, work)
    width = base_weight.shape[0]
    place, group, core = lax.axis_index("dp"), lax.axis_index("groups"), lax.axis_index("tensor")
    layer, side = place // 2, place % 2
    inner = (layer == 1) | (layer == 2)
    pair = [(i, i ^ 2) for i in range(8)]
    middle = [(2, 4), (3, 5), (4, 2), (5, 3)]
    outward = [(2, 0), (3, 1), (4, 6), (5, 7)]
    across = [(i, i ^ 1) for i in range(8)]

    def over(part, pairs):
        return lax.ppermute(part, "dp", pairs)

    def twin(part):
        return lax.ppermute(part, "groups", SWAP)

    barrier = lax.optimization_barrier
    half = lax.dynamic_slice_in_dim(base_weight, group * (width // 2), width // 2, 0)
    near = over(half, pair)
    mid_next = over(half, middle)
    own_across = over(half, across)
    asked = work.exchange(work.wanted.reshape(-1, 1))
    near, mid_next, own_across, asked = barrier((near, mid_next, own_across, asked))
    mid_far = over(near, middle)
    end_next = over(mid_next, outward)
    near_across = over(near, across)
    near_rest = twin(near)
    own_across_rest = twin(own_across)
    work.choose(asked)
    got_b = work.exchange(work.chosen(work.own_b))
    send_a = work.chosen(work.own_a)
    mid_far, end_next, near_across, near_rest, own_across_rest, got_b, send_a = barrier(
        (mid_far, end_next, near_across, near_rest, own_across_rest, got_b, send_a)
    )
    got_a = work.exchange(send_a)
    end_far = over(mid_far, outward)
    following = jnp.where(inner, mid_next, end_next)
    following_across = over(following, across)
    following_rest = twin(following)
    near_across_rest = twin(near_across)
    backward_pass = work.rank_space(dot(cotangent, got_b, ((1,), (1,))))
    home_a = work.term(backward_pass, tokens)
    own = beside(side, base_weight, in_order(group, own_across, own_across_rest))
    got_a, home_a, end_far, following_across, following_rest, near_across_rest, own = barrier(
        (got_a, home_a, end_far, following_across, following_rest, near_across_rest, own)
    )
    came_a = work.exchange(home_a)
    far = jnp.where(inner, mid_far, end_far)
    far_across = over(far, across)
    far_rest = twin(far)
    following_across_rest = twin(following_across)
    far_across_rest = twin(far_across)
    near = beside(
        side, in_order(group, near, near_rest), in_order(group, near_across, near_across_rest)
    )
    here = jnp.where(
        layer % 2 == 0, jnp.concatenate([own, near], 1), jnp.concatenate([near, own], 1)
    )
    product_here = jnp.dot(tokens, here, preferred_element_type=jnp.float32)
    hidden = work.rank_space(dot(tokens, got_a, ((1,), (1,))))
    home_b = work.term(hidden, cotangent)
    added = ADAPTER_SCALING * dot(hidden, got_b, ((1,), (0,)))
    following = beside(
        side,
        in_order(group, following, following_rest),
        in_order(group, following_across, following_across_rest),
    )
    far = beside(side, in_order(group, far, far_rest), in_order(group, far_across, far_across_rest))
    there = jnp.where(
        layer < 2, jnp.concatenate([following, far], 1), jnp.concatenate([far, following], 1)
    )
    product_there = jnp.dot(tokens, there, preferred_element_type=jnp.float32)
    keep_here = layer // 2 == core
    keep = jnp.where(keep_here, product_here, product_there)
    give = jnp.where(keep_here, product_there, product_here)
    base = keep + lax.ppermute(give, "tensor", SWAP)
    proj_out = (base + added).astype(jnp.bfloat16)
    came_a, home_b, proj_out = barrier((came_a, home_b, proj_out))
    came_b = work.exchange(home_b)
    return proj_out, work.total(came_a), work.total(came_b)


def solution(mesh):
    return jax.shard_map(
        shards,
        mesh=mesh,
        in_specs=(
            P(("groups", "dp"), "tensor"),
            P("tensor", "dp"),
            P(("groups", "dp"), None, "tensor"),
            P(("groups", "dp"), None, None),
            P(("groups", "dp"), "tensor"),
            P(("groups", "dp")),
            P("groups"),
        ),
        out_specs=(
            P(("groups", "dp"), "tensor"),
            P(("groups", "dp"), None, "tensor"),
            P(("groups", "dp"), None, "tensor"),
        ),
        check_vma=False,
    )
```

time: 299 us -> 177 us (0.59)
  waiting for transfers between devices: 196 us -> 58.6 us
  starting transfers between devices: 25.1 us -> 48.4 us
  other arithmetic: 4.23 us -> 19.9 us
  between operations: 14.2 us -> 1.19 us
  blocking collectives: 4.18 us -> 0 us
  local copies, waits for them, and re-layouts: 13 us -> 9.85 us
  matrix products: 41.2 us -> 38.2 us
    all_gather x1 -> x0, waiting for transfers between devices: 135 us -> none  [shards(): lax.all_gather(base_weight, 'dp', axis=1, tiled=True)]
    all_to_all x5, waiting for transfers between devices: 61.1 us -> 26.8 us  [exchange(): lax.all_to_all(sent.reshape(self.peers, -1, sent.shape[1]), 'dp', split_a...]
    ppermute x0 -> x19, waiting for transfers between devices: none -> 31.8 us  [the longest x9 24.3 us: over(): return lax.ppermute(part, 'dp', pairs)]
    ppermute x0 -> x19, starting transfers between devices: none -> 25.2 us  [the longest x9 16.9 us: over(): return lax.ppermute(part, 'dp', pairs)]
    select_n x1 -> x15, other arithmetic: 0.01 us -> 18.4 us  [the longest x7 9.86 us: in_order(): jnp.where(group == 0, jnp.concatenate([part, rest], 0), jnp.concatenate([...]
    convert_element_type x4 -> x0, local copies, waits for them, and re-layouts: 6.53 us -> none  [the longest x1 2.48 us: shards(): jnp.einsum('bn,brd->nrd', pick, part_a, preferred_element_type=jnp.float32)]
    psum x1 -> x0, blocking collectives: 4.18 us -> none  [shards(): hidden_sum, back_sum = lax.psum((hidden_fraction, back_part), 'tensor')]
    dot_general x14 -> x11, matrix products: 41.2 us -> 38.2 us  [the longest x9 22 us: dot(): lax.dot_general(left, right, ((contract[0], contract[1]), ((), ())), pref...]
  transfers between devices with their start and end apart: 7 -> 24, of which waited for: 4 -> 10; matrix products, arithmetic and copies ran while one was open for 18% -> 34% of each run, Pallas kernels for 0% -> 0%
where the time goes in v2:
time: 177 us; the launch traced here: 176 us
  waiting for transfers between devices  58.6 us (33%)
  starting transfers between devices  48.4 us (27%)
  matrix products  38.2 us (22%)
  other arithmetic  19.9 us (11%)
  local copies, waits for them, and re-layouts  9.85 us (6%)
    all_to_all x5, waiting for transfers between devices, exchange(): lax.all_to_all(sent.reshape(self.peers, -1, sent.shape[1]), 'dp', split_a...  26.8 us
    ppermute x9, waiting for transfers between devices, over(): return lax.ppermute(part, 'dp', pairs)  24.3 us
    all_to_all x5, starting transfers between devices, exchange(): lax.all_to_all(sent.reshape(self.peers, -1, sent.shape[1]), 'dp', split_a...  23.2 us
    dot_general x9, matrix products, dot(): lax.dot_general(left, right, ((contract[0], contract[1]), ((), ())), pref...  22 us
    ppermute x9, starting transfers between devices, over(): return lax.ppermute(part, 'dp', pairs)  16.9 us
    select_n x7, other arithmetic, in_order(): jnp.where(group == 0, jnp.concatenate([part, rest], 0), jnp.concatenate([...  9.86 us
    dot_general x1, matrix products, shards(): product_there = jnp.dot(tokens, there, preferred_element_type=jnp.float32)  8.17 us
    ppermute x7, starting transfers between devices, twin(): return lax.ppermute(part, 'groups', SWAP)  8.15 us
  transfers between devices with their start and end apart: 24, of which 10 were waited for; matrix products, arithmetic and copies ran while one was open for 34% of the time, Pallas kernels for 0%

profile of v2, /device:TPU:0, one launch (start us, length us, event | category | flops | bytes accessed | tf_op | source)
XLA Modules:
  0.0 176.2 jit_solution(17575188278897916016)
XLA Ops:
  0.7 1.2 constant_dynamic-slice_fusion.1
  1.8 3.0 %collective-permute-start.2 = (bf16[2048,128]{1,0:T(8,128)(2,1)S(1)}, bf16[2048,128]{1,0:T(8,128)(2,1)S(1)}, u32[]{:S(2)}, u32[]{:S(2)}) collective-permute-start(bf16[2048,128]{1,0:T(8,128)(2,1)S(1)} %constant_dynamic-slice_fusion.1), channel_id=1, source_target_pairs={{0,2},{2,0},{4,6},{6,4},{8,10},{10,8},{12,14},{14,12},{1,3},{3,1},... | collective-permute-start | bytes 1572872 | tf_op jit(solution)/shard_map/ppermute | solution.py:133
  5.5 4.4 %collective-permute-start = (bf16[2048,128]{1,0:T(8,128)(2,1)S(1)}, bf16[2048,128]{1,0:T(8,128)(2,1)S(1)}, u32[]{:S(2)}, u32[]{:S(2)}) collective-permute-start(bf16[2048,128]{1,0:T(8,128)(2,1)S(1)} %constant_dynamic-slice_fusion.1), channel_id=1, source_target_pairs={{0,4},{2,6},{4,0},{6,2},{8,12},{10,14},{12,8},{14,10},{1,5},{3,7},... | collective-permute-start | bytes 1572872 | tf_op jit(solution)/shard_map/ppermute | solution.py:133
  12.4 3.3 %all-to-all-start = ((s32[8,1,1]{2,1,0:T(1,128)}), s32[8,1,1]{2,1,0:T(1,128)S(1)}, u32[]{:S(2)}, u32[]{:S(2)}) async-start(s32[8,1,1]{2,1,0:T(1,128)} %copy.22), calls=%async_computation | async-start | bytes 8192 | tf_op jit(solution)/shard_map/all_to_all | solution.py:64
  16.7 5.7 %all-to-all-done = s32[8,1,1]{2,1,0:T(1,128)S(1)} async-done(((s32[8,1,1]{2,1,0:T(1,128)}), s32[8,1,1]{2,1,0:T(1,128)S(1)}, u32[]{:S(2)}, u32[]{:S(2)}) %all-to-all-start) | async-done | bytes 64 | tf_op jit(solution)/shard_map/all_to_all | solution.py:64
  23.5 1.5 collective-permute-start.6
  25.0 1.5 collective-permute-start.5
  26.5 1.5 collective-permute-start.3
  28.1 1.3 collective-permute-start.4
  30.0 1.0 convolution_convert_fusion.2
  31.0 5.7 %all-to-all-start.1 = ((bf16[8,32,512]{2,1,0:T(8,128)(2,1)}), bf16[8,32,512]{2,1,0:T(8,128)(2,1)S(1)}, u32[]{:S(2)}, u32[]{:S(2)}) async-start(bf16[8,32,512]{2,1,0:T(8,128)(2,1)} %bitcast.55), calls=%async_computation.1 | async-start | bytes 524288 | tf_op jit(solution)/shard_map/all_to_all | solution.py:64
  36.7 2.1 %convolution_convert_fusion = bf16[256,4096]{1,0:T(8,128)(2,1)} fusion(bf16[128,4096]{1,0:T(8,128)(2,1)S(1)} %bitcast.46, s32[128]{0:T(128)S(1)} %get-tuple-element.70, s32[128]{0:T(128)S(1)} %get-tuple-element.71, s32[256]{0:T(256)S(1)} %get-tuple-element.67, s32[256]{0:T(256)S(1)} %get-tuple-element.68, s32[128]{0:T(128)S(1)} %get-tuple-element.69, ...), kind=kOutput, calls=%fused_computation.2 | convolution fusion | flops 269680640 | bytes 3151360 | tf_op jit(solution)/shard_map/dot_general | solution.py:14
  38.8 6.9 %all-to-all-done.1 = bf16[8,32,512]{2,1,0:T(8,128)(2,1)S(1)} async-done(((bf16[8,32,512]{2,1,0:T(8,128)(2,1)}), bf16[8,32,512]{2,1,0:T(8,128)(2,1)S(1)}, u32[]{:S(2)}, u32[]{:S(2)}) %all-to-all-start.1) | async-done | bytes 262176 | tf_op jit(solution)/shard_map/all_to_all | solution.py:64
  45.7 1.0 collective-permute-done.7
  47.8 4.6 %all-to-all-start.2 = ((bf16[8,32,4096]{2,1,0:T(8,128)(2,1)}), bf16[8,32,4096]{2,1,0:T(8,128)(2,1)S(1)}, u32[]{:S(2)}, u32[]{:S(2)}) async-start(bf16[8,32,4096]{2,1,0:T(8,128)(2,1)} %bitcast.7), calls=%async_computation.2 | async-start | bytes 4194304 | tf_op jit(solution)/shard_map/all_to_all | solution.py:64
  52.6 1.2 broadcast_select_fusion.1
  53.8 1.6 collective-permute-start.11
  55.4 2.0 %collective-permute-start.10 = (bf16[2048,128]{1,0:T(8,128)(2,1)S(1)}, bf16[2048,128]{1,0:T(8,128)(2,1)S(1)}, u32[]{:S(2)}, u32[]{:S(2)}) collective-permute-start(bf16[2048,128]{1,0:T(8,128)(2,1)S(1)} %broadcast_select_fusion.1), channel_id=1, source_target_pairs={{0,2},{2,0},{4,6},{6,4},{8,10},{10,8},{12,14},{14,12},{1,3},{3,1},... | collective-permute-start | bytes 1572872 | tf_op jit(solution)/shard_map/ppermute | solution.py:133
  57.4 1.3 collective-permute-start.9
  59.8 1.5 maximum_select_fusion.8
  61.4 1.2 maximum_select_fusion.9
  62.7 2.1 %maximum_select_fusion.4 = bf16[4096,256]{1,0:T(8,128)(2,1)} fusion(bf16[4096,128]{1,0:T(8,128)(2,1)S(1)} %maximum_select_fusion.8, bf16[4096,128]{1,0:T(8,128)(2,1)S(1)} %copy-done.2, pred[]{:T(512)S(6)} %eq.102), kind=kLoop, calls=%fused_computation.20 | loop fusion | flops 9437184 | bytes 4194305 | tf_op jit(solution)/shard_map/jit(_where)/select_n | solution.py:30
  64.8 7.3 %fusion = bf16[256,4096]{1,0:T(8,128)(2,1)} fusion(bf16[1024,4096]{1,0:T(8,128)(2,1)} %param.7, f32[1024,256]{0,1:T(8,128)S(1)} %convolution_bitcast_fusion.1, f32[1024,256]{0,1:T(8,128)S(1)} %collective-permute-done.8, s32[256]{0:T(256)S(1)} %iota_shift-right-logical_fusion, s32[256]{0:T(256)S(1)} %broadcast_add_fusion, ...), kind=kOutput, calls=%fused_computation.1 | convolution fusion | flops 2151153664 | bytes 12590336 | tf_op jit(solution)/shard_map/dot_general | solution.py:14
  72.1 12.2 %collective-permute-done.10 = bf16[2048,128]{1,0:T(8,128)(2,1)S(1)} collective-permute-done((bf16[2048,128]{1,0:T(8,128)(2,1)S(1)}, bf16[2048,128]{1,0:T(8,128)(2,1)S(1)}, u32[]{:S(2)}, u32[]{:S(2)}) %collective-permute-start.10) | collective-permute-done | bytes 524320 | tf_op jit(solution)/shard_map/ppermute | solution.py:133
  84.3 4.2 %collective-permute-done.9 = bf16[2048,128]{1,0:T(8,128)(2,1)S(1)} collective-permute-done((bf16[2048,128]{1,0:T(8,128)(2,1)}, bf16[2048,128]{1,0:T(8,128)(2,1)S(1)}, u32[]{:S(2)}, u32[]{:S(2)}) %collective-permute-start.9) | collective-permute-done | bytes 524320 | tf_op jit(solution)/shard_map/ppermute | solution.py:133
  89.3 8.8 %all-to-all-done.2 = bf16[8,32,4096]{2,1,0:T(8,128)(2,1)S(1)} async-done(((bf16[8,32,4096]{2,1,0:T(8,128)(2,1)}), bf16[8,32,4096]{2,1,0:T(8,128)(2,1)S(1)}, u32[]{:S(2)}, u32[]{:S(2)}) %all-to-all-start.2) | async-done | bytes 2097184 | tf_op jit(solution)/shard_map/all_to_all | solution.py:64
  98.1 2.2 %broadcast_select_fusion = bf16[2048,128]{1,0:T(8,128)(2,1)} fusion(bf16[2048,128]{1,0:T(8,128)(2,1)} %collective-permute-done.3, bf16[2048,128]{1,0:T(8,128)(2,1)} %copy-done.22, pred[]{:T(512)S(6)} %or.3), kind=kLoop, calls=%fused_computation.50 | loop fusion | flops 262144 | bytes 1572865 | tf_op jit(solution)/shard_map/jit(_where)/select_n | solution.py:169
  100.3 1.2 collective-permute-start.16
  101.6 1.5 collective-permute-start.15
  103.1 3.8 %all-to-all-start.3 = ((bf16[8,32,4096]{2,1,0:T(8,128)(2,1)}), bf16[8,32,4096]{2,1,0:T(8,128)(2,1)S(1)}, u32[]{:S(2)}, u32[]{:S(2)}) async-start(bf16[8,32,4096]{2,1,0:T(8,128)(2,1)} %bitcast.51), calls=%async_computation.3 | async-start | bytes 4194304 | tf_op jit(solution)/shard_map/all_to_all | solution.py:64
  106.9 1.9 %maximum_select_fusion.10 = bf16[4096,128]{1,0:T(8,128)(2,1)S(1)} fusion(bf16[2048,128]{1,0:T(8,128)(2,1)} %collective-permute-done.12, bf16[2048,128]{1,0:T(8,128)(2,1)} %copy-done.14, pred[]{:T(512)S(6)} %eq.103), kind=kLoop, calls=%fused_computation.36 | loop fusion | flops 4718592 | bytes 2097153 | tf_op jit(solution)/shard_map/jit(_where)/select_n | solution.py:24
  110.4 8.0 %fusion.1 = f32[512,1024]{1,0:T(8,128)S(1)} fusion(bf16[1024,4096]{1,0:T(8,128)(2,1)} %param.7, bf16[4096,256]{1,0:T(8,128)(2,1)S(1)} %maximum_select_fusion.5, bf16[4096,256]{1,0:T(8,128)(2,1)S(1)} %copy-done.7, pred[]{:T(512)S(6)} %eq.105), kind=kOutput, calls=%fused_computation.5 | convolution fusion | flops 4313841664 | bytes 14680065 | tf_op jit(solution)/shard_map/dot_general | solution.py:180
  118.7 8.0 %collective-permute-done.16 = bf16[2048,128]{1,0:T(8,128)(2,1)} collective-permute-done((bf16[2048,128]{1,0:T(8,128)(2,1)}, bf16[2048,128]{1,0:T(8,128)(2,1)}, u32[]{:S(2)}, u32[]{:S(2)}) %collective-permute-start.16) | collective-permute-done | bytes 524320 | tf_op jit(solution)/shard_map/ppermute | solution.py:133
  126.7 1.8 %collective-permute-start.17 = (bf16[2048,128]{1,0:T(8,128)(2,1)}, bf16[2048,128]{1,0:T(8,128)(2,1)S(1)}, u32[]{:S(2)}, u32[]{:S(2)}) collective-permute-start(bf16[2048,128]{1,0:T(8,128)(2,1)} %collective-permute-done.16), channel_id=1, source_target_pairs={{0,16},{16,0},{1,17},{17,1},{2,18},{18,2},{3,19},{19,3},{4,20},{20... | collective-permute-start | bytes 1572872 | tf_op jit(solution)/shard_map/ppermute | solution.py:136
  128.5 1.8 %maximum_select_fusion.13 = bf16[4096,128]{1,0:T(8,128)(2,1)S(1)} fusion(bf16[2048,128]{1,0:T(8,128)(2,1)} %collective-permute-done.15, bf16[2048,128]{1,0:T(8,128)(2,1)} %broadcast_select_fusion, pred[]{:T(512)S(6)} %eq.103), kind=kLoop, calls=%fused_computation.39 | loop fusion | flops 4718592 | bytes 2097153 | tf_op jit(solution)/shard_map/jit(_where)/select_n | solution.py:24
  130.4 1.6 maximum_select_fusion.12
  132.7 3.8 %collective-permute-done.17 = bf16[2048,128]{1,0:T(8,128)(2,1)S(1)} collective-permute-done((bf16[2048,128]{1,0:T(8,128)(2,1)}, bf16[2048,128]{1,0:T(8,128)(2,1)S(1)}, u32[]{:S(2)}, u32[]{:S(2)}) %collective-permute-start.17) | collective-permute-done | bytes 524320 | tf_op jit(solution)/shard_map/ppermute | solution.py:136
  136.5 1.5 maximum_select_fusion.14
  138.8 8.2 %fusion.7 = f32[512,1024]{1,0:T(8,128)S(1)} fusion(bf16[1024,4096]{1,0:T(8,128)(2,1)} %param.7, bf16[4096,256]{1,0:T(8,128)(2,1)S(1)} %maximum_select_fusion.7, bf16[4096,256]{1,0:T(8,128)(2,1)S(1)} %maximum_select_fusion.6, pred[]{:T(512)S(6)} %lt.43), kind=kOutput, calls=%fused_computation.12 | convolution fusion | flops 4313841664 | bytes 14680065 | tf_op jit(solution)/shard_map/dot_general | solution.py:193
  148.6 5.7 %convolution_bitcast_fusion = f32[1024,256]{0,1:T(8,128)S(1)} fusion(bf16[256,4096]{1,0:T(8,128)(2,1)S(1)} %bitcast.50, bf16[1024,4096]{1,0:T(8,128)(2,1)} %param.7), kind=kOutput, calls=%fused_computation.28 | convolution fusion | flops 2147483648 | bytes 11534336 | tf_op jit(solution)/shard_map/dot_general | solution.py:14
  154.4 2.6 %collective-permute-done.13 = f32[1024,256]{0,1:T(8,128)S(1)} collective-permute-done((f32[1024,256]{0,1:T(8,128)S(1)}, f32[1024,256]{0,1:T(8,128)S(1)}, u32[]{:S(2)}, u32[]{:S(2)}) %collective-permute-start.13) | collective-permute-done | bytes 1048608 | tf_op jit(solution)/shard_map/ppermute | solution.py:83
  157.4 1.1 fusion.17
  158.5 1.5 fusion.16
  160.1 5.8 %all-to-all-start.4 = ((bf16[8,32,512]{2,1,0:T(8,128)(2,1)}), bf16[8,32,512]{2,1,0:T(8,128)(2,1)S(1)}, u32[]{:S(2)}, u32[]{:S(2)}) async-start(bf16[8,32,512]{2,1,0:T(8,128)(2,1)} %bitcast.53), calls=%async_computation.4 | async-start | bytes 524288 | tf_op jit(solution)/shard_map/all_to_all | solution.py:64
  165.9 2.3 %copy.24 = bf16[1024,512]{1,0:T(8,128)(2,1)} copy(bf16[1024,512]{0,1:T(8,128)(2,1)} %fusion.16) | data formatting | bytes 2097152
  168.2 1.6 convolution_convert_fusion.1
  169.8 5.3 %all-to-all-done.4 = bf16[8,32,512]{2,1,0:T(8,128)(2,1)S(1)} async-done(((bf16[8,32,512]{2,1,0:T(8,128)(2,1)}), bf16[8,32,512]{2,1,0:T(8,128)(2,1)S(1)}, u32[]{:S(2)}, u32[]{:S(2)}) %all-to-all-start.4) | async-done | bytes 262176 | tf_op jit(solution)/shard_map/all_to_all | solution.py:64
  175.1 1.1 convolution_convert_fusion.3
  (96 shorter events, 14.3 us)
Async XLA Ops:
  0.6 36.0 %copy-start = (bf16[4,32,4096]{2,1,0:T(8,128)(2,1)S(1)}, bf16[4,32,4096]{2,1,0:T(8,128)(2,1)}, u32[]{:S(2)}) copy-start(bf16[4,32,4096]{2,1,0:T(8,128)(2,1)} %param.9) | copy-start | bytes 3145732
  1.8 20.8 %collective-permute-start.2 = (bf16[2048,128]{1,0:T(8,128)(2,1)S(1)}, bf16[2048,128]{1,0:T(8,128)(2,1)S(1)}, u32[]{:S(2)}, u32[]{:S(2)}) collective-permute-start(bf16[2048,128]{1,0:T(8,128)(2,1)S(1)} %constant_dynamic-slice_fusion.1), channel_id=1, source_target_pairs={{0,2},{2,0},{4,6},{6,4},{8,10},{10,8},{12,14},{14,12},{1,3},{3,1},... | collective-permute-start | bytes 1572872 | tf_op jit(solution)/shard_map/ppermute | solution.py:133
  4.9 17.8 %collective-permute-start.1 = (bf16[2048,128]{1,0:T(8,128)(2,1)S(1)}, bf16[2048,128]{1,0:T(8,128)(2,1)S(1)}, u32[]{:S(2)}, u32[]{:S(2)}) collective-permute-start(bf16[2048,128]{1,0:T(8,128)(2,1)S(1)} %constant_dynamic-slice_fusion.1), channel_id=1, source_target_pairs={{4,8},{6,10},{8,4},{10,6},{5,9},{7,11},{9,5},{11,7},{20,24},{22,26... | collective-permute-start | bytes 1572872 | tf_op jit(solution)/shard_map/ppermute | solution.py:133
  5.5 17.2 %collective-permute-start = (bf16[2048,128]{1,0:T(8,128)(2,1)S(1)}, bf16[2048,128]{1,0:T(8,128)(2,1)S(1)}, u32[]{:S(2)}, u32[]{:S(2)}) collective-permute-start(bf16[2048,128]{1,0:T(8,128)(2,1)S(1)} %constant_dynamic-slice_fusion.1), channel_id=1, source_target_pairs={{0,4},{2,6},{4,0},{6,2},{8,12},{10,14},{12,8},{14,10},{1,5},{3,7},... | collective-permute-start | bytes 1572872 | tf_op jit(solution)/shard_map/ppermute | solution.py:133
  12.4 10.0 %all-to-all-start = ((s32[8,1,1]{2,1,0:T(1,128)}), s32[8,1,1]{2,1,0:T(1,128)S(1)}, u32[]{:S(2)}, u32[]{:S(2)}) async-start(s32[8,1,1]{2,1,0:T(1,128)} %copy.22), calls=%async_computation | async-start | bytes 8192 | tf_op jit(solution)/shard_map/all_to_all | solution.py:64
  22.7 24.1 %copy-start.10 = (bf16[2048,128]{1,0:T(8,128)(2,1)}, bf16[2048,128]{1,0:T(8,128)(2,1)S(1)}, u32[]{:S(2)}) copy-start(bf16[2048,128]{1,0:T(8,128)(2,1)S(1)} %collective-permute-done.2) | copy-start | bytes 1572868
  22.7 0.8 copy-start.21
  23.5 23.3 %copy-start.12 = (bf16[2048,128]{1,0:T(8,128)(2,1)}, bf16[2048,128]{1,0:T(8,128)(2,1)S(1)}, u32[]{:S(2)}) copy-start(bf16[2048,128]{1,0:T(8,128)(2,1)S(1)} %collective-permute-done) | copy-start | bytes 1572868
  23.5 23.2 %collective-permute-start.6 = (bf16[2048,128]{1,0:T(8,128)(2,1)S(1)}, bf16[2048,128]{1,0:T(8,128)(2,1)S(1)}, u32[]{:S(2)}, u32[]{:S(2)}) collective-permute-start(bf16[2048,128]{1,0:T(8,128)(2,1)S(1)} %collective-permute-done), channel_id=1, source_target_pairs={{0,16},{16,0},{1,17},{17,1},{2,18},{18,2},{3,19},{19,3},{4,20},{20... | collective-permute-start | bytes 1572872 | tf_op jit(solution)/shard_map/ppermute | solution.py:136
  25.0 21.7 %collective-permute-start.5 = (bf16[2048,128]{1,0:T(8,128)(2,1)S(1)}, bf16[2048,128]{1,0:T(8,128)(2,1)S(1)}, u32[]{:S(2)}, u32[]{:S(2)}) collective-permute-start(bf16[2048,128]{1,0:T(8,128)(2,1)S(1)} %collective-permute-done), channel_id=1, source_target_pairs={{0,2},{2,0},{4,6},{6,4},{8,10},{10,8},{12,14},{14,12},{1,3},{3,1},... | collective-permute-start | bytes 1572872 | tf_op jit(solution)/shard_map/ppermute | solution.py:133
  26.5 20.3 %collective-permute-start.3 = (bf16[2048,128]{1,0:T(8,128)(2,1)S(1)}, bf16[2048,128]{1,0:T(8,128)(2,1)}, u32[]{:S(2)}, u32[]{:S(2)}) collective-permute-start(bf16[2048,128]{1,0:T(8,128)(2,1)S(1)} %collective-permute-done), channel_id=1, source_target_pairs={{4,8},{6,10},{8,4},{10,6},{5,9},{7,11},{9,5},{11,7},{20,24},{22,26... | collective-permute-start | bytes 1572872 | tf_op jit(solution)/shard_map/ppermute | solution.py:133
  28.1 17.6 %collective-permute-start.4 = (bf16[2048,128]{1,0:T(8,128)(2,1)}, bf16[2048,128]{1,0:T(8,128)(2,1)}, u32[]{:S(2)}, u32[]{:S(2)}) collective-permute-start(bf16[2048,128]{1,0:T(8,128)(2,1)} %copy-done.21), channel_id=1, source_target_pairs={{4,0},{6,2},{8,12},{10,14},{5,1},{7,3},{9,13},{11,15},{20,16},{22,... | collective-permute-start | bytes 1572872 | tf_op jit(solution)/shard_map/ppermute | solution.py:133
  29.4 17.4 %collective-permute-start.7 = (bf16[2048,128]{1,0:T(8,128)(2,1)S(1)}, bf16[2048,128]{1,0:T(8,128)(2,1)}, u32[]{:S(2)}, u32[]{:S(2)}) collective-permute-start(bf16[2048,128]{1,0:T(8,128)(2,1)S(1)} %collective-permute-done.2), channel_id=1, source_target_pairs={{0,16},{16,0},{1,17},{17,1},{2,18},{18,2},{3,19},{19,3},{4,20},{20... | collective-permute-start | bytes 1572872 | tf_op jit(solution)/shard_map/ppermute | solution.py:136
  31.0 14.7 %all-to-all-start.1 = ((bf16[8,32,512]{2,1,0:T(8,128)(2,1)}), bf16[8,32,512]{2,1,0:T(8,128)(2,1)S(1)}, u32[]{:S(2)}, u32[]{:S(2)}) async-start(bf16[8,32,512]{2,1,0:T(8,128)(2,1)} %bitcast.55), calls=%async_computation.1 | async-start | bytes 524288 | tf_op jit(solution)/shard_map/all_to_all | solution.py:64
  46.8 0.8 copy-start.15
  46.8 1.0 copy-start.14
  46.8 5.8 %copy-start.23 = (s32[1024]{0:T(1024)S(1)}, s32[1024]{0:T(1024)}, u32[]{:S(2)}) copy-start(s32[1024]{0:T(1024)} %param.12) | copy-start | bytes 12292
  47.8 50.3 %all-to-all-start.2 = ((bf16[8,32,4096]{2,1,0:T(8,128)(2,1)}), bf16[8,32,4096]{2,1,0:T(8,128)(2,1)S(1)}, u32[]{:S(2)}, u32[]{:S(2)}) async-start(bf16[8,32,4096]{2,1,0:T(8,128)(2,1)} %bitcast.7), calls=%async_computation.2 | async-start | bytes 4194304 | tf_op jit(solution)/shard_map/all_to_all | solution.py:64
  52.4 6.8 %copy-start.8 = (bf16[1024,512]{1,0:T(8,128)(2,1)S(1)}, bf16[1024,512]{1,0:T(8,128)(2,1)}, u32[]{:S(2)}) copy-start(bf16[1024,512]{1,0:T(8,128)(2,1)} %param.11) | copy-start | bytes 3145732
  52.5 7.4 %copy-start.11 = (bf16[2048,128]{1,0:T(8,128)(2,1)S(1)}, bf16[2048,128]{1,0:T(8,128)(2,1)}, u32[]{:S(2)}) copy-start(bf16[2048,128]{1,0:T(8,128)(2,1)} %copy-done.10) | copy-start | bytes 1572868
  53.8 7.6 %copy-start.3 = (bf16[2048,128]{1,0:T(8,128)(2,1)}, bf16[2048,128]{1,0:T(8,128)(2,1)S(1)}, u32[]{:S(2)}) copy-start(bf16[2048,128]{1,0:T(8,128)(2,1)S(1)} %broadcast_select_fusion.1) | copy-start | bytes 1572868
  53.8 7.6 %copy-start.13 = (bf16[2048,128]{1,0:T(8,128)(2,1)S(1)}, bf16[2048,128]{1,0:T(8,128)(2,1)}, u32[]{:S(2)}) copy-start(bf16[2048,128]{1,0:T(8,128)(2,1)} %copy-done.12) | copy-start | bytes 1572868
  53.8 7.6 %copy-start.16 = (bf16[2048,128]{1,0:T(8,128)(2,1)S(1)}, bf16[2048,128]{1,0:T(8,128)(2,1)}, u32[]{:S(2)}) copy-start(bf16[2048,128]{1,0:T(8,128)(2,1)} %copy-done.15) | copy-start | bytes 1572868
  53.8 18.3 %collective-permute-start.11 = (bf16[2048,128]{1,0:T(8,128)(2,1)S(1)}, bf16[2048,128]{1,0:T(8,128)(2,1)S(1)}, u32[]{:S(2)}, u32[]{:S(2)}) collective-permute-start(bf16[2048,128]{1,0:T(8,128)(2,1)S(1)} %broadcast_select_fusion.1), channel_id=1, source_target_pairs={{0,16},{16,0},{1,17},{17,1},{2,18},{18,2},{3,19},{19,3},{4,20},{20... | collective-permute-start | bytes 1572872 | tf_op jit(solution)/shard_map/ppermute | solution.py:136
  55.4 28.9 %collective-permute-start.10 = (bf16[2048,128]{1,0:T(8,128)(2,1)S(1)}, bf16[2048,128]{1,0:T(8,128)(2,1)S(1)}, u32[]{:S(2)}, u32[]{:S(2)}) collective-permute-start(bf16[2048,128]{1,0:T(8,128)(2,1)S(1)} %broadcast_select_fusion.1), channel_id=1, source_target_pairs={{0,2},{2,0},{4,6},{6,4},{8,10},{10,8},{12,14},{14,12},{1,3},{3,1},... | collective-permute-start | bytes 1572872 | tf_op jit(solution)/shard_map/ppermute | solution.py:133
  57.4 31.1 %collective-permute-start.9 = (bf16[2048,128]{1,0:T(8,128)(2,1)}, bf16[2048,128]{1,0:T(8,128)(2,1)S(1)}, u32[]{:S(2)}, u32[]{:S(2)}) collective-permute-start(bf16[2048,128]{1,0:T(8,128)(2,1)} %collective-permute-done.3), channel_id=1, source_target_pairs={{4,0},{6,2},{8,12},{10,14},{5,1},{7,3},{9,13},{11,15},{20,16},{22,... | collective-permute-start | bytes 1572872 | tf_op jit(solution)/shard_map/ppermute | solution.py:133
  58.7 30.6 %collective-permute-start.12 = (bf16[2048,128]{1,0:T(8,128)(2,1)}, bf16[2048,128]{1,0:T(8,128)(2,1)}, u32[]{:S(2)}, u32[]{:S(2)}) collective-permute-start(bf16[2048,128]{1,0:T(8,128)(2,1)} %copy-done.14), channel_id=1, source_target_pairs={{0,16},{16,0},{1,17},{17,1},{2,18},{18,2},{3,19},{19,3},{4,20},{20... | collective-permute-start | bytes 1572872 | tf_op jit(solution)/shard_map/ppermute | solution.py:136
  59.7 2.9 %copy-start.2 = (bf16[4096,128]{1,0:T(8,128)(2,1)S(1)}, bf16[4096,128]{1,0:T(8,128)(2,1)}, u32[]{:S(2)}) copy-start(bf16[4096,128]{1,0:T(8,128)(2,1)} %param.8) | copy-start | bytes 3145732
  59.7 5.0 %collective-permute-start.8 = (f32[1024,256]{0,1:T(8,128)S(1)}, f32[1024,256]{0,1:T(8,128)S(1)}, u32[]{:S(2)}, u32[]{:S(2)}) collective-permute-start(f32[1024,256]{0,1:T(8,128)S(1)} %convolution_bitcast_fusion.1), channel_id=1, source_target_pairs={{0,1},{1,0},{2,3},{3,2},{4,5},{5,4},{6,7},{7,6},{8,9},{9,8},{10,11... | collective-permute-start | bytes 3145736 | tf_op jit(solution)/shard_map/ppermute | solution.py:83
  72.1 16.4 %copy-start.19 = (bf16[2048,128]{1,0:T(8,128)(2,1)}, bf16[2048,128]{1,0:T(8,128)(2,1)S(1)}, u32[]{:S(2)}) copy-start(bf16[2048,128]{1,0:T(8,128)(2,1)S(1)} %collective-permute-done.11) | copy-start | bytes 1572868
  84.3 4.2 %copy-start.17 = (bf16[2048,128]{1,0:T(8,128)(2,1)}, bf16[2048,128]{1,0:T(8,128)(2,1)S(1)}, u32[]{:S(2)}) copy-start(bf16[2048,128]{1,0:T(8,128)(2,1)S(1)} %collective-permute-done.10) | copy-start | bytes 1572868
  88.5 0.8 copy-start.22
  98.1 5.0 %copy-start.5 = (bf16[8,32,4096]{2,1,0:T(8,128)(2,1)}, bf16[8,32,4096]{2,1,0:T(8,128)(2,1)S(1)}, u32[]{:S(2)}) copy-start(bf16[8,32,4096]{2,1,0:T(8,128)(2,1)S(1)} %all-to-all-done.2) | copy-start | bytes 6291460
  100.3 26.4 %collective-permute-start.16 = (bf16[2048,128]{1,0:T(8,128)(2,1)}, bf16[2048,128]{1,0:T(8,128)(2,1)}, u32[]{:S(2)}, u32[]{:S(2)}) collective-permute-start(bf16[2048,128]{1,0:T(8,128)(2,1)} %broadcast_select_fusion), channel_id=1, source_target_pairs={{0,2},{2,0},{4,6},{6,4},{8,10},{10,8},{12,14},{14,12},{1,3},{3,1},... | collective-permute-start | bytes 1572872 | tf_op jit(solution)/shard_map/ppermute | solution.py:133
  101.6 26.9 %collective-permute-start.15 = (bf16[2048,128]{1,0:T(8,128)(2,1)}, bf16[2048,128]{1,0:T(8,128)(2,1)}, u32[]{:S(2)}, u32[]{:S(2)}) collective-permute-start(bf16[2048,128]{1,0:T(8,128)(2,1)} %broadcast_select_fusion), channel_id=1, source_target_pairs={{0,16},{16,0},{1,17},{17,1},{2,18},{18,2},{3,19},{19,3},{4,20},{20... | collective-permute-start | bytes 1572872 | tf_op jit(solution)/shard_map/ppermute | solution.py:136
  103.1 57.0 %all-to-all-start.3 = ((bf16[8,32,4096]{2,1,0:T(8,128)(2,1)}), bf16[8,32,4096]{2,1,0:T(8,128)(2,1)S(1)}, u32[]{:S(2)}, u32[]{:S(2)}) async-start(bf16[8,32,4096]{2,1,0:T(8,128)(2,1)} %bitcast.51), calls=%async_computation.3 | async-start | bytes 4194304 | tf_op jit(solution)/shard_map/all_to_all | solution.py:64
  106.9 1.9 %copy-start.18 = (bf16[2048,128]{1,0:T(8,128)(2,1)S(1)}, bf16[2048,128]{1,0:T(8,128)(2,1)}, u32[]{:S(2)}) copy-start(bf16[2048,128]{1,0:T(8,128)(2,1)} %copy-done.17) | copy-start | bytes 1572868
  106.9 2.5 %copy-start.1 = (bf16[4096,128]{1,0:T(8,128)(2,1)S(1)}, bf16[4096,128]{1,0:T(8,128)(2,1)}, u32[]{:S(2)}) copy-start(bf16[4096,128]{1,0:T(8,128)(2,1)} %maximum_select_fusion.9) | copy-start | bytes 3145732
  108.8 1.6 copy-start.7
  108.8 21.5 %collective-permute-start.14 = (bf16[2048,128]{1,0:T(8,128)(2,1)S(1)}, bf16[2048,128]{1,0:T(8,128)(2,1)}, u32[]{:S(2)}, u32[]{:S(2)}) collective-permute-start(bf16[2048,128]{1,0:T(8,128)(2,1)S(1)} %copy-done.18), channel_id=1, source_target_pairs={{0,16},{16,0},{1,17},{17,1},{2,18},{18,2},{3,19},{19,3},{4,20},{20... | collective-permute-start | bytes 1572872 | tf_op jit(solution)/shard_map/ppermute | solution.py:136
  110.4 8.0 %copy-start.4 = (bf16[2048,128]{1,0:T(8,128)(2,1)S(1)}, bf16[2048,128]{1,0:T(8,128)(2,1)}, u32[]{:S(2)}) copy-start(bf16[2048,128]{1,0:T(8,128)(2,1)} %copy-done.3) | copy-start | bytes 1572868
  110.4 8.0 %copy-start.20 = (bf16[2048,128]{1,0:T(8,128)(2,1)S(1)}, bf16[2048,128]{1,0:T(8,128)(2,1)}, u32[]{:S(2)}) copy-start(bf16[2048,128]{1,0:T(8,128)(2,1)} %copy-done.19) | copy-start | bytes 1572868
  126.7 9.8 %collective-permute-start.17 = (bf16[2048,128]{1,0:T(8,128)(2,1)}, bf16[2048,128]{1,0:T(8,128)(2,1)S(1)}, u32[]{:S(2)}, u32[]{:S(2)}) collective-permute-start(bf16[2048,128]{1,0:T(8,128)(2,1)} %collective-permute-done.16), channel_id=1, source_target_pairs={{0,16},{16,0},{1,17},{17,1},{2,18},{18,2},{3,19},{19,3},{4,20},{20... | collective-permute-start | bytes 1572872 | tf_op jit(solution)/shard_map/ppermute | solution.py:136
  147.0 1.6 copy-start.6
  147.6 11.0 %collective-permute-start.18 = (f32[1024,512]{0,1:T(8,128)S(1)}, f32[1024,512]{0,1:T(8,128)S(1)}, u32[]{:S(2)}, u32[]{:S(2)}) collective-permute-start(f32[1024,512]{0,1:T(8,128)S(1)} %select_bitcast_fusion), channel_id=1, source_target_pairs={{0,1},{1,0},{2,3},{3,2},{4,5},{5,4},{6,7},{7,6},{8,9},{9,8},{10,11... | collective-permute-start | bytes 6291464 | tf_op jit(solution)/shard_map/ppermute | solution.py:197
  154.3 3.0 %copy-start.9 = (bf16[1024,512]{1,0:T(8,128)(2,1)S(1)}, bf16[1024,512]{1,0:T(8,128)(2,1)}, u32[]{:S(2)}) copy-start(bf16[1024,512]{1,0:T(8,128)(2,1)} %param.11) | copy-start | bytes 3145732
  154.3 2.7 %collective-permute-start.13 = (f32[1024,256]{0,1:T(8,128)S(1)}, f32[1024,256]{0,1:T(8,128)S(1)}, u32[]{:S(2)}, u32[]{:S(2)}) collective-permute-start(f32[1024,256]{0,1:T(8,128)S(1)} %convolution_bitcast_fusion), channel_id=1, source_target_pairs={{0,1},{1,0},{2,3},{3,2},{4,5},{5,4},{6,7},{7,6},{8,9},{9,8},{10,11... | collective-permute-start | bytes 3145736 | tf_op jit(solution)/shard_map/ppermute | solution.py:83
  160.1 15.1 %all-to-all-start.4 = ((bf16[8,32,512]{2,1,0:T(8,128)(2,1)}), bf16[8,32,512]{2,1,0:T(8,128)(2,1)S(1)}, u32[]{:S(2)}, u32[]{:S(2)}) async-start(bf16[8,32,512]{2,1,0:T(8,128)(2,1)} %bitcast.53), calls=%async_computation.4 | async-start | bytes 524288 | tf_op jit(solution)/shard_map/all_to_all | solution.py:64

commit v3 on v2

--- a/solution.py
+++ b/solution.py
@@ -1,6 +1,10 @@
+import functools
+
 import jax
 import jax.numpy as jnp
 from jax import lax
+from jax.experimental import pallas as pl
+from jax.experimental.pallas import tpu as pltpu
 from jax.sharding import PartitionSpec as P
 
 BLOCK = 128
@@ -16,20 +20,109 @@
     )
 
 
-def after(value, *others):
-    return lax.optimization_barrier((value, *others))[0]
-
-
-def in_order(group, part, rest):
-    return jnp.where(
-        group == 0, jnp.concatenate([part, rest], 0), jnp.concatenate([rest, part], 0)
-    )
-
-
-def beside(side, part, other):
-    return jnp.where(
-        side == 0, jnp.concatenate([part, other], 1), jnp.concatenate([other, part], 1)
-    )
+LITTLE = pl.CostEstimate(flops=1_000_000, bytes_accessed=10_000, transcendentals=0)
+
+
+def cost(rows, depth, columns):
+    return pl.CostEstimate(
+        flops=2 * rows * depth * columns, bytes_accessed=2 * rows * depth, transcendentals=0
+    )
+
+
+VMEM_BYTES = 40 * 1024 * 1024
+
+
+def product_kernel(count, place_ref, tokens_ref, *refs):
+    pieces, out_ref, weight, sems = refs[:count], refs[count], refs[count + 1], refs[count + 2]
+
+    @pl.when(pl.program_id(0) == 0)
+    def _():
+        copies = []
+        for k, piece in enumerate(pieces):
+            depth = piece.shape[0]
+            row = pl.multiple_of(place_ref[2 * k] * depth, depth)
+            column = pl.multiple_of(place_ref[2 * k + 1] * piece.shape[1], piece.shape[1])
+            copies.append(
+                pltpu.make_async_copy(
+                    piece,
+                    weight.at[pl.ds(row, depth), pl.ds(column, piece.shape[1])],
+                    sems.at[k],
+                )
+            )
+        for copy in copies:
+            copy.start()
+        for copy in copies:
+            copy.wait()
+
+    out_ref[...] = jnp.dot(tokens_ref[...], weight[...], preferred_element_type=jnp.float32)
+
+
+def product(tokens, pieces, places, width, estimate):
+    rows, depth = tokens.shape
+    tile = rows // 4
+    return pl.pallas_call(
+        functools.partial(product_kernel, len(pieces)),
+        out_shape=jax.ShapeDtypeStruct((rows, width), jnp.float32),
+        grid_spec=pltpu.PrefetchScalarGridSpec(
+            num_scalar_prefetch=1,
+            grid=(rows // tile,),
+            in_specs=[pl.BlockSpec((tile, depth), lambda i, place: (i, 0))]
+            + [pl.BlockSpec(memory_space=pl.ANY)] * len(pieces),
+            out_specs=pl.BlockSpec((tile, width), lambda i, place: (i, 0)),
+            scratch_shapes=[
+                pltpu.VMEM((depth, width), jnp.bfloat16),
+                pltpu.SemaphoreType.DMA((len(pieces),)),
+            ],
+        ),
+        compiler_params=pltpu.CompilerParams(vmem_limit_bytes=VMEM_BYTES),
+        cost_estimate=estimate,
+        name="weight_product",
+    )(jnp.stack([jnp.int32(v) for place in places for v in place]), tokens, *pieces)
+
+
+def hidden_kernel(maps_ref, tokens_ref, out_ref):
+    out_ref[...] = dot(maps_ref[...], tokens_ref[...], ((1,), (1,)))
+
+
+def hidden_product(maps, tokens):
+    rows, depth = tokens.shape
+    tile = rows // 4
+    return pl.pallas_call(
+        hidden_kernel,
+        out_shape=jax.ShapeDtypeStruct((maps.shape[0], rows), jnp.float32),
+        grid=(rows // tile,),
+        in_specs=[
+            pl.BlockSpec(maps.shape, lambda i: (0, 0)),
+            pl.BlockSpec((tile, depth), lambda i: (i, 0)),
+        ],
+        out_specs=pl.BlockSpec((maps.shape[0], tile), lambda i: (0, i)),
+        compiler_params=pltpu.CompilerParams(vmem_limit_bytes=VMEM_BYTES),
+        cost_estimate=LITTLE,
+        name="hidden_product",
+    )(maps, tokens)
+
+
+def term_kernel(space_ref, tokens_ref, out_ref):
+    total = jnp.dot(space_ref[...], tokens_ref[...], preferred_element_type=jnp.float32)
+    out_ref[...] = (ADAPTER_SCALING * total).astype(jnp.bfloat16)
+
+
+def gradient_term(space, values):
+    rows, depth = values.shape
+    tile = depth // 8
+    return pl.pallas_call(
+        term_kernel,
+        out_shape=jax.ShapeDtypeStruct((space.shape[0], depth), jnp.bfloat16),
+        grid=(depth // tile,),
+        in_specs=[
+            pl.BlockSpec(space.shape, lambda i: (0, 0)),
+            pl.BlockSpec((rows, tile), lambda i: (0, i)),
+        ],
+        out_specs=pl.BlockSpec((space.shape[0], tile), lambda i: (0, i)),
+        compiler_params=pltpu.CompilerParams(vmem_limit_bytes=VMEM_BYTES),
+        cost_estimate=LITTLE,
+        name="gradient_term",
+    )(space, values)
 
 
 class Adapters:
@@ -52,9 +145,9 @@
             jnp.where(match, (block_local - self.ten_dev)[:, None], 0), axis=0
         )
         columns = self.peers * self.rank
-        row_home = jnp.broadcast_to(block_home[:, None], (blocks, BLOCK)).reshape(-1, 1)
-        home_of = lax.broadcasted_iota(jnp.int32, (self.rows, columns), 1) // self.rank
-        self.counted = (row_home == home_of) & (row_tenant != tenants_all)[:, None]
+        row_home = jnp.broadcast_to(block_home[:, None], (blocks, BLOCK)).reshape(1, -1)
+        home_of = lax.broadcasted_iota(jnp.int32, (columns, self.rows), 0) // self.rank
+        self.counted = (row_home == home_of) & (row_tenant != tenants_all)[None, :]
         output_columns = cotangent.shape[1]
         column = lax.axis_index("tensor") * output_columns
         self.own_a = adapt_a
@@ -83,8 +176,8 @@
         total = part + lax.ppermute(part, "tensor", SWAP)
         return jnp.where(self.counted, total, 0.0).astype(jnp.bfloat16)
 
-    def term(self, left, right):
-        return (ADAPTER_SCALING * dot(left, right, ((0,), (0,)))).astype(jnp.bfloat16)
+    def term(self, space, values):
+        return (ADAPTER_SCALING * dot(space, values, ((1,), (0,)))).astype(jnp.bfloat16)
 
     def total(self, came):
         return (
@@ -104,11 +197,11 @@
     base = lax.psum_scatter(full, "tensor", scatter_dimension=1, tiled=True)
     got_b = adapters.exchange(adapters.chosen(adapters.own_b))
     got_a = adapters.exchange(adapters.chosen(adapters.own_a))
-    backward_pass = adapters.rank_space(dot(adapters.cotangent, got_b, ((1,), (1,))))
+    backward_pass = adapters.rank_space(dot(got_b, adapters.cotangent, ((1,), (1,))))
     came_a = adapters.exchange(adapters.term(backward_pass, tokens))
-    hidden = adapters.rank_space(dot(tokens, got_a, ((1,), (1,))))
+    hidden = adapters.rank_space(dot(got_a, tokens, ((1,), (1,))))
     came_b = adapters.exchange(adapters.term(hidden, adapters.cotangent))
-    added = ADAPTER_SCALING * dot(hidden, got_b, ((1,), (0,)))
+    added = ADAPTER_SCALING * dot(hidden, got_b, ((0,), (0,)))
     return (
         (base + added).astype(jnp.bfloat16),
         adapters.total(came_a),
@@ -135,7 +228,9 @@
     def twin(part):
         return lax.ppermute(part, "groups", SWAP)
 
+    output_columns = cotangent.shape[1]
     barrier = lax.optimization_barrier
+
     half = lax.dynamic_slice_in_dim(base_weight, group * (width // 2), width // 2, 0)
     near = over(half, pair)
     mid_next = over(half, middle)
@@ -159,38 +254,80 @@
     following_across = over(following, across)
     following_rest = twin(following)
     near_across_rest = twin(near_across)
-    backward_pass = work.rank_space(dot(cotangent, got_b, ((1,), (1,))))
-    home_a = work.term(backward_pass, tokens)
-    own = beside(side, base_weight, in_order(group, own_across, own_across_rest))
-    got_a, home_a, end_far, following_across, following_rest, near_across_rest, own = barrier(
-        (got_a, home_a, end_far, following_across, following_rest, near_across_rest, own)
+    backward_pass = work.rank_space(dot(got_b, cotangent, ((1,), (1,))))
+    home_a = gradient_term(backward_pass, tokens)
+    following_across_rest = twin(following_across)
+    end_far, home_a = barrier((end_far, home_a))
+    far = jnp.where(inner, mid_far, end_far)
+    (
+        got_a,
+        home_a,
+        far,
+        following_across,
+        following_rest,
+        following_across_rest,
+        near_across_rest,
+    ) = barrier(
+        (
+            got_a,
+            home_a,
+            far,
+            following_across,
+            following_rest,
+            following_across_rest,
+            near_across_rest,
+        )
     )
     came_a = work.exchange(home_a)
-    far = jnp.where(inner, mid_far, end_far)
     far_across = over(far, across)
     far_rest = twin(far)
-    following_across_rest = twin(following_across)
+    parity = layer % 2
+    product_here = product(
+        tokens,
+        [
+            base_weight,
+            own_across,
+            own_across_rest,
+            near,
+            near_rest,
+            near_across,
+            near_across_rest,
+        ],
+        [
+            (0, 2 * parity + side),
+            (group, 2 * parity + 1 - side),
+            (1 - group, 2 * parity + 1 - side),
+            (group, 2 * (1 - parity) + side),
+            (1 - group, 2 * (1 - parity) + side),
+            (group, 2 * (1 - parity) + 1 - side),
+            (1 - group, 2 * (1 - parity) + 1 - side),
+        ],
+        output_columns,
+        cost(*tokens.shape, output_columns),
+    )
+    got_a, product_here, far_rest, far_across = barrier(
+        (got_a, product_here, far_rest, far_across)
+    )
     far_across_rest = twin(far_across)
-    near = beside(
-        side, in_order(group, near, near_rest), in_order(group, near_across, near_across_rest)
-    )
-    here = jnp.where(
-        layer % 2 == 0, jnp.concatenate([own, near], 1), jnp.concatenate([near, own], 1)
-    )
-    product_here = jnp.dot(tokens, here, preferred_element_type=jnp.float32)
-    hidden = work.rank_space(dot(tokens, got_a, ((1,), (1,))))
+    halves = [
+        product(
+            tokens,
+            list(pieces),
+            [(row, column) for column in (side, 1 - side) for row in (group, 1 - group)],
+            output_columns // 2,
+            LITTLE,
+        )
+        for pieces in (
+            (following, following_rest, following_across, following_across_rest),
+            (far, far_rest, far_across, far_across_rest),
+        )
+    ]
+    product_there = jnp.where(
+        layer < 2, jnp.concatenate(halves, 1), jnp.concatenate(halves[::-1], 1)
+    )
+    hidden = work.rank_space(hidden_product(got_a, tokens))
     home_b = work.term(hidden, cotangent)
-    added = ADAPTER_SCALING * dot(hidden, got_b, ((1,), (0,)))
-    following = beside(
-        side,
-        in_order(group, following, following_rest),
-        in_order(group, following_across, following_across_rest),
-    )
-    far = beside(side, in_order(group, far, far_rest), in_order(group, far_across, far_across_rest))
-    there = jnp.where(
-        layer < 2, jnp.concatenate([following, far], 1), jnp.concatenate([far, following], 1)
-    )
-    product_there = jnp.dot(tokens, there, preferred_element_type=jnp.float32)
+    added = ADAPTER_SCALING * dot(hidden, got_b, ((0,), (0,)))
     keep_here = layer // 2 == core
     keep = jnp.where(keep_here, product_here, product_there)
     give = jnp.where(keep_here, product_there, product_here)

time: 177 us -> 171 us (0.966)
  matrix products: 38.2 us -> 11.9 us
  Pallas kernels: 0 us -> 25.2 us
  local copies, waits for them, and re-layouts: 9.85 us -> 28.9 us
  other arithmetic: 19.9 us -> 4.29 us
  waiting for transfers between devices: 58.6 us -> 50.7 us
    pallas_call x0 -> x5, Pallas kernels: none -> 25.2 us  [the longest x3 17.8 us: product(): pl.pallas_call(functools.partial(product_kernel, len(pieces)), out_shape=...]
    unnamed x49 -> x62, local copies, waits for them, and re-layouts: 6.07 us -> 24.9 us
    dot_general x2 -> x0, matrix products: 16.2 us -> none  [the longest x1 8.17 us: shards(): product_there = jnp.dot(tokens, there, preferred_element_type=jnp.float32)]
    select_n x11 -> x0, other arithmetic: 14.4 us -> none  [the longest x7 9.86 us: in_order(): jnp.where(group == 0, jnp.concatenate([part, rest], 0), jnp.concatenate([...]
    dot_general x9 -> x7, matrix products: 22 us -> 11.9 us  [dot(): lax.dot_general(left, right, ((contract[0], contract[1]), ((), ())), pref...]
    all_to_all x5, waiting for transfers between devices: 26.8 us -> 22.3 us  [exchange(): lax.all_to_all(sent.reshape(self.peers, -1, sent.shape[1]), 'dp', split_a...]
    ppermute x7, waiting for transfers between devices: 4.82 us -> 1.07 us  [twin(): return lax.ppermute(part, 'groups', SWAP)]
  transfers between devices with their start and end apart: 24 -> 24, of which waited for: 10 -> 7; matrix products, arithmetic and copies ran while one was open for 34% -> 11% of each run, Pallas kernels for 0% -> 15%
where the time goes in v3:
time: 171 us; the launch traced here: 170 us
  waiting for transfers between devices  50.7 us (30%)
  starting transfers between devices  48 us (28%)
  local copies, waits for them, and re-layouts  28.9 us (17%)
  Pallas kernels  25.2 us (15%)
  matrix products  11.9 us (7%)
  other arithmetic  4.29 us (3%)
    ppermute x9, waiting for transfers between devices, over(): return lax.ppermute(part, 'dp', pairs)  25.1 us
    unnamed x62, local copies, waits for them, and re-layouts  24.9 us
    all_to_all x5, starting transfers between devices, exchange(): lax.all_to_all(sent.reshape(self.peers, -1, sent.shape[1]), 'dp', split_a...  24.8 us
    all_to_all x5, waiting for transfers between devices, exchange(): lax.all_to_all(sent.reshape(self.peers, -1, sent.shape[1]), 'dp', split_a...  22.3 us
    pallas_call x3, Pallas kernels, product(): pl.pallas_call(functools.partial(product_kernel, len(pieces)), out_shape=...  17.8 us
    ppermute x9, starting transfers between devices, over(): return lax.ppermute(part, 'dp', pairs)  15.7 us
    dot_general x7, matrix products, dot(): lax.dot_general(left, right, ((contract[0], contract[1]), ((), ())), pref...  11.9 us
    ppermute x7, starting transfers between devices, twin(): return lax.ppermute(part, 'groups', SWAP)  6.79 us
  transfers between devices with their start and end apart: 24, of which 7 were waited for; matrix products, arithmetic and copies ran while one was open for 11% of the time, Pallas kernels for 15%

profile of v3, /device:TPU:0, one launch (start us, length us, event | category | flops | bytes accessed | tf_op | source)
XLA Modules:
  0.0 170.1 jit_solution(13244862383926491312)
XLA Ops:
  0.7 1.2 constant_dynamic-slice_fusion.1
  1.8 3.0 %collective-permute-start.2 = (bf16[2048,128]{1,0:T(8,128)(2,1)S(1)}, bf16[2048,128]{1,0:T(8,128)(2,1)S(1)}, u32[]{:S(2)}, u32[]{:S(2)}) collective-permute-start(bf16[2048,128]{1,0:T(8,128)(2,1)S(1)} %constant_dynamic-slice_fusion.1), channel_id=1, source_target_pairs={{0,2},{2,0},{4,6},{6,4},{8,10},{10,8},{12,14},{14,12},{1,3},{3,1},... | collective-permute-start | bytes 1572872 | tf_op jit(solution)/shard_map/ppermute | solution.py:226
  5.5 4.4 %collective-permute-start = (bf16[2048,128]{1,0:T(8,128)(2,1)S(1)}, bf16[2048,128]{1,0:T(8,128)(2,1)S(1)}, u32[]{:S(2)}, u32[]{:S(2)}) collective-permute-start(bf16[2048,128]{1,0:T(8,128)(2,1)S(1)} %constant_dynamic-slice_fusion.1), channel_id=1, source_target_pairs={{0,4},{2,6},{4,0},{6,2},{8,12},{10,14},{12,8},{14,10},{1,5},{3,7},... | collective-permute-start | bytes 1572872 | tf_op jit(solution)/shard_map/ppermute | solution.py:226
  12.4 3.3 %all-to-all-start = ((s32[8,1,1]{2,1,0:T(1,128)}), s32[8,1,1]{2,1,0:T(1,128)S(1)}, u32[]{:S(2)}, u32[]{:S(2)}) async-start(s32[8,1,1]{2,1,0:T(1,128)} %copy.12), calls=%async_computation | async-start | bytes 8192 | tf_op jit(solution)/shard_map/all_to_all | solution.py:157
  16.7 5.7 %all-to-all-done = s32[8,1,1]{2,1,0:T(1,128)S(1)} async-done(((s32[8,1,1]{2,1,0:T(1,128)}), s32[8,1,1]{2,1,0:T(1,128)S(1)}, u32[]{:S(2)}, u32[]{:S(2)}) %all-to-all-start) | async-done | bytes 64 | tf_op jit(solution)/shard_map/all_to_all | solution.py:157
  23.5 1.5 collective-permute-start.6
  25.0 1.5 collective-permute-start.5
  26.5 1.4 collective-permute-start.3
  28.1 1.3 collective-permute-start.4
  31.0 5.7 %all-to-all-start.1 = ((bf16[8,32,512]{2,1,0:T(8,128)(2,1)}), bf16[8,32,512]{2,1,0:T(8,128)(2,1)S(1)}, u32[]{:S(2)}, u32[]{:S(2)}) async-start(bf16[8,32,512]{2,1,0:T(8,128)(2,1)} %bitcast.45), calls=%async_computation.1 | async-start | bytes 524288 | tf_op jit(solution)/shard_map/all_to_all | solution.py:157
  36.7 2.2 %convolution_convert_fusion = bf16[256,4096]{1,0:T(8,128)(2,1)} fusion(bf16[128,4096]{1,0:T(8,128)(2,1)S(1)} %bitcast.37, s32[128]{0:T(128)S(1)} %get-tuple-element.64, s32[128]{0:T(128)S(1)} %get-tuple-element.65, s32[256]{0:T(256)S(1)} %get-tuple-element.61, s32[256]{0:T(256)S(1)} %get-tuple-element.62, s32[128]{0:T(128)S(1)} %get-tuple-element.63, ...), kind=kOutput, calls=%fused_computation | convolution fusion | flops 269680640 | bytes 3151360 | tf_op jit(solution)/shard_map/dot_general | solution.py:18
  38.8 6.9 %all-to-all-done.1 = bf16[8,32,512]{2,1,0:T(8,128)(2,1)S(1)} async-done(((bf16[8,32,512]{2,1,0:T(8,128)(2,1)}), bf16[8,32,512]{2,1,0:T(8,128)(2,1)S(1)}, u32[]{:S(2)}, u32[]{:S(2)}) %all-to-all-start.1) | async-done | bytes 262176 | tf_op jit(solution)/shard_map/all_to_all | solution.py:157
  45.7 1.1 collective-permute-done.7.refs_2_
  48.4 4.6 %all-to-all-start.2 = ((bf16[8,32,4096]{2,1,0:T(8,128)(2,1)}), bf16[8,32,4096]{2,1,0:T(8,128)(2,1)S(1)}, u32[]{:S(2)}, u32[]{:S(2)}) async-start(bf16[8,32,4096]{2,1,0:T(8,128)(2,1)} %bitcast.40), calls=%async_computation.2 | async-start | bytes 4194304 | tf_op jit(solution)/shard_map/all_to_all | solution.py:157
  53.1 1.8 %fusion.11 = f32[256,1024]{1,0:T(8,128)S(1)} fusion(bf16[256,512]{1,0:T(8,128)(2,1)S(1)} %bitcast.41, bf16[1024,512]{1,0:T(8,128)(2,1)} %param.11), kind=kOutput, calls=%fused_computation.49 | convolution fusion | flops 268435456 | bytes 2359296 | tf_op jit(solution)/shard_map/dot_general | solution.py:18
  54.9 1.1 broadcast_select_fusion.refs_0_
  56.0 2.1 %collective-permute-start.10 = (bf16[2048,128]{1,0:T(8,128)(2,1)S(1)}, bf16[2048,128]{1,0:T(8,128)(2,1)S(1)}, u32[]{:S(2)}, u32[]{:S(2)}) collective-permute-start(bf16[2048,128]{1,0:T(8,128)(2,1)S(1)} %broadcast_select_fusion.refs_0_), channel_id=1, source_target_pairs={{0,2},{2,0},{4,6},{6,4},{8,10},{10,8},{12,14},{14,12},{1,3},{3,1},... | collective-permute-start | bytes 1572872 | tf_op jit(solution)/shard_map/ppermute | solution.py:226
  58.2 1.3 collective-permute-start.8
  59.5 1.6 collective-permute-start.11
  61.6 25.1 %collective-permute-done.10.refs_2_ = bf16[2048,128]{1,0:T(8,128)(2,1)S(1)} collective-permute-done((bf16[2048,128]{1,0:T(8,128)(2,1)S(1)}, bf16[2048,128]{1,0:T(8,128)(2,1)S(1)}, u32[]{:S(2)}, u32[]{:S(2)}) %collective-permute-start.10) | collective-permute-done | bytes 524320 | tf_op jit(solution)/shard_map/ppermute | solution.py:226
  86.7 1.5 collective-permute-start.12
  88.5 3.4 %copy-done.1 = bf16[1024,4096]{1,0:T(8,128)(2,1)S(1)} copy-done((bf16[1024,4096]{1,0:T(8,128)(2,1)S(1)}, bf16[1024,4096]{1,0:T(8,128)(2,1)}, u32[]{:S(2)}) %copy-start.1) | copy-done | bytes 8388632
  91.8 4.3 %gradient_term.1 = bf16[256,4096]{1,0:T(8,128)(2,1)S(1)} custom-call(bf16[256,1024]{1,0:T(8,128)(2,1)S(1)} %select_convert_fusion.1.space_ref, bf16[1024,4096]{1,0:T(8,128)(2,1)S(1)} %copy-done.1), custom_call_target="tpu_custom_call" | custom-call | flops 1000000 | bytes 10000 | tf_op jit(solution)/shard_map/gradient_term/pallas_call | solution.py:113
  96.2 1.3 copy-done.3
  101.5 7.8 %all-to-all-start.3 = ((bf16[8,32,4096]{2,1,0:T(8,128)(2,1)}), bf16[8,32,4096]{2,1,0:T(8,128)(2,1)}, u32[]{:S(2)}, u32[]{:S(2)}) async-start(bf16[8,32,4096]{2,1,0:T(8,128)(2,1)} %bitcast.39), calls=%async_computation.3 | async-start | bytes 4194304 | tf_op jit(solution)/shard_map/all_to_all | solution.py:157
  109.3 1.2 copy-done.15
  110.6 1.0 copy-done.17
  111.6 1.0 copy-done.19
  112.6 1.0 copy-done.21
  113.7 1.0 copy-done.24
  114.7 1.0 copy-done.26
  115.8 9.1 %weight_product.3 = f32[1024,512]{1,0:T(8,128)S(1)} custom-call(s32[14]{0:T(128)S(1)} %stack.26.place_ref, bf16[1024,4096]{1,0:T(8,128)(2,1)} %tokens_ref.9, bf16[4096,128]{1,0:T(8,128)(2,1)S(1)} %copy-done.15, bf16[2048,128]{1,0:T(8,128)(2,1)S(1)} %copy-done.17, bf16[2048,128]{1,0:T(8,128)(2,1)} %collective-permute-done.7.refs_2_, ...), custom_call_target="tpu_custom_call" | custom-call | flops 4294967296 | bytes 8388608 | tf_op jit(solution)/shard_map/weight_product/pallas_call | solution.py:63
  124.8 1.3 copy-done.4
  126.8 3.4 %copy-done.2 = bf16[1024,4096]{1,0:T(8,128)(2,1)S(1)} copy-done((bf16[1024,4096]{1,0:T(8,128)(2,1)S(1)}, bf16[1024,4096]{1,0:T(8,128)(2,1)}, u32[]{:S(2)}) %copy-start.2) | copy-done | bytes 8388632
  130.2 1.0 copy-done.7
  131.3 1.0 copy-done.10
  133.3 1.0 copy-done.14
  134.4 3.8 %weight_product.4 = f32[1024,256]{1,0:T(8,128)S(1)} custom-call(s32[8]{0:T(128)S(1)} %stack.29.place_ref, bf16[1024,4096]{1,0:T(8,128)(2,1)S(1)} %copy-done.2, bf16[2048,128]{1,0:T(8,128)(2,1)S(1)} %copy-done.7, bf16[2048,128]{1,0:T(8,128)(2,1)S(1)} %copy-done.12, bf16[2048,128]{1,0:T(8,128)(2,1)S(1)} %copy-done.10, bf16[2048,128]{1,0:T(8,128)(2,1)S(1)} %copy-done.14), custom_call_target="tpu_custom_call" | custom-call | flops 1000000 | bytes 10000 | tf_op jit(solution)/shard_map/weight_product/pallas_call | solution.py:63
  138.2 4.9 %weight_product.5 = f32[1024,256]{1,0:T(8,128)S(1)} custom-call(s32[8]{0:T(128)S(1)} %stack.29.place_ref, bf16[1024,4096]{1,0:T(8,128)(2,1)S(1)} %copy-done.2, bf16[2048,128]{1,0:T(8,128)(2,1)S(1)} %copy-done.8, bf16[2048,128]{1,0:T(8,128)(2,1)} %collective-permute-done.14.refs_1_, bf16[2048,128]{1,0:T(8,128)(2,1)} %collective-permute-done.15.refs_2_, ...), custom_call_target="tpu_custom_call" | custom-call | flops 1000000 | bytes 10000 | tf_op jit(solution)/shard_map/weight_product/pallas_call | solution.py:63
  143.8 3.0 %hidden_product.1 = f32[256,1024]{1,0:T(8,128)S(1)} custom-call(bf16[256,4096]{1,0:T(8,128)(2,1)S(1)} %bitcast.38, bf16[1024,4096]{1,0:T(8,128)(2,1)S(1)} %copy-done.2), custom_call_target="tpu_custom_call" | custom-call | flops 1000000 | bytes 10000 | tf_op jit(solution)/shard_map/hidden_product/pallas_call | solution.py:90
  147.4 2.3 %collective-permute-done.16 = f32[256,1024]{1,0:T(8,128)S(1)} collective-permute-done((f32[256,1024]{1,0:T(8,128)S(1)}, f32[256,1024]{1,0:T(8,128)S(1)}, u32[]{:S(2)}, u32[]{:S(2)}) %collective-permute-start.16) | collective-permute-done | bytes 1048608 | tf_op jit(solution)/shard_map/ppermute | solution.py:176
  150.0 1.2 fusion.1
  151.1 1.5 add_convert_fusion
  152.7 3.5 %all-to-all-done.3 = bf16[8,32,4096]{2,1,0:T(8,128)(2,1)} async-done(((bf16[8,32,4096]{2,1,0:T(8,128)(2,1)}), bf16[8,32,4096]{2,1,0:T(8,128)(2,1)}, u32[]{:S(2)}, u32[]{:S(2)}) %all-to-all-start.3) | async-done | bytes 2097184 | tf_op jit(solution)/shard_map/all_to_all | solution.py:157
  156.1 3.5 %all-to-all-start.4 = ((bf16[8,32,512]{2,1,0:T(8,128)(2,1)}), bf16[8,32,512]{2,1,0:T(8,128)(2,1)S(1)}, u32[]{:S(2)}, u32[]{:S(2)}) async-start(bf16[8,32,512]{2,1,0:T(8,128)(2,1)} %bitcast.21), calls=%async_computation.4 | async-start | bytes 524288 | tf_op jit(solution)/shard_map/all_to_all | solution.py:157
  159.6 3.2 %convolution_convert_fusion.1 = bf16[128,4096]{1,0:T(8,128)(2,1)} fusion(bf16[256,4096]{1,0:T(8,128)(2,1)} %bitcast.11, s32[128]{0:T(128)S(1)} %get-tuple-element.64, s32[128]{0:T(128)S(1)} %get-tuple-element.65, s32[256]{0:T(256)S(1)} %get-tuple-element.61, s32[256]{0:T(256)S(1)} %get-tuple-element.62, s32[128]{0:T(128)S(1)} %get-tuple-element.63, ...), kind=kOutput, calls=%fused_computation.1 | convolution fusion | flops 269156352 | bytes 3151360 | tf_op jit(solution)/shard_map/dot_general | solution.py:18
  162.8 6.2 %all-to-all-done.4 = bf16[8,32,512]{2,1,0:T(8,128)(2,1)S(1)} async-done(((bf16[8,32,512]{2,1,0:T(8,128)(2,1)}), bf16[8,32,512]{2,1,0:T(8,128)(2,1)S(1)}, u32[]{:S(2)}, u32[]{:S(2)}) %all-to-all-start.4) | async-done | bytes 262176 | tf_op jit(solution)/shard_map/all_to_all | solution.py:157
  169.0 1.1 convolution_convert_fusion.3
  (102 shorter events, 16.6 us)
Async XLA Ops:
  0.6 36.0 %copy-start = (bf16[4,32,4096]{2,1,0:T(8,128)(2,1)S(1)}, bf16[4,32,4096]{2,1,0:T(8,128)(2,1)}, u32[]{:S(2)}) copy-start(bf16[4,32,4096]{2,1,0:T(8,128)(2,1)} %param.9) | copy-start | bytes 3145732
  1.8 20.8 %collective-permute-start.2 = (bf16[2048,128]{1,0:T(8,128)(2,1)S(1)}, bf16[2048,128]{1,0:T(8,128)(2,1)S(1)}, u32[]{:S(2)}, u32[]{:S(2)}) collective-permute-start(bf16[2048,128]{1,0:T(8,128)(2,1)S(1)} %constant_dynamic-slice_fusion.1), channel_id=1, source_target_pairs={{0,2},{2,0},{4,6},{6,4},{8,10},{10,8},{12,14},{14,12},{1,3},{3,1},... | collective-permute-start | bytes 1572872 | tf_op jit(solution)/shard_map/ppermute | solution.py:226
  4.9 17.8 %collective-permute-start.1 = (bf16[2048,128]{1,0:T(8,128)(2,1)S(1)}, bf16[2048,128]{1,0:T(8,128)(2,1)S(1)}, u32[]{:S(2)}, u32[]{:S(2)}) collective-permute-start(bf16[2048,128]{1,0:T(8,128)(2,1)S(1)} %constant_dynamic-slice_fusion.1), channel_id=1, source_target_pairs={{4,8},{6,10},{8,4},{10,6},{5,9},{7,11},{9,5},{11,7},{20,24},{22,26... | collective-permute-start | bytes 1572872 | tf_op jit(solution)/shard_map/ppermute | solution.py:226
  5.5 17.2 %collective-permute-start = (bf16[2048,128]{1,0:T(8,128)(2,1)S(1)}, bf16[2048,128]{1,0:T(8,128)(2,1)S(1)}, u32[]{:S(2)}, u32[]{:S(2)}) collective-permute-start(bf16[2048,128]{1,0:T(8,128)(2,1)S(1)} %constant_dynamic-slice_fusion.1), channel_id=1, source_target_pairs={{0,4},{2,6},{4,0},{6,2},{8,12},{10,14},{12,8},{14,10},{1,5},{3,7},... | collective-permute-start | bytes 1572872 | tf_op jit(solution)/shard_map/ppermute | solution.py:226
  12.4 10.0 %all-to-all-start = ((s32[8,1,1]{2,1,0:T(1,128)}), s32[8,1,1]{2,1,0:T(1,128)S(1)}, u32[]{:S(2)}, u32[]{:S(2)}) async-start(s32[8,1,1]{2,1,0:T(1,128)} %copy.12), calls=%async_computation | async-start | bytes 8192 | tf_op jit(solution)/shard_map/all_to_all | solution.py:157
  22.7 24.9 %copy-start.16 = (bf16[2048,128]{1,0:T(8,128)(2,1)}, bf16[2048,128]{1,0:T(8,128)(2,1)S(1)}, u32[]{:S(2)}) copy-start(bf16[2048,128]{1,0:T(8,128)(2,1)S(1)} %collective-permute-done.2.refs_1_) | copy-start | bytes 1572868
  22.7 24.9 %copy-start.18 = (bf16[2048,128]{1,0:T(8,128)(2,1)}, bf16[2048,128]{1,0:T(8,128)(2,1)S(1)}, u32[]{:S(2)}) copy-start(bf16[2048,128]{1,0:T(8,128)(2,1)S(1)} %collective-permute-done.refs_3_) | copy-start | bytes 1572868
  23.5 23.2 %collective-permute-start.6 = (bf16[2048,128]{1,0:T(8,128)(2,1)S(1)}, bf16[2048,128]{1,0:T(8,128)(2,1)S(1)}, u32[]{:S(2)}, u32[]{:S(2)}) collective-permute-start(bf16[2048,128]{1,0:T(8,128)(2,1)S(1)} %collective-permute-done.refs_3_), channel_id=1, source_target_pairs={{0,16},{16,0},{1,17},{17,1},{2,18},{18,2},{3,19},{19,3},{4,20},{20... | collective-permute-start | bytes 1572872 | tf_op jit(solution)/shard_map/ppermute | solution.py:229
  25.0 22.5 %collective-permute-start.5 = (bf16[2048,128]{1,0:T(8,128)(2,1)S(1)}, bf16[2048,128]{1,0:T(8,128)(2,1)S(1)}, u32[]{:S(2)}, u32[]{:S(2)}) collective-permute-start(bf16[2048,128]{1,0:T(8,128)(2,1)S(1)} %collective-permute-done.refs_3_), channel_id=1, source_target_pairs={{0,2},{2,0},{4,6},{6,4},{8,10},{10,8},{12,14},{14,12},{1,3},{3,1},... | collective-permute-start | bytes 1572872 | tf_op jit(solution)/shard_map/ppermute | solution.py:226
  26.5 21.1 %collective-permute-start.3 = (bf16[2048,128]{1,0:T(8,128)(2,1)S(1)}, bf16[2048,128]{1,0:T(8,128)(2,1)}, u32[]{:S(2)}, u32[]{:S(2)}) collective-permute-start(bf16[2048,128]{1,0:T(8,128)(2,1)S(1)} %collective-permute-done.refs_3_), channel_id=1, source_target_pairs={{4,8},{6,10},{8,4},{10,6},{5,9},{7,11},{9,5},{11,7},{20,24},{22,26... | collective-permute-start | bytes 1572872 | tf_op jit(solution)/shard_map/ppermute | solution.py:226
  28.1 17.6 %collective-permute-start.4 = (bf16[2048,128]{1,0:T(8,128)(2,1)}, bf16[2048,128]{1,0:T(8,128)(2,1)}, u32[]{:S(2)}, u32[]{:S(2)}) collective-permute-start(bf16[2048,128]{1,0:T(8,128)(2,1)} %copy-done.28), channel_id=1, source_target_pairs={{4,0},{6,2},{8,12},{10,14},{5,1},{7,3},{9,13},{11,15},{20,16},{22,... | collective-permute-start | bytes 1572872 | tf_op jit(solution)/shard_map/ppermute | solution.py:226
  29.4 17.4 %collective-permute-start.7 = (bf16[2048,128]{1,0:T(8,128)(2,1)S(1)}, bf16[2048,128]{1,0:T(8,128)(2,1)}, u32[]{:S(2)}, u32[]{:S(2)}) collective-permute-start(bf16[2048,128]{1,0:T(8,128)(2,1)S(1)} %collective-permute-done.2.refs_1_), channel_id=1, source_target_pairs={{0,16},{16,0},{1,17},{17,1},{2,18},{18,2},{3,19},{19,3},{4,20},{20... | collective-permute-start | bytes 1572872 | tf_op jit(solution)/shard_map/ppermute | solution.py:229
  31.0 14.7 %all-to-all-start.1 = ((bf16[8,32,512]{2,1,0:T(8,128)(2,1)}), bf16[8,32,512]{2,1,0:T(8,128)(2,1)S(1)}, u32[]{:S(2)}, u32[]{:S(2)}) async-start(bf16[8,32,512]{2,1,0:T(8,128)(2,1)} %bitcast.45), calls=%async_computation.1 | async-start | bytes 524288 | tf_op jit(solution)/shard_map/all_to_all | solution.py:157
  48.4 52.5 %all-to-all-start.2 = ((bf16[8,32,4096]{2,1,0:T(8,128)(2,1)}), bf16[8,32,4096]{2,1,0:T(8,128)(2,1)S(1)}, u32[]{:S(2)}, u32[]{:S(2)}) async-start(bf16[8,32,4096]{2,1,0:T(8,128)(2,1)} %bitcast.40), calls=%async_computation.2 | async-start | bytes 4194304 | tf_op jit(solution)/shard_map/all_to_all | solution.py:157
  53.0 6.5 %copy-start.30 = (s32[1024]{0:T(1024)S(1)}, s32[1024]{0:T(1024)}, u32[]{:S(2)}) copy-start(s32[1024]{0:T(1024)} %param.12) | copy-start | bytes 12292
  53.0 1.9 %copy-start.29 = (bf16[2048,128]{1,0:T(8,128)(2,1)S(1)}, bf16[2048,128]{1,0:T(8,128)(2,1)}, u32[]{:S(2)}) copy-start(bf16[2048,128]{1,0:T(8,128)(2,1)} %copy-done.28) | copy-start | bytes 1572868
  53.0 8.0 %copy-start.23 = (bf16[2048,128]{1,0:T(8,128)(2,1)S(1)}, bf16[2048,128]{1,0:T(8,128)(2,1)}, u32[]{:S(2)}) copy-start(bf16[2048,128]{1,0:T(8,128)(2,1)} %copy-done.22) | copy-start | bytes 1572868
  54.8 33.3 %collective-permute-start.9 = (f32[256,1024]{1,0:T(8,128)S(1)}, f32[256,1024]{1,0:T(8,128)S(1)}, u32[]{:S(2)}, u32[]{:S(2)}) collective-permute-start(f32[256,1024]{1,0:T(8,128)S(1)} %fusion.11), channel_id=1, source_target_pairs={{0,1},{1,0},{2,3},{3,2},{4,5},{5,4},{6,7},{7,6},{8,9},{9,8},{10,11... | collective-permute-start | bytes 3145736 | tf_op jit(solution)/shard_map/ppermute | solution.py:176
  56.0 40.1 %copy-start.6 = (bf16[2048,128]{1,0:T(8,128)(2,1)}, bf16[2048,128]{1,0:T(8,128)(2,1)S(1)}, u32[]{:S(2)}) copy-start(bf16[2048,128]{1,0:T(8,128)(2,1)S(1)} %broadcast_select_fusion.refs_0_) | copy-start | bytes 1572868
  56.0 30.6 %collective-permute-start.10 = (bf16[2048,128]{1,0:T(8,128)(2,1)S(1)}, bf16[2048,128]{1,0:T(8,128)(2,1)S(1)}, u32[]{:S(2)}, u32[]{:S(2)}) collective-permute-start(bf16[2048,128]{1,0:T(8,128)(2,1)S(1)} %broadcast_select_fusion.refs_0_), channel_id=1, source_target_pairs={{0,2},{2,0},{4,6},{6,4},{8,10},{10,8},{12,14},{14,12},{1,3},{3,1},... | collective-permute-start | bytes 1572872 | tf_op jit(solution)/shard_map/ppermute | solution.py:226
  58.2 39.4 %collective-permute-start.8 = (bf16[2048,128]{1,0:T(8,128)(2,1)}, bf16[2048,128]{1,0:T(8,128)(2,1)S(1)}, u32[]{:S(2)}, u32[]{:S(2)}) collective-permute-start(bf16[2048,128]{1,0:T(8,128)(2,1)} %collective-permute-done.3), channel_id=1, source_target_pairs={{4,0},{6,2},{8,12},{10,14},{5,1},{7,3},{9,13},{11,15},{20,16},{22,... | collective-permute-start | bytes 1572872 | tf_op jit(solution)/shard_map/ppermute | solution.py:226
  59.5 38.9 %collective-permute-start.11 = (bf16[2048,128]{1,0:T(8,128)(2,1)S(1)}, bf16[2048,128]{1,0:T(8,128)(2,1)S(1)}, u32[]{:S(2)}, u32[]{:S(2)}) collective-permute-start(bf16[2048,128]{1,0:T(8,128)(2,1)S(1)} %broadcast_select_fusion.refs_0_), channel_id=1, source_target_pairs={{0,16},{16,0},{1,17},{17,1},{2,18},{18,2},{3,19},{19,3},{4,20},{20... | collective-permute-start | bytes 1572872 | tf_op jit(solution)/shard_map/ppermute | solution.py:229
  61.1 38.2 %collective-permute-start.13 = (bf16[2048,128]{1,0:T(8,128)(2,1)S(1)}, bf16[2048,128]{1,0:T(8,128)(2,1)S(1)}, u32[]{:S(2)}, u32[]{:S(2)}) collective-permute-start(bf16[2048,128]{1,0:T(8,128)(2,1)S(1)} %copy-done.23), channel_id=1, source_target_pairs={{0,16},{16,0},{1,17},{17,1},{2,18},{18,2},{3,19},{19,3},{4,20},{20... | collective-permute-start | bytes 1572872 | tf_op jit(solution)/shard_map/ppermute | solution.py:229
  86.7 9.5 %copy-start.9 = (bf16[2048,128]{1,0:T(8,128)(2,1)}, bf16[2048,128]{1,0:T(8,128)(2,1)S(1)}, u32[]{:S(2)}) copy-start(bf16[2048,128]{1,0:T(8,128)(2,1)S(1)} %collective-permute-done.10.refs_2_) | copy-start | bytes 1572868
  86.7 13.4 %collective-permute-start.12 = (bf16[2048,128]{1,0:T(8,128)(2,1)S(1)}, bf16[2048,128]{1,0:T(8,128)(2,1)S(1)}, u32[]{:S(2)}, u32[]{:S(2)}) collective-permute-start(bf16[2048,128]{1,0:T(8,128)(2,1)S(1)} %collective-permute-done.10.refs_2_), channel_id=1, source_target_pairs={{0,16},{16,0},{1,17},{17,1},{2,18},{18,2},{3,19},{19,3},{4,20},{20... | collective-permute-start | bytes 1572872 | tf_op jit(solution)/shard_map/ppermute | solution.py:229
  88.5 3.4 %copy-start.1 = (bf16[1024,4096]{1,0:T(8,128)(2,1)S(1)}, bf16[1024,4096]{1,0:T(8,128)(2,1)}, u32[]{:S(2)}) copy-start(bf16[1024,4096]{1,0:T(8,128)(2,1)} %tokens_ref.9) | copy-start | bytes 25165828
  96.2 1.3 copy-start.3
  100.9 25.3 %collective-permute-start.15 = (bf16[2048,128]{1,0:T(8,128)(2,1)}, bf16[2048,128]{1,0:T(8,128)(2,1)}, u32[]{:S(2)}, u32[]{:S(2)}) collective-permute-start(bf16[2048,128]{1,0:T(8,128)(2,1)} %broadcast_select_fusion.1.refs_0_), channel_id=1, source_target_pairs={{0,2},{2,0},{4,6},{6,4},{8,10},{10,8},{12,14},{14,12},{1,3},{3,1},... | collective-permute-start | bytes 1572872 | tf_op jit(solution)/shard_map/ppermute | solution.py:226
  100.9 25.3 %collective-permute-start.14 = (bf16[2048,128]{1,0:T(8,128)(2,1)}, bf16[2048,128]{1,0:T(8,128)(2,1)}, u32[]{:S(2)}, u32[]{:S(2)}) collective-permute-start(bf16[2048,128]{1,0:T(8,128)(2,1)} %broadcast_select_fusion.1.refs_0_), channel_id=1, source_target_pairs={{0,16},{16,0},{1,17},{17,1},{2,18},{18,2},{3,19},{19,3},{4,20},{20... | collective-permute-start | bytes 1572872 | tf_op jit(solution)/shard_map/ppermute | solution.py:229
  101.5 54.6 %all-to-all-start.3 = ((bf16[8,32,4096]{2,1,0:T(8,128)(2,1)}), bf16[8,32,4096]{2,1,0:T(8,128)(2,1)}, u32[]{:S(2)}, u32[]{:S(2)}) async-start(bf16[8,32,4096]{2,1,0:T(8,128)(2,1)} %bitcast.39), calls=%async_computation.3 | async-start | bytes 4194304 | tf_op jit(solution)/shard_map/all_to_all | solution.py:157
  109.3 1.2 copy-start.15
  110.6 1.0 copy-start.17
  111.6 1.0 copy-start.19
  112.6 1.0 copy-start.21
  113.7 1.0 copy-start.24
  114.7 1.0 copy-start.26
  124.8 1.4 copy-start.4
  126.2 12.0 %collective-permute-start.17 = (bf16[2048,128]{1,0:T(8,128)(2,1)}, bf16[2048,128]{1,0:T(8,128)(2,1)}, u32[]{:S(2)}, u32[]{:S(2)}) collective-permute-start(bf16[2048,128]{1,0:T(8,128)(2,1)} %collective-permute-done.15.refs_2_), channel_id=1, source_target_pairs={{0,16},{16,0},{1,17},{17,1},{2,18},{18,2},{3,19},{19,3},{4,20},{20... | collective-permute-start | bytes 1572872 | tf_op jit(solution)/shard_map/ppermute | solution.py:229
  126.8 3.4 %copy-start.2 = (bf16[1024,4096]{1,0:T(8,128)(2,1)S(1)}, bf16[1024,4096]{1,0:T(8,128)(2,1)}, u32[]{:S(2)}) copy-start(bf16[1024,4096]{1,0:T(8,128)(2,1)} %tokens_ref.9) | copy-start | bytes 25165828
  130.2 1.0 copy-start.7
  131.3 1.0 copy-start.10
  132.3 1.0 copy-start.12
  134.4 3.9 %copy-start.8 = (bf16[2048,128]{1,0:T(8,128)(2,1)S(1)}, bf16[2048,128]{1,0:T(8,128)(2,1)}, u32[]{:S(2)}) copy-start(bf16[2048,128]{1,0:T(8,128)(2,1)} %broadcast_select_fusion.1.refs_0_) | copy-start | bytes 1572868
  138.2 5.0 %copy-start.5 = (f32[1024,512]{1,0:T(8,128)S(1)}, f32[1024,512]{1,0:T(8,128)}, u32[]{:S(2)}) copy-start(f32[1024,512]{1,0:T(8,128)} %copy-done.4) | copy-start | bytes 6291460
  143.7 7.4 %collective-permute-start.18 = (f32[1024,512]{1,0:T(8,128)S(1)}, f32[1024,512]{1,0:T(8,128)S(1)}, u32[]{:S(2)}, u32[]{:S(2)}) collective-permute-start(f32[1024,512]{1,0:T(8,128)S(1)} %fusion), channel_id=1, source_target_pairs={{0,1},{1,0},{2,3},{3,2},{4,5},{5,4},{6,7},{7,6},{8,9},{9,8},{10,11... | collective-permute-start | bytes 6291464 | tf_op jit(solution)/shard_map/ppermute | solution.py:334
  146.8 3.1 %copy-start.27 = (bf16[1024,512]{1,0:T(8,128)(2,1)S(1)}, bf16[1024,512]{1,0:T(8,128)(2,1)}, u32[]{:S(2)}) copy-start(bf16[1024,512]{1,0:T(8,128)(2,1)} %param.11) | copy-start | bytes 3145732
  146.8 2.8 %collective-permute-start.16 = (f32[256,1024]{1,0:T(8,128)S(1)}, f32[256,1024]{1,0:T(8,128)S(1)}, u32[]{:S(2)}, u32[]{:S(2)}) collective-permute-start(f32[256,1024]{1,0:T(8,128)S(1)} %hidden_product.1), channel_id=1, source_target_pairs={{0,1},{1,0},{2,3},{3,2},{4,5},{5,4},{6,7},{7,6},{8,9},{9,8},{10,11... | collective-permute-start | bytes 3145736 | tf_op jit(solution)/shard_map/ppermute | solution.py:176
  156.1 12.9 %all-to-all-start.4 = ((bf16[8,32,512]{2,1,0:T(8,128)(2,1)}), bf16[8,32,512]{2,1,0:T(8,128)(2,1)S(1)}, u32[]{:S(2)}, u32[]{:S(2)}) async-start(bf16[8,32,512]{2,1,0:T(8,128)(2,1)} %bitcast.21), calls=%async_computation.4 | async-start | bytes 524288 | tf_op jit(solution)/shard_map/all_to_all | solution.py:157
  (7 other events, 6.0 us)

commit v4 on v3

--- a/solution.py
+++ b/solution.py
@@ -256,7 +256,6 @@
     near_across_rest = twin(near_across)
     backward_pass = work.rank_space(dot(got_b, cotangent, ((1,), (1,))))
     home_a = gradient_term(backward_pass, tokens)
-    following_across_rest = twin(following_across)
     end_far, home_a = barrier((end_far, home_a))
     far = jnp.where(inner, mid_far, end_far)
     (
@@ -265,7 +264,6 @@
         far,
         following_across,
         following_rest,
-        following_across_rest,
         near_across_rest,
     ) = barrier(
         (
@@ -274,13 +272,13 @@
             far,
             following_across,
             following_rest,
-            following_across_rest,
             near_across_rest,
         )
     )
     came_a = work.exchange(home_a)
     far_across = over(far, across)
     far_rest = twin(far)
+    following_across_rest = twin(following_across)
     parity = layer % 2
     product_here = product(
         tokens,
@@ -305,8 +303,8 @@
         output_columns,
         cost(*tokens.shape, output_columns),
     )
-    got_a, product_here, far_rest, far_across = barrier(
-        (got_a, product_here, far_rest, far_across)
+    got_a, product_here, far_rest, far_across, following_across_rest = barrier(
+        (got_a, product_here, far_rest, far_across, following_across_rest)
     )
     far_across_rest = twin(far_across)
     halves = [

time: 171 us -> 169 us (0.988)
  starting transfers between devices: 48 us -> 45.8 us
    ppermute x9, waiting for transfers between devices: 25.1 us -> 21.7 us  [over(): return lax.ppermute(part, 'dp', pairs)]
    all_to_all x5, waiting for transfers between devices: 22.3 us -> 25.3 us  [exchange(): lax.all_to_all(sent.reshape(self.peers, -1, sent.shape[1]), 'dp', split_a...]
    all_to_all x5, starting transfers between devices: 24.8 us -> 21.8 us  [exchange(): lax.all_to_all(sent.reshape(self.peers, -1, sent.shape[1]), 'dp', split_a...]
    unnamed x62 -> x58, local copies, waits for them, and re-layouts: 24.9 us -> 24 us
  transfers between devices with their start and end apart: 24 -> 24, of which waited for: 7 -> 9; matrix products, arithmetic and copies ran while one was open for 11% -> 11% of each run, Pallas kernels for 15% -> 16%
where the time goes in v4:
time: 169 us; the launch traced here: 167 us
  waiting for transfers between devices  50.4 us (30%)
  starting transfers between devices  45.8 us (27%)
  local copies, waits for them, and re-layouts  27.9 us (17%)
  Pallas kernels  26.1 us (15%)
  matrix products  11.9 us (7%)
  other arithmetic  4.28 us (3%)
    all_to_all x5, waiting for transfers between devices, exchange(): lax.all_to_all(sent.reshape(self.peers, -1, sent.shape[1]), 'dp', split_a...  25.3 us
    unnamed x58, local copies, waits for them, and re-layouts  24 us
    all_to_all x5, starting transfers between devices, exchange(): lax.all_to_all(sent.reshape(self.peers, -1, sent.shape[1]), 'dp', split_a...  21.8 us
    ppermute x9, waiting for transfers between devices, over(): return lax.ppermute(part, 'dp', pairs)  21.7 us
    pallas_call x3, Pallas kernels, product(): pl.pallas_call(functools.partial(product_kernel, len(pieces)), out_shape=...  18.8 us
    ppermute x9, starting transfers between devices, over(): return lax.ppermute(part, 'dp', pairs)  16.8 us
    dot_general x7, matrix products, dot(): lax.dot_general(left, right, ((contract[0], contract[1]), ((), ())), pref...  11.9 us
    ppermute x7, starting transfers between devices, twin(): return lax.ppermute(part, 'groups', SWAP)  6.44 us
  transfers between devices with their start and end apart: 24, of which 9 were waited for; matrix products, arithmetic and copies ran while one was open for 11% of the time, Pallas kernels for 16%

profile of v4, /device:TPU:0, one launch (start us, length us, event | category | flops | bytes accessed | tf_op | source)
XLA Modules:
  0.0 167.5 jit_solution(13928880753708884410)
XLA Ops:
  0.7 1.2 constant_dynamic-slice_fusion.1
  1.8 3.0 %collective-permute-start.2 = (bf16[2048,128]{1,0:T(8,128)(2,1)S(1)}, bf16[2048,128]{1,0:T(8,128)(2,1)S(1)}, u32[]{:S(2)}, u32[]{:S(2)}) collective-permute-start(bf16[2048,128]{1,0:T(8,128)(2,1)S(1)} %constant_dynamic-slice_fusion.1), channel_id=1, source_target_pairs={{0,2},{2,0},{4,6},{6,4},{8,10},{10,8},{12,14},{14,12},{1,3},{3,1},... | collective-permute-start | bytes 1572872 | tf_op jit(solution)/shard_map/ppermute | solution.py:226
  5.5 4.4 %collective-permute-start = (bf16[2048,128]{1,0:T(8,128)(2,1)S(1)}, bf16[2048,128]{1,0:T(8,128)(2,1)S(1)}, u32[]{:S(2)}, u32[]{:S(2)}) collective-permute-start(bf16[2048,128]{1,0:T(8,128)(2,1)S(1)} %constant_dynamic-slice_fusion.1), channel_id=1, source_target_pairs={{0,4},{2,6},{4,0},{6,2},{8,12},{10,14},{12,8},{14,10},{1,5},{3,7},... | collective-permute-start | bytes 1572872 | tf_op jit(solution)/shard_map/ppermute | solution.py:226
  12.4 3.3 %all-to-all-start = ((s32[8,1,1]{2,1,0:T(1,128)}), s32[8,1,1]{2,1,0:T(1,128)S(1)}, u32[]{:S(2)}, u32[]{:S(2)}) async-start(s32[8,1,1]{2,1,0:T(1,128)} %copy.12), calls=%async_computation | async-start | bytes 8192 | tf_op jit(solution)/shard_map/all_to_all | solution.py:157
  16.7 5.7 %all-to-all-done = s32[8,1,1]{2,1,0:T(1,128)S(1)} async-done(((s32[8,1,1]{2,1,0:T(1,128)}), s32[8,1,1]{2,1,0:T(1,128)S(1)}, u32[]{:S(2)}, u32[]{:S(2)}) %all-to-all-start) | async-done | bytes 64 | tf_op jit(solution)/shard_map/all_to_all | solution.py:157
  23.5 1.5 collective-permute-start.6
  25.0 1.5 collective-permute-start.5
  26.5 1.5 collective-permute-start.3
  28.1 1.3 collective-permute-start.4
  31.0 5.7 %all-to-all-start.1 = ((bf16[8,32,512]{2,1,0:T(8,128)(2,1)}), bf16[8,32,512]{2,1,0:T(8,128)(2,1)S(1)}, u32[]{:S(2)}, u32[]{:S(2)}) async-start(bf16[8,32,512]{2,1,0:T(8,128)(2,1)} %bitcast.45), calls=%async_computation.1 | async-start | bytes 524288 | tf_op jit(solution)/shard_map/all_to_all | solution.py:157
  36.7 2.1 %convolution_convert_fusion = bf16[256,4096]{1,0:T(8,128)(2,1)} fusion(bf16[128,4096]{1,0:T(8,128)(2,1)S(1)} %bitcast.37, s32[128]{0:T(128)S(1)} %get-tuple-element.64, s32[128]{0:T(128)S(1)} %get-tuple-element.65, s32[256]{0:T(256)S(1)} %get-tuple-element.61, s32[256]{0:T(256)S(1)} %get-tuple-element.62, s32[128]{0:T(128)S(1)} %get-tuple-element.63, ...), kind=kOutput, calls=%fused_computation | convolution fusion | flops 269680640 | bytes 3151360 | tf_op jit(solution)/shard_map/dot_general | solution.py:18
  38.8 6.9 %all-to-all-done.1 = bf16[8,32,512]{2,1,0:T(8,128)(2,1)S(1)} async-done(((bf16[8,32,512]{2,1,0:T(8,128)(2,1)}), bf16[8,32,512]{2,1,0:T(8,128)(2,1)S(1)}, u32[]{:S(2)}, u32[]{:S(2)}) %all-to-all-start.1) | async-done | bytes 262176 | tf_op jit(solution)/shard_map/all_to_all | solution.py:157
  48.4 4.6 %all-to-all-start.2 = ((bf16[8,32,4096]{2,1,0:T(8,128)(2,1)}), bf16[8,32,4096]{2,1,0:T(8,128)(2,1)S(1)}, u32[]{:S(2)}, u32[]{:S(2)}) async-start(bf16[8,32,4096]{2,1,0:T(8,128)(2,1)} %bitcast.40), calls=%async_computation.2 | async-start | bytes 4194304 | tf_op jit(solution)/shard_map/all_to_all | solution.py:157
  53.1 1.8 %fusion.11 = f32[256,1024]{1,0:T(8,128)S(1)} fusion(bf16[256,512]{1,0:T(8,128)(2,1)S(1)} %bitcast.41, bf16[1024,512]{1,0:T(8,128)(2,1)} %param.11), kind=kOutput, calls=%fused_computation.49 | convolution fusion | flops 268435456 | bytes 2359296 | tf_op jit(solution)/shard_map/dot_general | solution.py:18
  55.0 1.3 collective-permute-start.8
  56.3 1.1 broadcast_select_fusion.refs_0_
  57.4 1.6 collective-permute-start.11
  59.0 2.0 %collective-permute-start.10 = (bf16[2048,128]{1,0:T(8,128)(2,1)S(1)}, bf16[2048,128]{1,0:T(8,128)(2,1)S(1)}, u32[]{:S(2)}, u32[]{:S(2)}) collective-permute-start(bf16[2048,128]{1,0:T(8,128)(2,1)S(1)} %broadcast_select_fusion.refs_0_), channel_id=1, source_target_pairs={{0,2},{2,0},{4,6},{6,4},{8,10},{10,8},{12,14},{14,12},{1,3},{3,1},... | collective-permute-start | bytes 1572872 | tf_op jit(solution)/shard_map/ppermute | solution.py:226
  61.9 3.4 %copy-done.1 = bf16[1024,4096]{1,0:T(8,128)(2,1)S(1)} copy-done((bf16[1024,4096]{1,0:T(8,128)(2,1)S(1)}, bf16[1024,4096]{1,0:T(8,128)(2,1)}, u32[]{:S(2)}) %copy-start.1) | copy-done | bytes 8388632
  65.2 4.3 %gradient_term.1 = bf16[256,4096]{1,0:T(8,128)(2,1)S(1)} custom-call(bf16[256,1024]{1,0:T(8,128)(2,1)S(1)} %select_convert_fusion.1.space_ref, bf16[1024,4096]{1,0:T(8,128)(2,1)S(1)} %copy-done.1), custom_call_target="tpu_custom_call" | custom-call | flops 1000000 | bytes 10000 | tf_op jit(solution)/shard_map/gradient_term/pallas_call | solution.py:113
  69.6 1.3 copy-done.3
  70.9 18.2 %collective-permute-done.8 = bf16[2048,128]{1,0:T(8,128)(2,1)S(1)} collective-permute-done((bf16[2048,128]{1,0:T(8,128)(2,1)}, bf16[2048,128]{1,0:T(8,128)(2,1)S(1)}, u32[]{:S(2)}, u32[]{:S(2)}) %collective-permute-start.8) | collective-permute-done | bytes 524320 | tf_op jit(solution)/shard_map/ppermute | solution.py:226
  92.4 6.3 %all-to-all-done.2 = bf16[8,32,4096]{2,1,0:T(8,128)(2,1)S(1)} async-done(((bf16[8,32,4096]{2,1,0:T(8,128)(2,1)}), bf16[8,32,4096]{2,1,0:T(8,128)(2,1)S(1)}, u32[]{:S(2)}, u32[]{:S(2)}) %all-to-all-start.2) | async-done | bytes 2097184 | tf_op jit(solution)/shard_map/all_to_all | solution.py:157
  98.7 1.5 collective-permute-start.15
  100.2 1.2 collective-permute-start.14
  102.1 4.4 %all-to-all-start.3 = ((bf16[8,32,4096]{2,1,0:T(8,128)(2,1)}), bf16[8,32,4096]{2,1,0:T(8,128)(2,1)}, u32[]{:S(2)}, u32[]{:S(2)}) async-start(bf16[8,32,4096]{2,1,0:T(8,128)(2,1)} %bitcast.39), calls=%async_computation.3 | async-start | bytes 4194304 | tf_op jit(solution)/shard_map/all_to_all | solution.py:157
  106.5 1.2 copy-done.13
  107.7 1.0 copy-done.15
  108.8 1.0 copy-done.17
  109.8 1.0 copy-done.19
  110.8 1.0 copy-done.22
  111.9 1.0 copy-done.24
  112.9 9.1 %weight_product.3 = f32[1024,512]{1,0:T(8,128)S(1)} custom-call(s32[14]{0:T(128)S(1)} %stack.26.place_ref, bf16[1024,4096]{1,0:T(8,128)(2,1)} %tokens_ref.9, bf16[4096,128]{1,0:T(8,128)(2,1)S(1)} %copy-done.13, bf16[2048,128]{1,0:T(8,128)(2,1)S(1)} %copy-done.15, bf16[2048,128]{1,0:T(8,128)(2,1)} %collective-permute-done.7.refs_2_, ...), custom_call_target="tpu_custom_call" | custom-call | flops 4294967296 | bytes 8388608 | tf_op jit(solution)/shard_map/weight_product/pallas_call | solution.py:63
  122.0 1.4 copy-done.4
  123.4 3.5 %collective-permute-done.14.refs_2_ = bf16[2048,128]{1,0:T(8,128)(2,1)} collective-permute-done((bf16[2048,128]{1,0:T(8,128)(2,1)}, bf16[2048,128]{1,0:T(8,128)(2,1)}, u32[]{:S(2)}, u32[]{:S(2)}) %collective-permute-start.14) | collective-permute-done | bytes 524320 | tf_op jit(solution)/shard_map/ppermute | solution.py:226
  127.2 3.4 %copy-done.2 = bf16[1024,4096]{1,0:T(8,128)(2,1)S(1)} copy-done((bf16[1024,4096]{1,0:T(8,128)(2,1)S(1)}, bf16[1024,4096]{1,0:T(8,128)(2,1)}, u32[]{:S(2)}) %copy-start.2) | copy-done | bytes 8388632
  131.6 1.0 copy-done.10
  132.7 1.0 copy-done.12
  133.7 4.8 %weight_product.4 = f32[1024,256]{1,0:T(8,128)S(1)} custom-call(s32[8]{0:T(128)S(1)} %stack.29.place_ref, bf16[1024,4096]{1,0:T(8,128)(2,1)S(1)} %copy-done.2, bf16[2048,128]{1,0:T(8,128)(2,1)S(1)} %copy-done.7, bf16[2048,128]{1,0:T(8,128)(2,1)S(1)} %copy-done.10, bf16[2048,128]{1,0:T(8,128)(2,1)S(1)} %copy-done.12, ...), custom_call_target="tpu_custom_call" | custom-call | flops 1000000 | bytes 10000 | tf_op jit(solution)/shard_map/weight_product/pallas_call | solution.py:63
  138.5 4.9 %weight_product.5 = f32[1024,256]{1,0:T(8,128)S(1)} custom-call(s32[8]{0:T(128)S(1)} %stack.29.place_ref, bf16[1024,4096]{1,0:T(8,128)(2,1)S(1)} %copy-done.2, bf16[2048,128]{1,0:T(8,128)(2,1)S(1)} %copy-done.8, bf16[2048,128]{1,0:T(8,128)(2,1)} %collective-permute-done.13.refs_1_, bf16[2048,128]{1,0:T(8,128)(2,1)} %collective-permute-done.14.refs_2_, ...), custom_call_target="tpu_custom_call" | custom-call | flops 1000000 | bytes 10000 | tf_op jit(solution)/shard_map/weight_product/pallas_call | solution.py:63
  144.1 3.0 %hidden_product.1 = f32[256,1024]{1,0:T(8,128)S(1)} custom-call(bf16[256,4096]{1,0:T(8,128)(2,1)S(1)} %bitcast.38, bf16[1024,4096]{1,0:T(8,128)(2,1)S(1)} %copy-done.2), custom_call_target="tpu_custom_call" | custom-call | flops 1000000 | bytes 10000 | tf_op jit(solution)/shard_map/hidden_product/pallas_call | solution.py:90
  147.7 2.3 %collective-permute-done.16 = f32[256,1024]{1,0:T(8,128)S(1)} collective-permute-done((f32[256,1024]{1,0:T(8,128)S(1)}, f32[256,1024]{1,0:T(8,128)S(1)}, u32[]{:S(2)}, u32[]{:S(2)}) %collective-permute-start.16) | collective-permute-done | bytes 1048608 | tf_op jit(solution)/shard_map/ppermute | solution.py:176
  150.3 1.1 fusion.1
  151.4 1.5 add_convert_fusion
  153.2 3.8 %all-to-all-start.4 = ((bf16[8,32,512]{2,1,0:T(8,128)(2,1)}), bf16[8,32,512]{2,1,0:T(8,128)(2,1)S(1)}, u32[]{:S(2)}, u32[]{:S(2)}) async-start(bf16[8,32,512]{2,1,0:T(8,128)(2,1)} %bitcast.21), calls=%async_computation.4 | async-start | bytes 524288 | tf_op jit(solution)/shard_map/all_to_all | solution.py:157
  157.0 3.2 %convolution_convert_fusion.1 = bf16[128,4096]{1,0:T(8,128)(2,1)} fusion(bf16[256,4096]{1,0:T(8,128)(2,1)} %bitcast.11, s32[128]{0:T(128)S(1)} %get-tuple-element.64, s32[128]{0:T(128)S(1)} %get-tuple-element.65, s32[256]{0:T(256)S(1)} %get-tuple-element.61, s32[256]{0:T(256)S(1)} %get-tuple-element.62, s32[128]{0:T(128)S(1)} %get-tuple-element.63, ...), kind=kOutput, calls=%fused_computation.1 | convolution fusion | flops 269156352 | bytes 3151360 | tf_op jit(solution)/shard_map/dot_general | solution.py:18
  160.2 6.2 %all-to-all-done.4 = bf16[8,32,512]{2,1,0:T(8,128)(2,1)S(1)} async-done(((bf16[8,32,512]{2,1,0:T(8,128)(2,1)}), bf16[8,32,512]{2,1,0:T(8,128)(2,1)S(1)}, u32[]{:S(2)}, u32[]{:S(2)}) %all-to-all-start.4) | async-done | bytes 262176 | tf_op jit(solution)/shard_map/all_to_all | solution.py:157
  166.4 1.1 convolution_convert_fusion.3
  (98 shorter events, 17.6 us)
Async XLA Ops:
  0.6 36.1 %copy-start = (bf16[4,32,4096]{2,1,0:T(8,128)(2,1)S(1)}, bf16[4,32,4096]{2,1,0:T(8,128)(2,1)}, u32[]{:S(2)}) copy-start(bf16[4,32,4096]{2,1,0:T(8,128)(2,1)} %param.9) | copy-start | bytes 3145732
  1.8 20.8 %collective-permute-start.2 = (bf16[2048,128]{1,0:T(8,128)(2,1)S(1)}, bf16[2048,128]{1,0:T(8,128)(2,1)S(1)}, u32[]{:S(2)}, u32[]{:S(2)}) collective-permute-start(bf16[2048,128]{1,0:T(8,128)(2,1)S(1)} %constant_dynamic-slice_fusion.1), channel_id=1, source_target_pairs={{0,2},{2,0},{4,6},{6,4},{8,10},{10,8},{12,14},{14,12},{1,3},{3,1},... | collective-permute-start | bytes 1572872 | tf_op jit(solution)/shard_map/ppermute | solution.py:226
  4.9 17.8 %collective-permute-start.1 = (bf16[2048,128]{1,0:T(8,128)(2,1)S(1)}, bf16[2048,128]{1,0:T(8,128)(2,1)S(1)}, u32[]{:S(2)}, u32[]{:S(2)}) collective-permute-start(bf16[2048,128]{1,0:T(8,128)(2,1)S(1)} %constant_dynamic-slice_fusion.1), channel_id=1, source_target_pairs={{4,8},{6,10},{8,4},{10,6},{5,9},{7,11},{9,5},{11,7},{20,24},{22,26... | collective-permute-start | bytes 1572872 | tf_op jit(solution)/shard_map/ppermute | solution.py:226
  5.5 17.2 %collective-permute-start = (bf16[2048,128]{1,0:T(8,128)(2,1)S(1)}, bf16[2048,128]{1,0:T(8,128)(2,1)S(1)}, u32[]{:S(2)}, u32[]{:S(2)}) collective-permute-start(bf16[2048,128]{1,0:T(8,128)(2,1)S(1)} %constant_dynamic-slice_fusion.1), channel_id=1, source_target_pairs={{0,4},{2,6},{4,0},{6,2},{8,12},{10,14},{12,8},{14,10},{1,5},{3,7},... | collective-permute-start | bytes 1572872 | tf_op jit(solution)/shard_map/ppermute | solution.py:226
  12.4 10.0 %all-to-all-start = ((s32[8,1,1]{2,1,0:T(1,128)}), s32[8,1,1]{2,1,0:T(1,128)S(1)}, u32[]{:S(2)}, u32[]{:S(2)}) async-start(s32[8,1,1]{2,1,0:T(1,128)} %copy.12), calls=%async_computation | async-start | bytes 8192 | tf_op jit(solution)/shard_map/all_to_all | solution.py:157
  22.7 24.9 %copy-start.14 = (bf16[2048,128]{1,0:T(8,128)(2,1)}, bf16[2048,128]{1,0:T(8,128)(2,1)S(1)}, u32[]{:S(2)}) copy-start(bf16[2048,128]{1,0:T(8,128)(2,1)S(1)} %collective-permute-done.2.refs_1_) | copy-start | bytes 1572868
  22.7 24.9 %copy-start.16 = (bf16[2048,128]{1,0:T(8,128)(2,1)}, bf16[2048,128]{1,0:T(8,128)(2,1)S(1)}, u32[]{:S(2)}) copy-start(bf16[2048,128]{1,0:T(8,128)(2,1)S(1)} %collective-permute-done.refs_3_) | copy-start | bytes 1572868
  23.5 23.2 %collective-permute-start.6 = (bf16[2048,128]{1,0:T(8,128)(2,1)S(1)}, bf16[2048,128]{1,0:T(8,128)(2,1)S(1)}, u32[]{:S(2)}, u32[]{:S(2)}) collective-permute-start(bf16[2048,128]{1,0:T(8,128)(2,1)S(1)} %collective-permute-done.refs_3_), channel_id=1, source_target_pairs={{0,16},{16,0},{1,17},{17,1},{2,18},{18,2},{3,19},{19,3},{4,20},{20... | collective-permute-start | bytes 1572872 | tf_op jit(solution)/shard_map/ppermute | solution.py:229
  25.0 22.6 %collective-permute-start.5 = (bf16[2048,128]{1,0:T(8,128)(2,1)S(1)}, bf16[2048,128]{1,0:T(8,128)(2,1)S(1)}, u32[]{:S(2)}, u32[]{:S(2)}) collective-permute-start(bf16[2048,128]{1,0:T(8,128)(2,1)S(1)} %collective-permute-done.refs_3_), channel_id=1, source_target_pairs={{0,2},{2,0},{4,6},{6,4},{8,10},{10,8},{12,14},{14,12},{1,3},{3,1},... | collective-permute-start | bytes 1572872 | tf_op jit(solution)/shard_map/ppermute | solution.py:226
  26.5 21.1 %collective-permute-start.3 = (bf16[2048,128]{1,0:T(8,128)(2,1)S(1)}, bf16[2048,128]{1,0:T(8,128)(2,1)}, u32[]{:S(2)}, u32[]{:S(2)}) collective-permute-start(bf16[2048,128]{1,0:T(8,128)(2,1)S(1)} %collective-permute-done.refs_3_), channel_id=1, source_target_pairs={{4,8},{6,10},{8,4},{10,6},{5,9},{7,11},{9,5},{11,7},{20,24},{22,26... | collective-permute-start | bytes 1572872 | tf_op jit(solution)/shard_map/ppermute | solution.py:226
  28.1 17.6 %collective-permute-start.4 = (bf16[2048,128]{1,0:T(8,128)(2,1)}, bf16[2048,128]{1,0:T(8,128)(2,1)}, u32[]{:S(2)}, u32[]{:S(2)}) collective-permute-start(bf16[2048,128]{1,0:T(8,128)(2,1)} %copy-done.26), channel_id=1, source_target_pairs={{4,0},{6,2},{8,12},{10,14},{5,1},{7,3},{9,13},{11,15},{20,16},{22,... | collective-permute-start | bytes 1572872 | tf_op jit(solution)/shard_map/ppermute | solution.py:226
  29.4 17.4 %collective-permute-start.7 = (bf16[2048,128]{1,0:T(8,128)(2,1)S(1)}, bf16[2048,128]{1,0:T(8,128)(2,1)}, u32[]{:S(2)}, u32[]{:S(2)}) collective-permute-start(bf16[2048,128]{1,0:T(8,128)(2,1)S(1)} %collective-permute-done.2.refs_1_), channel_id=1, source_target_pairs={{0,16},{16,0},{1,17},{17,1},{2,18},{18,2},{3,19},{19,3},{4,20},{20... | collective-permute-start | bytes 1572872 | tf_op jit(solution)/shard_map/ppermute | solution.py:229
  31.0 14.7 %all-to-all-start.1 = ((bf16[8,32,512]{2,1,0:T(8,128)(2,1)}), bf16[8,32,512]{2,1,0:T(8,128)(2,1)S(1)}, u32[]{:S(2)}, u32[]{:S(2)}) async-start(bf16[8,32,512]{2,1,0:T(8,128)(2,1)} %bitcast.45), calls=%async_computation.1 | async-start | bytes 524288 | tf_op jit(solution)/shard_map/all_to_all | solution.py:157
  48.4 50.3 %all-to-all-start.2 = ((bf16[8,32,4096]{2,1,0:T(8,128)(2,1)}), bf16[8,32,4096]{2,1,0:T(8,128)(2,1)S(1)}, u32[]{:S(2)}, u32[]{:S(2)}) async-start(bf16[8,32,4096]{2,1,0:T(8,128)(2,1)} %bitcast.40), calls=%async_computation.2 | async-start | bytes 4194304 | tf_op jit(solution)/shard_map/all_to_all | solution.py:157
  53.0 2.0 %copy-start.28 = (s32[1024]{0:T(1024)S(1)}, s32[1024]{0:T(1024)}, u32[]{:S(2)}) copy-start(s32[1024]{0:T(1024)} %param.12) | copy-start | bytes 12292
  53.0 3.3 %copy-start.27 = (bf16[2048,128]{1,0:T(8,128)(2,1)S(1)}, bf16[2048,128]{1,0:T(8,128)(2,1)}, u32[]{:S(2)}) copy-start(bf16[2048,128]{1,0:T(8,128)(2,1)} %copy-done.26) | copy-start | bytes 1572868
  53.0 8.0 %copy-start.21 = (bf16[2048,128]{1,0:T(8,128)(2,1)S(1)}, bf16[2048,128]{1,0:T(8,128)(2,1)}, u32[]{:S(2)}) copy-start(bf16[2048,128]{1,0:T(8,128)(2,1)} %copy-done.20) | copy-start | bytes 1572868
  54.9 6.7 %collective-permute-start.9 = (f32[256,1024]{1,0:T(8,128)S(1)}, f32[256,1024]{1,0:T(8,128)S(1)}, u32[]{:S(2)}, u32[]{:S(2)}) collective-permute-start(f32[256,1024]{1,0:T(8,128)S(1)} %fusion.11), channel_id=1, source_target_pairs={{0,1},{1,0},{2,3},{3,2},{4,5},{5,4},{6,7},{7,6},{8,9},{9,8},{10,11... | collective-permute-start | bytes 3145736 | tf_op jit(solution)/shard_map/ppermute | solution.py:176
  55.0 34.1 %collective-permute-start.8 = (bf16[2048,128]{1,0:T(8,128)(2,1)}, bf16[2048,128]{1,0:T(8,128)(2,1)S(1)}, u32[]{:S(2)}, u32[]{:S(2)}) collective-permute-start(bf16[2048,128]{1,0:T(8,128)(2,1)} %collective-permute-done.3), channel_id=1, source_target_pairs={{4,0},{6,2},{8,12},{10,14},{5,1},{7,3},{9,13},{11,15},{20,16},{22,... | collective-permute-start | bytes 1572872 | tf_op jit(solution)/shard_map/ppermute | solution.py:226
  57.4 12.1 %copy-start.6 = (bf16[2048,128]{1,0:T(8,128)(2,1)}, bf16[2048,128]{1,0:T(8,128)(2,1)S(1)}, u32[]{:S(2)}) copy-start(bf16[2048,128]{1,0:T(8,128)(2,1)S(1)} %broadcast_select_fusion.refs_0_) | copy-start | bytes 1572868
  57.4 32.5 %collective-permute-start.11 = (bf16[2048,128]{1,0:T(8,128)(2,1)S(1)}, bf16[2048,128]{1,0:T(8,128)(2,1)S(1)}, u32[]{:S(2)}, u32[]{:S(2)}) collective-permute-start(bf16[2048,128]{1,0:T(8,128)(2,1)S(1)} %broadcast_select_fusion.refs_0_), channel_id=1, source_target_pairs={{0,16},{16,0},{1,17},{17,1},{2,18},{18,2},{3,19},{19,3},{4,20},{20... | collective-permute-start | bytes 1572872 | tf_op jit(solution)/shard_map/ppermute | solution.py:229
  59.0 31.8 %collective-permute-start.10 = (bf16[2048,128]{1,0:T(8,128)(2,1)S(1)}, bf16[2048,128]{1,0:T(8,128)(2,1)S(1)}, u32[]{:S(2)}, u32[]{:S(2)}) collective-permute-start(bf16[2048,128]{1,0:T(8,128)(2,1)S(1)} %broadcast_select_fusion.refs_0_), channel_id=1, source_target_pairs={{0,2},{2,0},{4,6},{6,4},{8,10},{10,8},{12,14},{14,12},{1,3},{3,1},... | collective-permute-start | bytes 1572872 | tf_op jit(solution)/shard_map/ppermute | solution.py:226
  61.0 30.6 %collective-permute-start.12 = (bf16[2048,128]{1,0:T(8,128)(2,1)S(1)}, bf16[2048,128]{1,0:T(8,128)(2,1)S(1)}, u32[]{:S(2)}, u32[]{:S(2)}) collective-permute-start(bf16[2048,128]{1,0:T(8,128)(2,1)S(1)} %copy-done.21), channel_id=1, source_target_pairs={{0,16},{16,0},{1,17},{17,1},{2,18},{18,2},{3,19},{19,3},{4,20},{20... | collective-permute-start | bytes 1572872 | tf_op jit(solution)/shard_map/ppermute | solution.py:229
  61.8 3.4 %copy-start.1 = (bf16[1024,4096]{1,0:T(8,128)(2,1)S(1)}, bf16[1024,4096]{1,0:T(8,128)(2,1)}, u32[]{:S(2)}) copy-start(bf16[1024,4096]{1,0:T(8,128)(2,1)} %tokens_ref.9) | copy-start | bytes 25165828
  69.6 1.3 copy-start.3
  90.8 0.8 copy-start.11
  98.7 24.6 %collective-permute-start.15 = (bf16[2048,128]{1,0:T(8,128)(2,1)}, bf16[2048,128]{1,0:T(8,128)(2,1)}, u32[]{:S(2)}, u32[]{:S(2)}) collective-permute-start(bf16[2048,128]{1,0:T(8,128)(2,1)} %copy-done.11), channel_id=1, source_target_pairs={{0,16},{16,0},{1,17},{17,1},{2,18},{18,2},{3,19},{19,3},{4,20},{20... | collective-permute-start | bytes 1572872 | tf_op jit(solution)/shard_map/ppermute | solution.py:229
  100.2 26.6 %collective-permute-start.14 = (bf16[2048,128]{1,0:T(8,128)(2,1)}, bf16[2048,128]{1,0:T(8,128)(2,1)}, u32[]{:S(2)}, u32[]{:S(2)}) collective-permute-start(bf16[2048,128]{1,0:T(8,128)(2,1)} %broadcast_select_fusion.1.refs_0_), channel_id=1, source_target_pairs={{0,2},{2,0},{4,6},{6,4},{8,10},{10,8},{12,14},{14,12},{1,3},{3,1},... | collective-permute-start | bytes 1572872 | tf_op jit(solution)/shard_map/ppermute | solution.py:226
  101.5 25.4 %collective-permute-start.13 = (bf16[2048,128]{1,0:T(8,128)(2,1)}, bf16[2048,128]{1,0:T(8,128)(2,1)}, u32[]{:S(2)}, u32[]{:S(2)}) collective-permute-start(bf16[2048,128]{1,0:T(8,128)(2,1)} %broadcast_select_fusion.1.refs_0_), channel_id=1, source_target_pairs={{0,16},{16,0},{1,17},{17,1},{2,18},{18,2},{3,19},{19,3},{4,20},{20... | collective-permute-start | bytes 1572872 | tf_op jit(solution)/shard_map/ppermute | solution.py:229
  102.1 51.1 %all-to-all-start.3 = ((bf16[8,32,4096]{2,1,0:T(8,128)(2,1)}), bf16[8,32,4096]{2,1,0:T(8,128)(2,1)}, u32[]{:S(2)}, u32[]{:S(2)}) async-start(bf16[8,32,4096]{2,1,0:T(8,128)(2,1)} %bitcast.39), calls=%async_computation.3 | async-start | bytes 4194304 | tf_op jit(solution)/shard_map/all_to_all | solution.py:157
  106.5 1.2 copy-start.13
  107.7 1.0 copy-start.15
  108.8 1.0 copy-start.17
  109.8 1.0 copy-start.19
  110.8 1.0 copy-start.22
  111.9 1.0 copy-start.24
  122.0 1.4 copy-start.4
  126.9 11.6 %collective-permute-start.17 = (bf16[2048,128]{1,0:T(8,128)(2,1)}, bf16[2048,128]{1,0:T(8,128)(2,1)}, u32[]{:S(2)}, u32[]{:S(2)}) collective-permute-start(bf16[2048,128]{1,0:T(8,128)(2,1)} %collective-permute-done.14.refs_2_), channel_id=1, source_target_pairs={{0,16},{16,0},{1,17},{17,1},{2,18},{18,2},{3,19},{19,3},{4,20},{20... | collective-permute-start | bytes 1572872 | tf_op jit(solution)/shard_map/ppermute | solution.py:229
  127.2 3.4 %copy-start.2 = (bf16[1024,4096]{1,0:T(8,128)(2,1)S(1)}, bf16[1024,4096]{1,0:T(8,128)(2,1)}, u32[]{:S(2)}) copy-start(bf16[1024,4096]{1,0:T(8,128)(2,1)} %tokens_ref.9) | copy-start | bytes 25165828
  130.6 1.0 copy-start.7
  131.6 1.0 copy-start.10
  132.7 1.0 copy-start.12
  133.7 4.8 %copy-start.8 = (bf16[2048,128]{1,0:T(8,128)(2,1)S(1)}, bf16[2048,128]{1,0:T(8,128)(2,1)}, u32[]{:S(2)}) copy-start(bf16[2048,128]{1,0:T(8,128)(2,1)} %broadcast_select_fusion.1.refs_0_) | copy-start | bytes 1572868
  138.5 5.0 %copy-start.5 = (f32[1024,512]{1,0:T(8,128)S(1)}, f32[1024,512]{1,0:T(8,128)}, u32[]{:S(2)}) copy-start(f32[1024,512]{1,0:T(8,128)} %copy-done.4) | copy-start | bytes 6291460
  144.0 7.4 %collective-permute-start.18 = (f32[1024,512]{1,0:T(8,128)S(1)}, f32[1024,512]{1,0:T(8,128)S(1)}, u32[]{:S(2)}, u32[]{:S(2)}) collective-permute-start(f32[1024,512]{1,0:T(8,128)S(1)} %fusion), channel_id=1, source_target_pairs={{0,1},{1,0},{2,3},{3,2},{4,5},{5,4},{6,7},{7,6},{8,9},{9,8},{10,11... | collective-permute-start | bytes 6291464 | tf_op jit(solution)/shard_map/ppermute | solution.py:332
  147.1 3.2 %copy-start.25 = (bf16[1024,512]{1,0:T(8,128)(2,1)S(1)}, bf16[1024,512]{1,0:T(8,128)(2,1)}, u32[]{:S(2)}) copy-start(bf16[1024,512]{1,0:T(8,128)(2,1)} %param.11) | copy-start | bytes 3145732
  147.1 2.8 %collective-permute-start.16 = (f32[256,1024]{1,0:T(8,128)S(1)}, f32[256,1024]{1,0:T(8,128)S(1)}, u32[]{:S(2)}, u32[]{:S(2)}) collective-permute-start(f32[256,1024]{1,0:T(8,128)S(1)} %hidden_product.1), channel_id=1, source_target_pairs={{0,1},{1,0},{2,3},{3,2},{4,5},{5,4},{6,7},{7,6},{8,9},{9,8},{10,11... | collective-permute-start | bytes 3145736 | tf_op jit(solution)/shard_map/ppermute | solution.py:176
  153.2 13.3 %all-to-all-start.4 = ((bf16[8,32,512]{2,1,0:T(8,128)(2,1)}), bf16[8,32,512]{2,1,0:T(8,128)(2,1)S(1)}, u32[]{:S(2)}, u32[]{:S(2)}) async-start(bf16[8,32,512]{2,1,0:T(8,128)(2,1)} %bitcast.21), calls=%async_computation.4 | async-start | bytes 524288 | tf_op jit(solution)/shard_map/all_to_all | solution.py:157
  (5 other events, 4.1 us)

commit v5 on v4

--- a/solution.py
+++ b/solution.py
@@ -57,7 +57,7 @@
     out_ref[...] = jnp.dot(tokens_ref[...], weight[...], preferred_element_type=jnp.float32)
 
 
-def product(tokens, pieces, places, width, estimate):
+def product(tokens, pieces, places, width, estimate, vmem=VMEM_BYTES):
     rows, depth = tokens.shape
     tile = rows // 4
     return pl.pallas_call(
@@ -74,7 +74,7 @@
                 pltpu.SemaphoreType.DMA((len(pieces),)),
             ],
         ),
-        compiler_params=pltpu.CompilerParams(vmem_limit_bytes=VMEM_BYTES),
+        compiler_params=pltpu.CompilerParams(vmem_limit_bytes=vmem),
         cost_estimate=estimate,
         name="weight_product",
     )(jnp.stack([jnp.int32(v) for place in places for v in place]), tokens, *pieces)
@@ -236,24 +236,25 @@
     mid_next = over(half, middle)
     own_across = over(half, across)
     asked = work.exchange(work.wanted.reshape(-1, 1))
-    near, mid_next, own_across, asked = barrier((near, mid_next, own_across, asked))
+    near, mid_next = barrier((near, mid_next))
     mid_far = over(near, middle)
     end_next = over(mid_next, outward)
     near_across = over(near, across)
     near_rest = twin(near)
-    own_across_rest = twin(own_across)
     work.choose(asked)
     got_b = work.exchange(work.chosen(work.own_b))
-    send_a = work.chosen(work.own_a)
-    mid_far, end_next, near_across, near_rest, own_across_rest, got_b, send_a = barrier(
-        (mid_far, end_next, near_across, near_rest, own_across_rest, got_b, send_a)
-    )
+    own_a, own_across, near_rest, near_across, mid_far, end_next = barrier(
+        (work.own_a, own_across, near_rest, near_across, mid_far, end_next)
+    )
+    send_a = work.chosen(own_a)
+    got_b, send_a = barrier((got_b, send_a))
     got_a = work.exchange(send_a)
     end_far = over(mid_far, outward)
     following = jnp.where(inner, mid_next, end_next)
     following_across = over(following, across)
     following_rest = twin(following)
     near_across_rest = twin(near_across)
+    own_across_rest = twin(own_across)
     backward_pass = work.rank_space(dot(got_b, cotangent, ((1,), (1,))))
     home_a = gradient_term(backward_pass, tokens)
     end_far, home_a = barrier((end_far, home_a))
@@ -265,6 +266,7 @@
         following_across,
         following_rest,
         near_across_rest,
+        own_across_rest,
     ) = barrier(
         (
             got_a,
@@ -273,6 +275,7 @@
             following_across,
             following_rest,
             near_across_rest,
+            own_across_rest,
         )
     )
     came_a = work.exchange(home_a)
@@ -302,9 +305,10 @@
         ],
         output_columns,
         cost(*tokens.shape, output_columns),
-    )
-    got_a, product_here, far_rest, far_across, following_across_rest = barrier(
-        (got_a, product_here, far_rest, far_across, following_across_rest)
+        56 * 1024 * 1024,
+    )
+    got_a, product_here, far_rest, following_across_rest, far_across = barrier(
+        (got_a, product_here, far_rest, following_across_rest, far_across)
     )
     far_across_rest = twin(far_across)
     halves = [

time: 169 us -> 161 us (0.953)
  local copies, waits for them, and re-layouts: 27.9 us -> 18.2 us
  waiting for transfers between devices: 50.4 us -> 52.7 us
  Pallas kernels: 26.1 us -> 28.2 us
    ppermute x9, waiting for transfers between devices: 21.7 us -> 36.6 us  [over(): return lax.ppermute(part, 'dp', pairs)]
    all_to_all x5, waiting for transfers between devices: 25.3 us -> 11.2 us  [exchange(): lax.all_to_all(sent.reshape(self.peers, -1, sent.shape[1]), 'dp', split_a...]
    unnamed x58 -> x42, local copies, waits for them, and re-layouts: 24 us -> 13.7 us
    pallas_call x3, Pallas kernels: 18.8 us -> 20.8 us  [product(): pl.pallas_call(functools.partial(product_kernel, len(pieces)), out_shape=...]
  transfers between devices with their start and end apart: 24 -> 24, of which waited for: 9 -> 9; matrix products, arithmetic and copies ran while one was open for 11% -> 11% of each run, Pallas kernels for 16% -> 18%
where the time goes in v5:
time: 161 us; the launch traced here: 160 us
  waiting for transfers between devices  52.7 us (33%)
  starting transfers between devices  44.8 us (28%)
  Pallas kernels  28.2 us (18%)
  local copies, waits for them, and re-layouts  18.2 us (11%)
  matrix products  11.9 us (7%)
  other arithmetic  3.26 us (2%)
    ppermute x9, waiting for transfers between devices, over(): return lax.ppermute(part, 'dp', pairs)  36.6 us
    pallas_call x3, Pallas kernels, product(): pl.pallas_call(functools.partial(product_kernel, len(pieces)), out_shape=...  20.8 us
    all_to_all x5, starting transfers between devices, exchange(): lax.all_to_all(sent.reshape(self.peers, -1, sent.shape[1]), 'dp', split_a...  20.5 us
    ppermute x9, starting transfers between devices, over(): return lax.ppermute(part, 'dp', pairs)  16.2 us
    unnamed x42, local copies, waits for them, and re-layouts  13.7 us
    dot_general x7, matrix products, dot(): lax.dot_general(left, right, ((contract[0], contract[1]), ((), ())), pref...  11.9 us
    all_to_all x5, waiting for transfers between devices, exchange(): lax.all_to_all(sent.reshape(self.peers, -1, sent.shape[1]), 'dp', split_a...  11.2 us
    ppermute x7, starting transfers between devices, twin(): return lax.ppermute(part, 'groups', SWAP)  7.45 us
  transfers between devices with their start and end apart: 24, of which 9 were waited for; matrix products, arithmetic and copies ran while one was open for 11% of the time, Pallas kernels for 18%

profile of v5, /device:TPU:0, one launch (start us, length us, event | category | flops | bytes accessed | tf_op | source)
XLA Modules:
  0.0 160.2 jit_solution(2841623738344220606)
XLA Ops:
  0.7 1.2 constant_dynamic-slice_fusion
  2.5 5.9 %collective-permute-start.1 = (bf16[2048,128]{1,0:T(8,128)(2,1)S(1)}, bf16[2048,128]{1,0:T(8,128)(2,1)}, u32[]{:S(2)}, u32[]{:S(2)}) collective-permute-start(bf16[2048,128]{1,0:T(8,128)(2,1)S(1)} %constant_dynamic-slice_fusion), channel_id=1, source_target_pairs={{0,4},{2,6},{4,0},{6,2},{8,12},{10,14},{12,8},{14,10},{1,5},{3,7},... | collective-permute-start | bytes 1572872 | tf_op jit(solution)/shard_map/ppermute | solution.py:226
  8.4 1.5 collective-permute-start
  10.7 0.8 select_reduce_fusion.1
  12.3 3.3 %all-to-all-start = ((s32[8,1,1]{2,1,0:T(1,128)}), s32[8,1,1]{2,1,0:T(1,128)S(1)}, u32[]{:S(2)}, u32[]{:S(2)}) async-start(s32[8,1,1]{2,1,0:T(1,128)} %copy.12), calls=%async_computation | async-start | bytes 8192 | tf_op jit(solution)/shard_map/all_to_all | solution.py:157
  15.7 0.9 constant_dynamic-slice_fusion.1
  16.7 3.5 %collective-permute-done.1.refs_3_ = bf16[2048,128]{1,0:T(8,128)(2,1)} collective-permute-done((bf16[2048,128]{1,0:T(8,128)(2,1)S(1)}, bf16[2048,128]{1,0:T(8,128)(2,1)}, u32[]{:S(2)}, u32[]{:S(2)}) %collective-permute-start.1) | collective-permute-done | bytes 524320 | tf_op jit(solution)/shard_map/ppermute | solution.py:226
  20.9 1.6 collective-permute-start.4
  22.5 1.5 collective-permute-start.3
  24.0 1.3 collective-permute-start.6
  25.7 1.1 convolution_convert_fusion.2
  26.7 5.7 %all-to-all-start.1 = ((bf16[8,32,512]{2,1,0:T(8,128)(2,1)}), bf16[8,32,512]{2,1,0:T(8,128)(2,1)S(1)}, u32[]{:S(2)}, u32[]{:S(2)}) async-start(bf16[8,32,512]{2,1,0:T(8,128)(2,1)} %bitcast.42), calls=%async_computation.1 | async-start | bytes 524288 | tf_op jit(solution)/shard_map/all_to_all | solution.py:157
  32.4 9.6 %collective-permute-done.6 = bf16[2048,128]{1,0:T(8,128)(2,1)S(1)} collective-permute-done((bf16[2048,128]{1,0:T(8,128)(2,1)S(1)}, bf16[2048,128]{1,0:T(8,128)(2,1)S(1)}, u32[]{:S(2)}, u32[]{:S(2)}) %collective-permute-start.6) | collective-permute-done | bytes 524320 | tf_op jit(solution)/shard_map/ppermute | solution.py:226
  42.1 2.1 %convolution_convert_fusion = bf16[256,4096]{1,0:T(8,128)(2,1)} fusion(bf16[128,4096]{1,0:T(8,128)(2,1)S(1)} %bitcast.35, s32[128]{0:T(128)S(1)} %get-tuple-element.64, s32[128]{0:T(128)S(1)} %get-tuple-element.65, s32[256]{0:T(256)S(1)} %get-tuple-element.61, s32[256]{0:T(256)S(1)} %get-tuple-element.62, s32[128]{0:T(128)S(1)} %get-tuple-element.63, ...), kind=kOutput, calls=%fused_computation | convolution fusion | flops 269680640 | bytes 3151360 | tf_op jit(solution)/shard_map/dot_general | solution.py:18
  44.2 3.7 %all-to-all-start.2 = ((bf16[8,32,4096]{2,1,0:T(8,128)(2,1)}), bf16[8,32,4096]{2,1,0:T(8,128)(2,1)S(1)}, u32[]{:S(2)}, u32[]{:S(2)}) async-start(bf16[8,32,4096]{2,1,0:T(8,128)(2,1)} %bitcast.38), calls=%async_computation.2 | async-start | bytes 4194304 | tf_op jit(solution)/shard_map/all_to_all | solution.py:157
  48.0 1.8 %fusion.11 = f32[256,1024]{1,0:T(8,128)S(1)} fusion(bf16[256,512]{1,0:T(8,128)(2,1)S(1)} %bitcast.39, bf16[1024,512]{1,0:T(8,128)(2,1)} %param.11), kind=kOutput, calls=%fused_computation.49 | convolution fusion | flops 268435456 | bytes 2359296 | tf_op jit(solution)/shard_map/dot_general | solution.py:18
  50.0 1.3 collective-permute-start.7
  52.0 2.0 %collective-permute-start.9 = (bf16[2048,128]{1,0:T(8,128)(2,1)S(1)}, bf16[2048,128]{1,0:T(8,128)(2,1)S(1)}, u32[]{:S(2)}, u32[]{:S(2)}) collective-permute-start(bf16[2048,128]{1,0:T(8,128)(2,1)S(1)} %broadcast_select_fusion.refs_0_), channel_id=1, source_target_pairs={{0,2},{2,0},{4,6},{6,4},{8,10},{10,8},{12,14},{14,12},{1,3},{3,1},... | collective-permute-start | bytes 1572872 | tf_op jit(solution)/shard_map/ppermute | solution.py:226
  54.0 1.5 collective-permute-start.11
  56.4 3.4 %copy-done.1 = bf16[1024,4096]{1,0:T(8,128)(2,1)S(1)} copy-done((bf16[1024,4096]{1,0:T(8,128)(2,1)S(1)}, bf16[1024,4096]{1,0:T(8,128)(2,1)}, u32[]{:S(2)}) %copy-start.1) | copy-done | bytes 8388632
  59.7 4.3 %gradient_term.1 = bf16[256,4096]{1,0:T(8,128)(2,1)S(1)} custom-call(bf16[256,1024]{1,0:T(8,128)(2,1)S(1)} %select_convert_fusion.1.space_ref, bf16[1024,4096]{1,0:T(8,128)(2,1)S(1)} %copy-done.1), custom_call_target="tpu_custom_call" | custom-call | flops 1000000 | bytes 10000 | tf_op jit(solution)/shard_map/gradient_term/pallas_call | solution.py:113
  64.1 1.3 copy-done.3
  65.4 17.0 %collective-permute-done.7 = bf16[2048,128]{1,0:T(8,128)(2,1)S(1)} collective-permute-done((bf16[2048,128]{1,0:T(8,128)(2,1)S(1)}, bf16[2048,128]{1,0:T(8,128)(2,1)S(1)}, u32[]{:S(2)}, u32[]{:S(2)}) %collective-permute-start.7) | collective-permute-done | bytes 524320 | tf_op jit(solution)/shard_map/ppermute | solution.py:226
  82.4 0.8 broadcast_select_fusion.1.refs_0_
  83.3 0.8 copy-done.7
  85.7 2.7 %collective-permute-done.12.refs_2_ = bf16[2048,128]{1,0:T(8,128)(2,1)} collective-permute-done((bf16[2048,128]{1,0:T(8,128)(2,1)}, bf16[2048,128]{1,0:T(8,128)(2,1)}, u32[]{:S(2)}, u32[]{:S(2)}) %collective-permute-start.12) | collective-permute-done | bytes 524320 | tf_op jit(solution)/shard_map/ppermute | solution.py:229
  88.3 3.7 %all-to-all-done.2 = bf16[8,32,4096]{2,1,0:T(8,128)(2,1)S(1)} async-done(((bf16[8,32,4096]{2,1,0:T(8,128)(2,1)}), bf16[8,32,4096]{2,1,0:T(8,128)(2,1)S(1)}, u32[]{:S(2)}, u32[]{:S(2)}) %all-to-all-start.2) | async-done | bytes 2097184 | tf_op jit(solution)/shard_map/all_to_all | solution.py:157
  92.8 1.2 collective-permute-start.15
  94.0 1.3 collective-permute-start.13
  96.0 4.4 %all-to-all-start.3 = ((bf16[8,32,4096]{2,1,0:T(8,128)(2,1)}), bf16[8,32,4096]{2,1,0:T(8,128)(2,1)}, u32[]{:S(2)}, u32[]{:S(2)}) async-start(bf16[8,32,4096]{2,1,0:T(8,128)(2,1)} %bitcast.37), calls=%async_computation.3 | async-start | bytes 4194304 | tf_op jit(solution)/shard_map/all_to_all | solution.py:157
  100.3 11.1 %weight_product.3 = f32[1024,512]{1,0:T(8,128)} custom-call(s32[14]{0:T(128)} %stack.26.place_ref, bf16[1024,4096]{1,0:T(8,128)(2,1)} %tokens_ref.9, bf16[4096,128]{1,0:T(8,128)(2,1)} %refs_0_.1, bf16[2048,128]{1,0:T(8,128)(2,1)} %collective-permute-done.refs_1_, bf16[2048,128]{1,0:T(8,128)(2,1)} %collective-permute-done.12.refs_2_, ...), custom_call_target="tpu_custom_call" | custom-call | flops 4294967296 | bytes 8388608 | tf_op jit(solution)/shard_map/weight_product/pallas_call | solution.py:63
  111.5 6.4 %collective-permute-done.15.refs_2_ = bf16[2048,128]{1,0:T(8,128)(2,1)} collective-permute-done((bf16[2048,128]{1,0:T(8,128)(2,1)}, bf16[2048,128]{1,0:T(8,128)(2,1)}, u32[]{:S(2)}, u32[]{:S(2)}) %collective-permute-start.15) | collective-permute-done | bytes 524320 | tf_op jit(solution)/shard_map/ppermute | solution.py:226
  117.9 1.3 collective-permute-start.17
  119.3 3.4 %copy-done.2 = bf16[1024,4096]{1,0:T(8,128)(2,1)S(1)} copy-done((bf16[1024,4096]{1,0:T(8,128)(2,1)S(1)}, bf16[1024,4096]{1,0:T(8,128)(2,1)}, u32[]{:S(2)}) %copy-start.2) | copy-done | bytes 8388632
  122.7 1.0 copy-done.5
  123.7 1.0 copy-done.8
  124.8 1.0 copy-done.10
  125.8 4.8 %weight_product.4 = f32[1024,256]{1,0:T(8,128)S(1)} custom-call(s32[8]{0:T(128)S(1)} %stack.29.place_ref, bf16[1024,4096]{1,0:T(8,128)(2,1)S(1)} %copy-done.2, bf16[2048,128]{1,0:T(8,128)(2,1)S(1)} %copy-done.5, bf16[2048,128]{1,0:T(8,128)(2,1)S(1)} %copy-done.8, bf16[2048,128]{1,0:T(8,128)(2,1)S(1)} %copy-done.10, ...), custom_call_target="tpu_custom_call" | custom-call | flops 1000000 | bytes 10000 | tf_op jit(solution)/shard_map/weight_product/pallas_call | solution.py:63
  130.6 4.9 %weight_product.5 = f32[1024,256]{1,0:T(8,128)S(1)} custom-call(s32[8]{0:T(128)S(1)} %stack.29.place_ref, bf16[1024,4096]{1,0:T(8,128)(2,1)S(1)} %copy-done.2, bf16[2048,128]{1,0:T(8,128)(2,1)S(1)} %copy-done.6, bf16[2048,128]{1,0:T(8,128)(2,1)} %collective-permute-done.13.refs_1_, bf16[2048,128]{1,0:T(8,128)(2,1)} %collective-permute-done.15.refs_2_, ...), custom_call_target="tpu_custom_call" | custom-call | flops 1000000 | bytes 10000 | tf_op jit(solution)/shard_map/weight_product/pallas_call | solution.py:63
  136.1 3.0 %hidden_product.1 = f32[256,1024]{1,0:T(8,128)S(1)} custom-call(bf16[256,4096]{1,0:T(8,128)(2,1)S(1)} %bitcast.36, bf16[1024,4096]{1,0:T(8,128)(2,1)S(1)} %copy-done.2), custom_call_target="tpu_custom_call" | custom-call | flops 1000000 | bytes 10000 | tf_op jit(solution)/shard_map/hidden_product/pallas_call | solution.py:90
  139.8 2.3 %collective-permute-done.16 = f32[256,1024]{1,0:T(8,128)S(1)} collective-permute-done((f32[256,1024]{1,0:T(8,128)S(1)}, f32[256,1024]{1,0:T(8,128)S(1)}, u32[]{:S(2)}, u32[]{:S(2)}) %collective-permute-start.16) | collective-permute-done | bytes 1048608 | tf_op jit(solution)/shard_map/ppermute | solution.py:176
  142.4 1.2 fusion.1
  143.5 1.5 add_convert_fusion
  145.1 1.6 all-to-all-done.3
  146.6 3.4 %all-to-all-start.4 = ((bf16[8,32,512]{2,1,0:T(8,128)(2,1)}), bf16[8,32,512]{2,1,0:T(8,128)(2,1)S(1)}, u32[]{:S(2)}, u32[]{:S(2)}) async-start(bf16[8,32,512]{2,1,0:T(8,128)(2,1)} %bitcast.20), calls=%async_computation.4 | async-start | bytes 524288 | tf_op jit(solution)/shard_map/all_to_all | solution.py:157
  150.0 3.2 %convolution_convert_fusion.1 = bf16[128,4096]{1,0:T(8,128)(2,1)} fusion(bf16[256,4096]{1,0:T(8,128)(2,1)} %bitcast.10, s32[128]{0:T(128)S(1)} %get-tuple-element.64, s32[128]{0:T(128)S(1)} %get-tuple-element.65, s32[256]{0:T(256)S(1)} %get-tuple-element.61, s32[256]{0:T(256)S(1)} %get-tuple-element.62, s32[128]{0:T(128)S(1)} %get-tuple-element.63, ...), kind=kOutput, calls=%fused_computation.1 | convolution fusion | flops 269156352 | bytes 3151360 | tf_op jit(solution)/shard_map/dot_general | solution.py:18
  153.3 5.9 %all-to-all-done.4 = bf16[8,32,512]{2,1,0:T(8,128)(2,1)S(1)} async-done(((bf16[8,32,512]{2,1,0:T(8,128)(2,1)}), bf16[8,32,512]{2,1,0:T(8,128)(2,1)S(1)}, u32[]{:S(2)}, u32[]{:S(2)}) %all-to-all-start.4) | async-done | bytes 262176 | tf_op jit(solution)/shard_map/all_to_all | solution.py:157
  159.2 1.1 convolution_convert_fusion.3
  (81 shorter events, 9.6 us)
Async XLA Ops:
  0.6 41.5 %copy-start = (bf16[4,32,4096]{2,1,0:T(8,128)(2,1)S(1)}, bf16[4,32,4096]{2,1,0:T(8,128)(2,1)}, u32[]{:S(2)}) copy-start(bf16[4,32,4096]{2,1,0:T(8,128)(2,1)} %param.9) | copy-start | bytes 3145732
  1.8 14.8 %collective-permute-start.2 = (bf16[2048,128]{1,0:T(8,128)(2,1)S(1)}, bf16[2048,128]{1,0:T(8,128)(2,1)S(1)}, u32[]{:S(2)}, u32[]{:S(2)}) collective-permute-start(bf16[2048,128]{1,0:T(8,128)(2,1)S(1)} %constant_dynamic-slice_fusion), channel_id=1, source_target_pairs={{4,8},{6,10},{8,4},{10,6},{5,9},{7,11},{9,5},{11,7},{20,24},{22,26... | collective-permute-start | bytes 1572872 | tf_op jit(solution)/shard_map/ppermute | solution.py:226
  2.5 17.7 %collective-permute-start.1 = (bf16[2048,128]{1,0:T(8,128)(2,1)S(1)}, bf16[2048,128]{1,0:T(8,128)(2,1)}, u32[]{:S(2)}, u32[]{:S(2)}) collective-permute-start(bf16[2048,128]{1,0:T(8,128)(2,1)S(1)} %constant_dynamic-slice_fusion), channel_id=1, source_target_pairs={{0,4},{2,6},{4,0},{6,2},{8,12},{10,14},{12,8},{14,10},{1,5},{3,7},... | collective-permute-start | bytes 1572872 | tf_op jit(solution)/shard_map/ppermute | solution.py:226
  8.4 24.0 %collective-permute-start = (bf16[2048,128]{1,0:T(8,128)(2,1)S(1)}, bf16[2048,128]{1,0:T(8,128)(2,1)}, u32[]{:S(2)}, u32[]{:S(2)}) collective-permute-start(bf16[2048,128]{1,0:T(8,128)(2,1)S(1)} %constant_dynamic-slice_fusion), channel_id=1, source_target_pairs={{0,2},{2,0},{4,6},{6,4},{8,10},{10,8},{12,14},{14,12},{1,3},{3,1},... | collective-permute-start | bytes 1572872 | tf_op jit(solution)/shard_map/ppermute | solution.py:226
  12.3 12.9 %all-to-all-start = ((s32[8,1,1]{2,1,0:T(1,128)}), s32[8,1,1]{2,1,0:T(1,128)S(1)}, u32[]{:S(2)}, u32[]{:S(2)}) async-start(s32[8,1,1]{2,1,0:T(1,128)} %copy.12), calls=%async_computation | async-start | bytes 8192 | tf_op jit(solution)/shard_map/all_to_all | solution.py:157
  16.6 27.6 %copy-start.13 = (bf16[2048,128]{1,0:T(8,128)(2,1)}, bf16[2048,128]{1,0:T(8,128)(2,1)S(1)}, u32[]{:S(2)}) copy-start(bf16[2048,128]{1,0:T(8,128)(2,1)S(1)} %collective-permute-done.2) | copy-start | bytes 1572868
  20.2 21.9 %collective-permute-start.5 = (bf16[2048,128]{1,0:T(8,128)(2,1)}, bf16[2048,128]{1,0:T(8,128)(2,1)S(1)}, u32[]{:S(2)}, u32[]{:S(2)}) collective-permute-start(bf16[2048,128]{1,0:T(8,128)(2,1)} %collective-permute-done.1.refs_3_), channel_id=1, source_target_pairs={{4,8},{6,10},{8,4},{10,6},{5,9},{7,11},{9,5},{11,7},{20,24},{22,26... | collective-permute-start | bytes 1572872 | tf_op jit(solution)/shard_map/ppermute | solution.py:226
  20.9 21.2 %collective-permute-start.4 = (bf16[2048,128]{1,0:T(8,128)(2,1)}, bf16[2048,128]{1,0:T(8,128)(2,1)}, u32[]{:S(2)}, u32[]{:S(2)}) collective-permute-start(bf16[2048,128]{1,0:T(8,128)(2,1)} %collective-permute-done.1.refs_3_), channel_id=1, source_target_pairs={{0,2},{2,0},{4,6},{6,4},{8,10},{10,8},{12,14},{14,12},{1,3},{3,1},... | collective-permute-start | bytes 1572872 | tf_op jit(solution)/shard_map/ppermute | solution.py:226
  22.5 19.6 %collective-permute-start.3 = (bf16[2048,128]{1,0:T(8,128)(2,1)}, bf16[2048,128]{1,0:T(8,128)(2,1)}, u32[]{:S(2)}, u32[]{:S(2)}) collective-permute-start(bf16[2048,128]{1,0:T(8,128)(2,1)} %collective-permute-done.1.refs_3_), channel_id=1, source_target_pairs={{0,16},{16,0},{1,17},{17,1},{2,18},{18,2},{3,19},{19,3},{4,20},{20... | collective-permute-start | bytes 1572872 | tf_op jit(solution)/shard_map/ppermute | solution.py:229
  24.0 18.1 %collective-permute-start.6 = (bf16[2048,128]{1,0:T(8,128)(2,1)S(1)}, bf16[2048,128]{1,0:T(8,128)(2,1)S(1)}, u32[]{:S(2)}, u32[]{:S(2)}) collective-permute-start(bf16[2048,128]{1,0:T(8,128)(2,1)S(1)} %collective-permute-done.2), channel_id=1, source_target_pairs={{4,0},{6,2},{8,12},{10,14},{5,1},{7,3},{9,13},{11,15},{20,16},{22,... | collective-permute-start | bytes 1572872 | tf_op jit(solution)/shard_map/ppermute | solution.py:226
  26.7 17.5 %all-to-all-start.1 = ((bf16[8,32,512]{2,1,0:T(8,128)(2,1)}), bf16[8,32,512]{2,1,0:T(8,128)(2,1)S(1)}, u32[]{:S(2)}, u32[]{:S(2)}) async-start(bf16[8,32,512]{2,1,0:T(8,128)(2,1)} %bitcast.42), calls=%async_computation.1 | async-start | bytes 524288 | tf_op jit(solution)/shard_map/all_to_all | solution.py:157
  42.1 2.2 %copy-start.17 = (bf16[2048,128]{1,0:T(8,128)(2,1)}, bf16[2048,128]{1,0:T(8,128)(2,1)S(1)}, u32[]{:S(2)}) copy-start(bf16[2048,128]{1,0:T(8,128)(2,1)S(1)} %collective-permute-done.6) | copy-start | bytes 1572868
  42.1 2.2 %copy-start.15 = (bf16[2048,128]{1,0:T(8,128)(2,1)}, bf16[2048,128]{1,0:T(8,128)(2,1)S(1)}, u32[]{:S(2)}) copy-start(bf16[2048,128]{1,0:T(8,128)(2,1)S(1)} %collective-permute-done.5) | copy-start | bytes 1572868
  44.2 47.8 %all-to-all-start.2 = ((bf16[8,32,4096]{2,1,0:T(8,128)(2,1)}), bf16[8,32,4096]{2,1,0:T(8,128)(2,1)S(1)}, u32[]{:S(2)}, u32[]{:S(2)}) async-start(bf16[8,32,4096]{2,1,0:T(8,128)(2,1)} %bitcast.38), calls=%async_computation.2 | async-start | bytes 4194304 | tf_op jit(solution)/shard_map/all_to_all | solution.py:157
  47.9 2.0 %copy-start.19 = (s32[1024]{0:T(1024)S(1)}, s32[1024]{0:T(1024)}, u32[]{:S(2)}) copy-start(s32[1024]{0:T(1024)} %param.12) | copy-start | bytes 12292
  48.0 2.0 %copy-start.16 = (bf16[2048,128]{1,0:T(8,128)(2,1)S(1)}, bf16[2048,128]{1,0:T(8,128)(2,1)}, u32[]{:S(2)}) copy-start(bf16[2048,128]{1,0:T(8,128)(2,1)} %copy-done.15) | copy-start | bytes 1572868
  48.0 3.3 %copy-start.14 = (bf16[2048,128]{1,0:T(8,128)(2,1)S(1)}, bf16[2048,128]{1,0:T(8,128)(2,1)}, u32[]{:S(2)}) copy-start(bf16[2048,128]{1,0:T(8,128)(2,1)} %copy-done.13) | copy-start | bytes 1572868
  48.0 3.3 %copy-start.18 = (bf16[2048,128]{1,0:T(8,128)(2,1)S(1)}, bf16[2048,128]{1,0:T(8,128)(2,1)}, u32[]{:S(2)}) copy-start(bf16[2048,128]{1,0:T(8,128)(2,1)} %copy-done.17) | copy-start | bytes 1572868
  49.8 5.7 %collective-permute-start.8 = (f32[256,1024]{1,0:T(8,128)S(1)}, f32[256,1024]{1,0:T(8,128)S(1)}, u32[]{:S(2)}, u32[]{:S(2)}) collective-permute-start(f32[256,1024]{1,0:T(8,128)S(1)} %fusion.11), channel_id=1, source_target_pairs={{0,1},{1,0},{2,3},{3,2},{4,5},{5,4},{6,7},{7,6},{8,9},{9,8},{10,11... | collective-permute-start | bytes 3145736 | tf_op jit(solution)/shard_map/ppermute | solution.py:176
  50.0 32.4 %collective-permute-start.7 = (bf16[2048,128]{1,0:T(8,128)(2,1)S(1)}, bf16[2048,128]{1,0:T(8,128)(2,1)S(1)}, u32[]{:S(2)}, u32[]{:S(2)}) collective-permute-start(bf16[2048,128]{1,0:T(8,128)(2,1)S(1)} %copy-done.16), channel_id=1, source_target_pairs={{4,0},{6,2},{8,12},{10,14},{5,1},{7,3},{9,13},{11,15},{20,16},{22,... | collective-permute-start | bytes 1572872 | tf_op jit(solution)/shard_map/ppermute | solution.py:226
  51.4 12.7 %copy-start.4 = (bf16[2048,128]{1,0:T(8,128)(2,1)}, bf16[2048,128]{1,0:T(8,128)(2,1)S(1)}, u32[]{:S(2)}) copy-start(bf16[2048,128]{1,0:T(8,128)(2,1)S(1)} %broadcast_select_fusion.refs_0_) | copy-start | bytes 1572868
  51.4 31.9 %collective-permute-start.10 = (bf16[2048,128]{1,0:T(8,128)(2,1)S(1)}, bf16[2048,128]{1,0:T(8,128)(2,1)S(1)}, u32[]{:S(2)}, u32[]{:S(2)}) collective-permute-start(bf16[2048,128]{1,0:T(8,128)(2,1)S(1)} %broadcast_select_fusion.refs_0_), channel_id=1, source_target_pairs={{0,16},{16,0},{1,17},{17,1},{2,18},{18,2},{3,19},{19,3},{4,20},{20... | collective-permute-start | bytes 1572872 | tf_op jit(solution)/shard_map/ppermute | solution.py:229
  52.0 32.1 %collective-permute-start.9 = (bf16[2048,128]{1,0:T(8,128)(2,1)S(1)}, bf16[2048,128]{1,0:T(8,128)(2,1)S(1)}, u32[]{:S(2)}, u32[]{:S(2)}) collective-permute-start(bf16[2048,128]{1,0:T(8,128)(2,1)S(1)} %broadcast_select_fusion.refs_0_), channel_id=1, source_target_pairs={{0,2},{2,0},{4,6},{6,4},{8,10},{10,8},{12,14},{14,12},{1,3},{3,1},... | collective-permute-start | bytes 1572872 | tf_op jit(solution)/shard_map/ppermute | solution.py:226
  54.0 30.1 %collective-permute-start.11 = (bf16[2048,128]{1,0:T(8,128)(2,1)}, bf16[2048,128]{1,0:T(8,128)(2,1)S(1)}, u32[]{:S(2)}, u32[]{:S(2)}) collective-permute-start(bf16[2048,128]{1,0:T(8,128)(2,1)} %collective-permute-done.4.refs_5_), channel_id=1, source_target_pairs={{0,16},{16,0},{1,17},{17,1},{2,18},{18,2},{3,19},{19,3},{4,20},{20... | collective-permute-start | bytes 1572872 | tf_op jit(solution)/shard_map/ppermute | solution.py:229
  55.5 32.9 %collective-permute-start.12 = (bf16[2048,128]{1,0:T(8,128)(2,1)}, bf16[2048,128]{1,0:T(8,128)(2,1)}, u32[]{:S(2)}, u32[]{:S(2)}) collective-permute-start(bf16[2048,128]{1,0:T(8,128)(2,1)} %collective-permute-done.refs_1_), channel_id=1, source_target_pairs={{0,16},{16,0},{1,17},{17,1},{2,18},{18,2},{3,19},{19,3},{4,20},{20... | collective-permute-start | bytes 1572872 | tf_op jit(solution)/shard_map/ppermute | solution.py:229
  56.4 3.4 %copy-start.1 = (bf16[1024,4096]{1,0:T(8,128)(2,1)S(1)}, bf16[1024,4096]{1,0:T(8,128)(2,1)}, u32[]{:S(2)}) copy-start(bf16[1024,4096]{1,0:T(8,128)(2,1)} %tokens_ref.9) | copy-start | bytes 25165828
  64.1 1.4 copy-start.3
  83.3 0.8 copy-start.7
  84.1 0.8 copy-start.9
  84.9 0.8 copy-start.20
  92.1 19.4 %collective-permute-start.14 = (bf16[2048,128]{1,0:T(8,128)(2,1)}, bf16[2048,128]{1,0:T(8,128)(2,1)}, u32[]{:S(2)}, u32[]{:S(2)}) collective-permute-start(bf16[2048,128]{1,0:T(8,128)(2,1)} %copy-done.9), channel_id=1, source_target_pairs={{0,16},{16,0},{1,17},{17,1},{2,18},{18,2},{3,19},{19,3},{4,20},{20... | collective-permute-start | bytes 1572872 | tf_op jit(solution)/shard_map/ppermute | solution.py:229
  92.8 25.1 %collective-permute-start.15 = (bf16[2048,128]{1,0:T(8,128)(2,1)}, bf16[2048,128]{1,0:T(8,128)(2,1)}, u32[]{:S(2)}, u32[]{:S(2)}) collective-permute-start(bf16[2048,128]{1,0:T(8,128)(2,1)} %broadcast_select_fusion.1.refs_0_), channel_id=1, source_target_pairs={{0,2},{2,0},{4,6},{6,4},{8,10},{10,8},{12,14},{14,12},{1,3},{3,1},... | collective-permute-start | bytes 1572872 | tf_op jit(solution)/shard_map/ppermute | solution.py:226
  94.0 23.9 %collective-permute-start.13 = (bf16[2048,128]{1,0:T(8,128)(2,1)}, bf16[2048,128]{1,0:T(8,128)(2,1)}, u32[]{:S(2)}, u32[]{:S(2)}) collective-permute-start(bf16[2048,128]{1,0:T(8,128)(2,1)} %broadcast_select_fusion.1.refs_0_), channel_id=1, source_target_pairs={{0,16},{16,0},{1,17},{17,1},{2,18},{18,2},{3,19},{19,3},{4,20},{20... | collective-permute-start | bytes 1572872 | tf_op jit(solution)/shard_map/ppermute | solution.py:229
  96.0 50.6 %all-to-all-start.3 = ((bf16[8,32,4096]{2,1,0:T(8,128)(2,1)}), bf16[8,32,4096]{2,1,0:T(8,128)(2,1)}, u32[]{:S(2)}, u32[]{:S(2)}) async-start(bf16[8,32,4096]{2,1,0:T(8,128)(2,1)} %bitcast.37), calls=%async_computation.3 | async-start | bytes 4194304 | tf_op jit(solution)/shard_map/all_to_all | solution.py:157
  117.9 12.7 %collective-permute-start.17 = (bf16[2048,128]{1,0:T(8,128)(2,1)}, bf16[2048,128]{1,0:T(8,128)(2,1)}, u32[]{:S(2)}, u32[]{:S(2)}) collective-permute-start(bf16[2048,128]{1,0:T(8,128)(2,1)} %collective-permute-done.15.refs_2_), channel_id=1, source_target_pairs={{0,16},{16,0},{1,17},{17,1},{2,18},{18,2},{3,19},{19,3},{4,20},{20... | collective-permute-start | bytes 1572872 | tf_op jit(solution)/shard_map/ppermute | solution.py:229
  119.3 3.4 %copy-start.2 = (bf16[1024,4096]{1,0:T(8,128)(2,1)S(1)}, bf16[1024,4096]{1,0:T(8,128)(2,1)}, u32[]{:S(2)}) copy-start(bf16[1024,4096]{1,0:T(8,128)(2,1)} %tokens_ref.9) | copy-start | bytes 25165828
  122.7 1.0 copy-start.5
  123.7 1.0 copy-start.8
  124.8 1.0 copy-start.10
  125.8 4.8 %copy-start.6 = (bf16[2048,128]{1,0:T(8,128)(2,1)S(1)}, bf16[2048,128]{1,0:T(8,128)(2,1)}, u32[]{:S(2)}) copy-start(bf16[2048,128]{1,0:T(8,128)(2,1)} %broadcast_select_fusion.1.refs_0_) | copy-start | bytes 1572868
  130.6 5.0 %copy-start.11 = (f32[1024,512]{1,0:T(8,128)S(1)}, f32[1024,512]{1,0:T(8,128)}, u32[]{:S(2)}) copy-start(f32[1024,512]{1,0:T(8,128)} %weight_product.3) | copy-start | bytes 6291460
  136.1 7.5 %collective-permute-start.18 = (f32[1024,512]{1,0:T(8,128)S(1)}, f32[1024,512]{1,0:T(8,128)S(1)}, u32[]{:S(2)}, u32[]{:S(2)}) collective-permute-start(f32[1024,512]{1,0:T(8,128)S(1)} %fusion), channel_id=1, source_target_pairs={{0,1},{1,0},{2,3},{3,2},{4,5},{5,4},{6,7},{7,6},{8,9},{9,8},{10,11... | collective-permute-start | bytes 6291464 | tf_op jit(solution)/shard_map/ppermute | solution.py:336
  139.2 3.1 %copy-start.12 = (bf16[1024,512]{1,0:T(8,128)(2,1)S(1)}, bf16[1024,512]{1,0:T(8,128)(2,1)}, u32[]{:S(2)}) copy-start(bf16[1024,512]{1,0:T(8,128)(2,1)} %param.11) | copy-start | bytes 3145732
  139.2 2.8 %collective-permute-start.16 = (f32[256,1024]{1,0:T(8,128)S(1)}, f32[256,1024]{1,0:T(8,128)S(1)}, u32[]{:S(2)}, u32[]{:S(2)}) collective-permute-start(f32[256,1024]{1,0:T(8,128)S(1)} %hidden_product.1), channel_id=1, source_target_pairs={{0,1},{1,0},{2,3},{3,2},{4,5},{5,4},{6,7},{7,6},{8,9},{9,8},{10,11... | collective-permute-start | bytes 3145736 | tf_op jit(solution)/shard_map/ppermute | solution.py:176
  146.6 12.6 %all-to-all-start.4 = ((bf16[8,32,512]{2,1,0:T(8,128)(2,1)}), bf16[8,32,512]{2,1,0:T(8,128)(2,1)S(1)}, u32[]{:S(2)}, u32[]{:S(2)}) async-start(bf16[8,32,512]{2,1,0:T(8,128)(2,1)} %bitcast.20), calls=%async_computation.4 | async-start | bytes 524288 | tf_op jit(solution)/shard_map/all_to_all | solution.py:157

commit v6 on v5

--- a/solution.py
+++ b/solution.py
@@ -55,6 +55,10 @@
             copy.wait()
 
     out_ref[...] = jnp.dot(tokens_ref[...], weight[...], preferred_element_type=jnp.float32)
+
+
+def flat(places):
+    return jnp.stack([jnp.int32(v) for place in places for v in place])
 
 
 def product(tokens, pieces, places, width, estimate, vmem=VMEM_BYTES):
@@ -77,7 +81,7 @@
         compiler_params=pltpu.CompilerParams(vmem_limit_bytes=vmem),
         cost_estimate=estimate,
         name="weight_product",
-    )(jnp.stack([jnp.int32(v) for place in places for v in place]), tokens, *pieces)
+    )(places, tokens, *pieces)
 
 
 def hidden_kernel(maps_ref, tokens_ref, out_ref):
@@ -231,12 +235,26 @@
     output_columns = cotangent.shape[1]
     barrier = lax.optimization_barrier
 
+    parity = layer % 2
+    places_here = flat(
+        [(0, 2 * parity + side)]
+        + [
+            (row, column)
+            for column in (
+                2 * parity + 1 - side,
+                2 * (1 - parity) + side,
+                2 * (1 - parity) + 1 - side,
+            )
+            for row in (group, 1 - group)
+        ]
+    )
+    places_half = flat([(row, column) for column in (side, 1 - side) for row in (group, 1 - group)])
     half = lax.dynamic_slice_in_dim(base_weight, group * (width // 2), width // 2, 0)
     near = over(half, pair)
     mid_next = over(half, middle)
     own_across = over(half, across)
     asked = work.exchange(work.wanted.reshape(-1, 1))
-    near, mid_next = barrier((near, mid_next))
+    near, mid_next, places_here, places_half = barrier((near, mid_next, places_here, places_half))
     mid_far = over(near, middle)
     end_next = over(mid_next, outward)
     near_across = over(near, across)
@@ -257,32 +275,15 @@
     own_across_rest = twin(own_across)
     backward_pass = work.rank_space(dot(got_b, cotangent, ((1,), (1,))))
     home_a = gradient_term(backward_pass, tokens)
-    end_far, home_a = barrier((end_far, home_a))
+    end_far, home_a, following_across = barrier((end_far, home_a, following_across))
     far = jnp.where(inner, mid_far, end_far)
-    (
-        got_a,
-        home_a,
-        far,
-        following_across,
-        following_rest,
-        near_across_rest,
-        own_across_rest,
-    ) = barrier(
-        (
-            got_a,
-            home_a,
-            far,
-            following_across,
-            following_rest,
-            near_across_rest,
-            own_across_rest,
-        )
+    got_a, home_a, following_rest, near_across_rest, own_across_rest = barrier(
+        (got_a, home_a, following_rest, near_across_rest, own_across_rest)
     )
     came_a = work.exchange(home_a)
     far_across = over(far, across)
     far_rest = twin(far)
     following_across_rest = twin(following_across)
-    parity = layer % 2
     product_here = product(
         tokens,
         [
@@ -294,15 +295,7 @@
             near_across,
             near_across_rest,
         ],
-        [
-            (0, 2 * parity + side),
-            (group, 2 * parity + 1 - side),
-            (1 - group, 2 * parity + 1 - side),
-            (group, 2 * (1 - parity) + side),
-            (1 - group, 2 * (1 - parity) + side),
-            (group, 2 * (1 - parity) + 1 - side),
-            (1 - group, 2 * (1 - parity) + 1 - side),
-        ],
+        places_here,
         output_columns,
         cost(*tokens.shape, output_columns),
         56 * 1024 * 1024,
@@ -315,7 +308,7 @@
         product(
             tokens,
             list(pieces),
-            [(row, column) for column in (side, 1 - side) for row in (group, 1 - group)],
+            places_half,
             output_columns // 2,
             LITTLE,
         )

time: 161 us -> 159 us (0.988)
  waiting for transfers between devices: 52.7 us -> 47.3 us
  starting transfers between devices: 44.8 us -> 49.3 us
  local copies, waits for them, and re-layouts: 18.2 us -> 16.3 us
    ppermute x9, waiting for transfers between devices: 36.6 us -> 29.4 us  [over(): return lax.ppermute(part, 'dp', pairs)]
    ppermute x9, starting transfers between devices: 16.2 us -> 21.4 us  [over(): return lax.ppermute(part, 'dp', pairs)]
    unnamed x42 -> x36, local copies, waits for them, and re-layouts: 13.7 us -> 11.8 us
  transfers between devices with their start and end apart: 24 -> 24, of which waited for: 9 -> 8; matrix products, arithmetic and copies ran while one was open for 11% -> 11% of each run, Pallas kernels for 18% -> 18%
where the time goes in v6:
time: 159 us; the launch traced here: 158 us
  starting transfers between devices  49.3 us (31%)
  waiting for transfers between devices  47.3 us (30%)
  Pallas kernels  28.5 us (18%)
  local copies, waits for them, and re-layouts  16.3 us (10%)
  matrix products  11.9 us (7%)
  other arithmetic  3.23 us (2%)
    ppermute x9, waiting for transfers between devices, over(): return lax.ppermute(part, 'dp', pairs)  29.4 us
    ppermute x9, starting transfers between devices, over(): return lax.ppermute(part, 'dp', pairs)  21.4 us
    pallas_call x3, Pallas kernels, product(): pl.pallas_call(functools.partial(product_kernel, len(pieces)), out_shape=...  21.1 us
    all_to_all x5, starting transfers between devices, exchange(): lax.all_to_all(sent.reshape(self.peers, -1, sent.shape[1]), 'dp', split_a...  20.5 us
    dot_general x7, matrix products, dot(): lax.dot_general(left, right, ((contract[0], contract[1]), ((), ())), pref...  11.9 us
    unnamed x36, local copies, waits for them, and re-layouts  11.8 us
    all_to_all x5, waiting for transfers between devices, exchange(): lax.all_to_all(sent.reshape(self.peers, -1, sent.shape[1]), 'dp', split_a...  11.5 us
    ppermute x7, starting transfers between devices, twin(): return lax.ppermute(part, 'groups', SWAP)  6.69 us
  transfers between devices with their start and end apart: 24, of which 8 were waited for; matrix products, arithmetic and copies ran while one was open for 11% of the time, Pallas kernels for 18%

profile of v6, /device:TPU:0, one launch (start us, length us, event | category | flops | bytes accessed | tf_op | source)
XLA Modules:
  0.0 157.8 jit_solution(14665531844050981148)
XLA Ops:
  0.7 1.2 constant_dynamic-slice_fusion
  1.8 0.7 collective-permute-start.2
  2.5 5.9 %collective-permute-start.1 = (bf16[2048,128]{1,0:T(8,128)(2,1)S(1)}, bf16[2048,128]{1,0:T(8,128)(2,1)}, u32[]{:S(2)}, u32[]{:S(2)}) collective-permute-start(bf16[2048,128]{1,0:T(8,128)(2,1)S(1)} %constant_dynamic-slice_fusion), channel_id=1, source_target_pairs={{0,4},{2,6},{4,0},{6,2},{8,12},{10,14},{12,8},{14,10},{1,5},{3,7},... | collective-permute-start | bytes 1572872 | tf_op jit(solution)/shard_map/ppermute | solution.py:230
  8.4 1.5 collective-permute-start
  9.9 0.8 slice_reduce_fusion
  10.7 0.8 select_reduce_fusion.1
  12.4 3.3 %all-to-all-start = ((s32[8,1,1]{2,1,0:T(1,128)}), s32[8,1,1]{2,1,0:T(1,128)S(1)}, u32[]{:S(2)}, u32[]{:S(2)}) async-start(s32[8,1,1]{2,1,0:T(1,128)} %copy.12), calls=%async_computation | async-start | bytes 8192 | tf_op jit(solution)/shard_map/all_to_all | solution.py:161
  16.5 0.9 constant_dynamic-slice_fusion.1
  17.4 2.8 %collective-permute-done.1.refs_3_ = bf16[2048,128]{1,0:T(8,128)(2,1)} collective-permute-done((bf16[2048,128]{1,0:T(8,128)(2,1)S(1)}, bf16[2048,128]{1,0:T(8,128)(2,1)}, u32[]{:S(2)}, u32[]{:S(2)}) %collective-permute-start.1) | collective-permute-done | bytes 524320 | tf_op jit(solution)/shard_map/ppermute | solution.py:230
  20.9 1.6 %collective-permute-start.4 = (bf16[2048,128]{1,0:T(8,128)(2,1)}, bf16[2048,128]{1,0:T(8,128)(2,1)}, u32[]{:S(2)}, u32[]{:S(2)}) collective-permute-start(bf16[2048,128]{1,0:T(8,128)(2,1)} %collective-permute-done.1.refs_3_), channel_id=1, source_target_pairs={{0,2},{2,0},{4,6},{6,4},{8,10},{10,8},{12,14},{14,12},{1,3},{3,1},... | collective-permute-start | bytes 1572872 | tf_op jit(solution)/shard_map/ppermute | solution.py:230
  22.5 1.5 collective-permute-start.3
  24.0 1.3 collective-permute-start.6
  25.7 1.0 convolution_convert_fusion.2
  26.7 5.7 %all-to-all-start.1 = ((bf16[8,32,512]{2,1,0:T(8,128)(2,1)}), bf16[8,32,512]{2,1,0:T(8,128)(2,1)S(1)}, u32[]{:S(2)}, u32[]{:S(2)}) async-start(bf16[8,32,512]{2,1,0:T(8,128)(2,1)} %bitcast.42), calls=%async_computation.1 | async-start | bytes 524288 | tf_op jit(solution)/shard_map/all_to_all | solution.py:161
  32.4 9.6 %collective-permute-done.6 = bf16[2048,128]{1,0:T(8,128)(2,1)S(1)} collective-permute-done((bf16[2048,128]{1,0:T(8,128)(2,1)S(1)}, bf16[2048,128]{1,0:T(8,128)(2,1)S(1)}, u32[]{:S(2)}, u32[]{:S(2)}) %collective-permute-start.6) | collective-permute-done | bytes 524320 | tf_op jit(solution)/shard_map/ppermute | solution.py:230
  42.1 2.1 %convolution_convert_fusion = bf16[256,4096]{1,0:T(8,128)(2,1)} fusion(bf16[128,4096]{1,0:T(8,128)(2,1)S(1)} %bitcast.35, s32[128]{0:T(128)S(1)} %get-tuple-element.66, s32[128]{0:T(128)S(1)} %get-tuple-element.67, s32[256]{0:T(256)S(1)} %get-tuple-element.63, s32[256]{0:T(256)S(1)} %get-tuple-element.64, s32[128]{0:T(128)S(1)} %get-tuple-element.65, ...), kind=kOutput, calls=%fused_computation | convolution fusion | flops 269680640 | bytes 3151360 | tf_op jit(solution)/shard_map/dot_general | solution.py:18
  44.3 3.7 %all-to-all-start.2 = ((bf16[8,32,4096]{2,1,0:T(8,128)(2,1)}), bf16[8,32,4096]{2,1,0:T(8,128)(2,1)S(1)}, u32[]{:S(2)}, u32[]{:S(2)}) async-start(bf16[8,32,4096]{2,1,0:T(8,128)(2,1)} %bitcast.38), calls=%async_computation.2 | async-start | bytes 4194304 | tf_op jit(solution)/shard_map/all_to_all | solution.py:161
  48.0 1.8 %fusion.11 = f32[256,1024]{1,0:T(8,128)S(1)} fusion(bf16[256,512]{1,0:T(8,128)(2,1)S(1)} %bitcast.39, bf16[1024,512]{1,0:T(8,128)(2,1)} %param.11), kind=kOutput, calls=%fused_computation.49 | convolution fusion | flops 268435456 | bytes 2359296 | tf_op jit(solution)/shard_map/dot_general | solution.py:18
  50.0 2.1 %collective-permute-start.9 = (bf16[2048,128]{1,0:T(8,128)(2,1)S(1)}, bf16[2048,128]{1,0:T(8,128)(2,1)}, u32[]{:S(2)}, u32[]{:S(2)}) collective-permute-start(bf16[2048,128]{1,0:T(8,128)(2,1)S(1)} %broadcast_select_fusion.1.refs_0_), channel_id=1, source_target_pairs={{0,2},{2,0},{4,6},{6,4},{8,10},{10,8},{12,14},{14,12},{1,3},{3,1},... | collective-permute-start | bytes 1572872 | tf_op jit(solution)/shard_map/ppermute | solution.py:230
  52.1 1.3 collective-permute-start.7
  54.0 1.5 collective-permute-start.11
  56.4 3.4 %copy-done.1 = bf16[1024,4096]{1,0:T(8,128)(2,1)S(1)} copy-done((bf16[1024,4096]{1,0:T(8,128)(2,1)S(1)}, bf16[1024,4096]{1,0:T(8,128)(2,1)}, u32[]{:S(2)}) %copy-start.1) | copy-done | bytes 8388632
  59.8 4.3 %gradient_term.1 = bf16[256,4096]{1,0:T(8,128)(2,1)S(1)} custom-call(bf16[256,1024]{1,0:T(8,128)(2,1)S(1)} %select_convert_fusion.1.space_ref, bf16[1024,4096]{1,0:T(8,128)(2,1)S(1)} %copy-done.1), custom_call_target="tpu_custom_call" | custom-call | flops 1000000 | bytes 10000 | tf_op jit(solution)/shard_map/gradient_term/pallas_call | solution.py:117
  64.1 1.3 copy-done.3
  65.5 15.2 %collective-permute-done.9.refs_2_ = bf16[2048,128]{1,0:T(8,128)(2,1)} collective-permute-done((bf16[2048,128]{1,0:T(8,128)(2,1)S(1)}, bf16[2048,128]{1,0:T(8,128)(2,1)}, u32[]{:S(2)}, u32[]{:S(2)}) %collective-permute-start.9) | collective-permute-done | bytes 524320 | tf_op jit(solution)/shard_map/ppermute | solution.py:230
  80.7 1.8 %collective-permute-done.7 = bf16[2048,128]{1,0:T(8,128)(2,1)S(1)} collective-permute-done((bf16[2048,128]{1,0:T(8,128)(2,1)S(1)}, bf16[2048,128]{1,0:T(8,128)(2,1)S(1)}, u32[]{:S(2)}, u32[]{:S(2)}) %collective-permute-start.7) | collective-permute-done | bytes 524320 | tf_op jit(solution)/shard_map/ppermute | solution.py:230
  82.4 0.9 broadcast_select_fusion.refs_0_
  83.3 6.4 %collective-permute-start.15 = (bf16[2048,128]{1,0:T(8,128)(2,1)}, bf16[2048,128]{1,0:T(8,128)(2,1)}, u32[]{:S(2)}, u32[]{:S(2)}) collective-permute-start(bf16[2048,128]{1,0:T(8,128)(2,1)} %broadcast_select_fusion.refs_0_), channel_id=1, source_target_pairs={{0,2},{2,0},{4,6},{6,4},{8,10},{10,8},{12,14},{14,12},{1,3},{3,1},... | collective-permute-start | bytes 1572872 | tf_op jit(solution)/shard_map/ppermute | solution.py:230
  90.3 0.8 copy-done.6
  91.1 1.5 collective-permute-start.14
  92.5 0.8 copy-done.17
  93.3 4.4 %all-to-all-start.3 = ((bf16[8,32,4096]{2,1,0:T(8,128)(2,1)}), bf16[8,32,4096]{2,1,0:T(8,128)(2,1)}, u32[]{:S(2)}, u32[]{:S(2)}) async-start(bf16[8,32,4096]{2,1,0:T(8,128)(2,1)} %bitcast.37), calls=%async_computation.3 | async-start | bytes 4194304 | tf_op jit(solution)/shard_map/all_to_all | solution.py:161
  97.7 11.1 %weight_product.3 = f32[1024,512]{1,0:T(8,128)} custom-call(s32[14]{0:T(128)} %stack.49.place_ref, bf16[1024,4096]{1,0:T(8,128)(2,1)} %tokens_ref.9, bf16[4096,128]{1,0:T(8,128)(2,1)} %refs_0_.1, bf16[2048,128]{1,0:T(8,128)(2,1)} %collective-permute-done.refs_1_, bf16[2048,128]{1,0:T(8,128)(2,1)} %collective-permute-done.12.refs_2_, ...), custom_call_target="tpu_custom_call" | custom-call | flops 4294967296 | bytes 8388608 | tf_op jit(solution)/shard_map/weight_product/pallas_call | solution.py:67
  108.9 4.2 %collective-permute-done.14.refs_3_ = bf16[2048,128]{1,0:T(8,128)(2,1)} collective-permute-done((bf16[2048,128]{1,0:T(8,128)(2,1)}, bf16[2048,128]{1,0:T(8,128)(2,1)}, u32[]{:S(2)}, u32[]{:S(2)}) %collective-permute-start.14) | collective-permute-done | bytes 524320 | tf_op jit(solution)/shard_map/ppermute | solution.py:233
  113.6 3.4 %copy-done.2 = bf16[1024,4096]{1,0:T(8,128)(2,1)S(1)} copy-done((bf16[1024,4096]{1,0:T(8,128)(2,1)S(1)}, bf16[1024,4096]{1,0:T(8,128)(2,1)}, u32[]{:S(2)}) %copy-start.2) | copy-done | bytes 8388632
  117.0 1.0 copy-done.5
  118.0 1.0 copy-done.7
  119.0 4.8 %weight_product.4 = f32[1024,256]{1,0:T(8,128)S(1)} custom-call(s32[8]{0:T(128)S(1)} %stack.52.place_ref, bf16[1024,4096]{1,0:T(8,128)(2,1)S(1)} %copy-done.2, bf16[2048,128]{1,0:T(8,128)(2,1)S(1)} %copy-done.5, bf16[2048,128]{1,0:T(8,128)(2,1)S(1)} %copy-done.7, bf16[2048,128]{1,0:T(8,128)(2,1)} %collective-permute-done.9.refs_2_, ...), custom_call_target="tpu_custom_call" | custom-call | flops 1000000 | bytes 10000 | tf_op jit(solution)/shard_map/weight_product/pallas_call | solution.py:67
  123.9 5.1 %weight_product.5 = f32[1024,256]{1,0:T(8,128)S(1)} custom-call(s32[8]{0:T(128)S(1)} %stack.52.place_ref, bf16[1024,4096]{1,0:T(8,128)(2,1)S(1)} %copy-done.2, bf16[2048,128]{1,0:T(8,128)(2,1)} %broadcast_select_fusion.refs_0_, bf16[2048,128]{1,0:T(8,128)(2,1)} %collective-permute-done.13.refs_1_, bf16[2048,128]{1,0:T(8,128)(2,1)} %collective-permute-done.15.refs_2_, ...), custom_call_target="tpu_custom_call" | custom-call | flops 1000000 | bytes 10000 | tf_op jit(solution)/shard_map/weight_product/pallas_call | solution.py:67
  129.6 3.1 %hidden_product.1 = f32[256,1024]{1,0:T(8,128)S(1)} custom-call(bf16[256,4096]{1,0:T(8,128)(2,1)S(1)} %bitcast.36, bf16[1024,4096]{1,0:T(8,128)(2,1)S(1)} %copy-done.2), custom_call_target="tpu_custom_call" | custom-call | flops 1000000 | bytes 10000 | tf_op jit(solution)/shard_map/hidden_product/pallas_call | solution.py:94
  133.3 2.3 %collective-permute-done.16 = f32[256,1024]{1,0:T(8,128)S(1)} collective-permute-done((f32[256,1024]{1,0:T(8,128)S(1)}, f32[256,1024]{1,0:T(8,128)S(1)}, u32[]{:S(2)}, u32[]{:S(2)}) %collective-permute-start.16) | collective-permute-done | bytes 1048608 | tf_op jit(solution)/shard_map/ppermute | solution.py:180
  135.9 1.1 fusion.1
  137.0 1.5 add_convert_fusion
  138.6 5.7 %all-to-all-done.3 = bf16[8,32,4096]{2,1,0:T(8,128)(2,1)} async-done(((bf16[8,32,4096]{2,1,0:T(8,128)(2,1)}), bf16[8,32,4096]{2,1,0:T(8,128)(2,1)}, u32[]{:S(2)}, u32[]{:S(2)}) %all-to-all-start.3) | async-done | bytes 2097184 | tf_op jit(solution)/shard_map/all_to_all | solution.py:161
  144.2 3.4 %all-to-all-start.4 = ((bf16[8,32,512]{2,1,0:T(8,128)(2,1)}), bf16[8,32,512]{2,1,0:T(8,128)(2,1)S(1)}, u32[]{:S(2)}, u32[]{:S(2)}) async-start(bf16[8,32,512]{2,1,0:T(8,128)(2,1)} %bitcast.20), calls=%async_computation.4 | async-start | bytes 524288 | tf_op jit(solution)/shard_map/all_to_all | solution.py:161
  147.7 3.2 %convolution_convert_fusion.1 = bf16[128,4096]{1,0:T(8,128)(2,1)} fusion(bf16[256,4096]{1,0:T(8,128)(2,1)} %bitcast.18, s32[128]{0:T(128)S(1)} %get-tuple-element.66, s32[128]{0:T(128)S(1)} %get-tuple-element.67, s32[256]{0:T(256)S(1)} %get-tuple-element.63, s32[256]{0:T(256)S(1)} %get-tuple-element.64, s32[128]{0:T(128)S(1)} %get-tuple-element.65, ...), kind=kOutput, calls=%fused_computation.1 | convolution fusion | flops 269156352 | bytes 3151360 | tf_op jit(solution)/shard_map/dot_general | solution.py:18
  150.9 5.8 %all-to-all-done.4 = bf16[8,32,512]{2,1,0:T(8,128)(2,1)S(1)} async-done(((bf16[8,32,512]{2,1,0:T(8,128)(2,1)}), bf16[8,32,512]{2,1,0:T(8,128)(2,1)S(1)}, u32[]{:S(2)}, u32[]{:S(2)}) %all-to-all-start.4) | async-done | bytes 262176 | tf_op jit(solution)/shard_map/all_to_all | solution.py:161
  156.7 1.1 convolution_convert_fusion.3
  (75 shorter events, 6.9 us)
Async XLA Ops:
  0.6 41.5 %copy-start = (bf16[4,32,4096]{2,1,0:T(8,128)(2,1)S(1)}, bf16[4,32,4096]{2,1,0:T(8,128)(2,1)}, u32[]{:S(2)}) copy-start(bf16[4,32,4096]{2,1,0:T(8,128)(2,1)} %param.9) | copy-start | bytes 3145732
  1.8 15.6 %collective-permute-start.2 = (bf16[2048,128]{1,0:T(8,128)(2,1)S(1)}, bf16[2048,128]{1,0:T(8,128)(2,1)S(1)}, u32[]{:S(2)}, u32[]{:S(2)}) collective-permute-start(bf16[2048,128]{1,0:T(8,128)(2,1)S(1)} %constant_dynamic-slice_fusion), channel_id=1, source_target_pairs={{4,8},{6,10},{8,4},{10,6},{5,9},{7,11},{9,5},{11,7},{20,24},{22,26... | collective-permute-start | bytes 1572872 | tf_op jit(solution)/shard_map/ppermute | solution.py:230
  2.5 17.7 %collective-permute-start.1 = (bf16[2048,128]{1,0:T(8,128)(2,1)S(1)}, bf16[2048,128]{1,0:T(8,128)(2,1)}, u32[]{:S(2)}, u32[]{:S(2)}) collective-permute-start(bf16[2048,128]{1,0:T(8,128)(2,1)S(1)} %constant_dynamic-slice_fusion), channel_id=1, source_target_pairs={{0,4},{2,6},{4,0},{6,2},{8,12},{10,14},{12,8},{14,10},{1,5},{3,7},... | collective-permute-start | bytes 1572872 | tf_op jit(solution)/shard_map/ppermute | solution.py:230
  8.4 24.0 %collective-permute-start = (bf16[2048,128]{1,0:T(8,128)(2,1)S(1)}, bf16[2048,128]{1,0:T(8,128)(2,1)}, u32[]{:S(2)}, u32[]{:S(2)}) collective-permute-start(bf16[2048,128]{1,0:T(8,128)(2,1)S(1)} %constant_dynamic-slice_fusion), channel_id=1, source_target_pairs={{0,2},{2,0},{4,6},{6,4},{8,10},{10,8},{12,14},{14,12},{1,3},{3,1},... | collective-permute-start | bytes 1572872 | tf_op jit(solution)/shard_map/ppermute | solution.py:230
  12.4 12.9 %all-to-all-start = ((s32[8,1,1]{2,1,0:T(1,128)}), s32[8,1,1]{2,1,0:T(1,128)S(1)}, u32[]{:S(2)}, u32[]{:S(2)}) async-start(s32[8,1,1]{2,1,0:T(1,128)} %copy.12), calls=%async_computation | async-start | bytes 8192 | tf_op jit(solution)/shard_map/all_to_all | solution.py:161
  17.4 26.8 %copy-start.10 = (bf16[2048,128]{1,0:T(8,128)(2,1)}, bf16[2048,128]{1,0:T(8,128)(2,1)S(1)}, u32[]{:S(2)}) copy-start(bf16[2048,128]{1,0:T(8,128)(2,1)S(1)} %collective-permute-done.2) | copy-start | bytes 1572868
  20.2 21.9 %collective-permute-start.5 = (bf16[2048,128]{1,0:T(8,128)(2,1)}, bf16[2048,128]{1,0:T(8,128)(2,1)S(1)}, u32[]{:S(2)}, u32[]{:S(2)}) collective-permute-start(bf16[2048,128]{1,0:T(8,128)(2,1)} %collective-permute-done.1.refs_3_), channel_id=1, source_target_pairs={{4,8},{6,10},{8,4},{10,6},{5,9},{7,11},{9,5},{11,7},{20,24},{22,26... | collective-permute-start | bytes 1572872 | tf_op jit(solution)/shard_map/ppermute | solution.py:230
  20.9 21.2 %collective-permute-start.4 = (bf16[2048,128]{1,0:T(8,128)(2,1)}, bf16[2048,128]{1,0:T(8,128)(2,1)}, u32[]{:S(2)}, u32[]{:S(2)}) collective-permute-start(bf16[2048,128]{1,0:T(8,128)(2,1)} %collective-permute-done.1.refs_3_), channel_id=1, source_target_pairs={{0,2},{2,0},{4,6},{6,4},{8,10},{10,8},{12,14},{14,12},{1,3},{3,1},... | collective-permute-start | bytes 1572872 | tf_op jit(solution)/shard_map/ppermute | solution.py:230
  22.5 19.6 %collective-permute-start.3 = (bf16[2048,128]{1,0:T(8,128)(2,1)}, bf16[2048,128]{1,0:T(8,128)(2,1)}, u32[]{:S(2)}, u32[]{:S(2)}) collective-permute-start(bf16[2048,128]{1,0:T(8,128)(2,1)} %collective-permute-done.1.refs_3_), channel_id=1, source_target_pairs={{0,16},{16,0},{1,17},{17,1},{2,18},{18,2},{3,19},{19,3},{4,20},{20... | collective-permute-start | bytes 1572872 | tf_op jit(solution)/shard_map/ppermute | solution.py:233
  24.0 18.1 %collective-permute-start.6 = (bf16[2048,128]{1,0:T(8,128)(2,1)S(1)}, bf16[2048,128]{1,0:T(8,128)(2,1)S(1)}, u32[]{:S(2)}, u32[]{:S(2)}) collective-permute-start(bf16[2048,128]{1,0:T(8,128)(2,1)S(1)} %collective-permute-done.2), channel_id=1, source_target_pairs={{4,0},{6,2},{8,12},{10,14},{5,1},{7,3},{9,13},{11,15},{20,16},{22,... | collective-permute-start | bytes 1572872 | tf_op jit(solution)/shard_map/ppermute | solution.py:230
  26.7 17.5 %all-to-all-start.1 = ((bf16[8,32,512]{2,1,0:T(8,128)(2,1)}), bf16[8,32,512]{2,1,0:T(8,128)(2,1)S(1)}, u32[]{:S(2)}, u32[]{:S(2)}) async-start(bf16[8,32,512]{2,1,0:T(8,128)(2,1)} %bitcast.42), calls=%async_computation.1 | async-start | bytes 524288 | tf_op jit(solution)/shard_map/all_to_all | solution.py:161
  42.1 2.2 %copy-start.14 = (bf16[2048,128]{1,0:T(8,128)(2,1)}, bf16[2048,128]{1,0:T(8,128)(2,1)S(1)}, u32[]{:S(2)}) copy-start(bf16[2048,128]{1,0:T(8,128)(2,1)S(1)} %collective-permute-done.6) | copy-start | bytes 1572868
  42.1 2.2 %copy-start.12 = (bf16[2048,128]{1,0:T(8,128)(2,1)}, bf16[2048,128]{1,0:T(8,128)(2,1)S(1)}, u32[]{:S(2)}) copy-start(bf16[2048,128]{1,0:T(8,128)(2,1)S(1)} %collective-permute-done.5) | copy-start | bytes 1572868
  44.3 49.1 %all-to-all-start.2 = ((bf16[8,32,4096]{2,1,0:T(8,128)(2,1)}), bf16[8,32,4096]{2,1,0:T(8,128)(2,1)S(1)}, u32[]{:S(2)}, u32[]{:S(2)}) async-start(bf16[8,32,4096]{2,1,0:T(8,128)(2,1)} %bitcast.38), calls=%async_computation.2 | async-start | bytes 4194304 | tf_op jit(solution)/shard_map/all_to_all | solution.py:161
  47.9 5.5 %copy-start.16 = (s32[1024]{0:T(1024)S(1)}, s32[1024]{0:T(1024)}, u32[]{:S(2)}) copy-start(s32[1024]{0:T(1024)} %param.12) | copy-start | bytes 12292
  48.0 2.0 %copy-start.11 = (bf16[2048,128]{1,0:T(8,128)(2,1)S(1)}, bf16[2048,128]{1,0:T(8,128)(2,1)}, u32[]{:S(2)}) copy-start(bf16[2048,128]{1,0:T(8,128)(2,1)} %copy-done.10) | copy-start | bytes 1572868
  48.0 2.0 %copy-start.15 = (bf16[2048,128]{1,0:T(8,128)(2,1)S(1)}, bf16[2048,128]{1,0:T(8,128)(2,1)}, u32[]{:S(2)}) copy-start(bf16[2048,128]{1,0:T(8,128)(2,1)} %copy-done.14) | copy-start | bytes 1572868
  48.0 4.1 %copy-start.13 = (bf16[2048,128]{1,0:T(8,128)(2,1)S(1)}, bf16[2048,128]{1,0:T(8,128)(2,1)}, u32[]{:S(2)}) copy-start(bf16[2048,128]{1,0:T(8,128)(2,1)} %copy-done.12) | copy-start | bytes 1572868
  49.8 5.7 %collective-permute-start.8 = (f32[256,1024]{1,0:T(8,128)S(1)}, f32[256,1024]{1,0:T(8,128)S(1)}, u32[]{:S(2)}, u32[]{:S(2)}) collective-permute-start(f32[256,1024]{1,0:T(8,128)S(1)} %fusion.11), channel_id=1, source_target_pairs={{0,1},{1,0},{2,3},{3,2},{4,5},{5,4},{6,7},{7,6},{8,9},{9,8},{10,11... | collective-permute-start | bytes 3145736 | tf_op jit(solution)/shard_map/ppermute | solution.py:180
  50.0 14.1 %copy-start.4 = (bf16[2048,128]{1,0:T(8,128)(2,1)}, bf16[2048,128]{1,0:T(8,128)(2,1)S(1)}, u32[]{:S(2)}) copy-start(bf16[2048,128]{1,0:T(8,128)(2,1)S(1)} %broadcast_select_fusion.1.refs_0_) | copy-start | bytes 1572868
  50.0 30.6 %collective-permute-start.9 = (bf16[2048,128]{1,0:T(8,128)(2,1)S(1)}, bf16[2048,128]{1,0:T(8,128)(2,1)}, u32[]{:S(2)}, u32[]{:S(2)}) collective-permute-start(bf16[2048,128]{1,0:T(8,128)(2,1)S(1)} %broadcast_select_fusion.1.refs_0_), channel_id=1, source_target_pairs={{0,2},{2,0},{4,6},{6,4},{8,10},{10,8},{12,14},{14,12},{1,3},{3,1},... | collective-permute-start | bytes 1572872 | tf_op jit(solution)/shard_map/ppermute | solution.py:230
  52.1 30.3 %collective-permute-start.7 = (bf16[2048,128]{1,0:T(8,128)(2,1)S(1)}, bf16[2048,128]{1,0:T(8,128)(2,1)S(1)}, u32[]{:S(2)}, u32[]{:S(2)}) collective-permute-start(bf16[2048,128]{1,0:T(8,128)(2,1)S(1)} %copy-done.13), channel_id=1, source_target_pairs={{4,0},{6,2},{8,12},{10,14},{5,1},{7,3},{9,13},{11,15},{20,16},{22,... | collective-permute-start | bytes 1572872 | tf_op jit(solution)/shard_map/ppermute | solution.py:230
  53.4 36.8 %collective-permute-start.10 = (bf16[2048,128]{1,0:T(8,128)(2,1)S(1)}, bf16[2048,128]{1,0:T(8,128)(2,1)S(1)}, u32[]{:S(2)}, u32[]{:S(2)}) collective-permute-start(bf16[2048,128]{1,0:T(8,128)(2,1)S(1)} %broadcast_select_fusion.1.refs_0_), channel_id=1, source_target_pairs={{0,16},{16,0},{1,17},{17,1},{2,18},{18,2},{3,19},{19,3},{4,20},{20... | collective-permute-start | bytes 1572872 | tf_op jit(solution)/shard_map/ppermute | solution.py:233
  54.0 38.5 %collective-permute-start.11 = (bf16[2048,128]{1,0:T(8,128)(2,1)}, bf16[2048,128]{1,0:T(8,128)(2,1)S(1)}, u32[]{:S(2)}, u32[]{:S(2)}) collective-permute-start(bf16[2048,128]{1,0:T(8,128)(2,1)} %collective-permute-done.4.refs_5_), channel_id=1, source_target_pairs={{0,16},{16,0},{1,17},{17,1},{2,18},{18,2},{3,19},{19,3},{4,20},{20... | collective-permute-start | bytes 1572872 | tf_op jit(solution)/shard_map/ppermute | solution.py:233
  55.5 37.8 %collective-permute-start.12 = (bf16[2048,128]{1,0:T(8,128)(2,1)}, bf16[2048,128]{1,0:T(8,128)(2,1)}, u32[]{:S(2)}, u32[]{:S(2)}) collective-permute-start(bf16[2048,128]{1,0:T(8,128)(2,1)} %collective-permute-done.refs_1_), channel_id=1, source_target_pairs={{0,16},{16,0},{1,17},{17,1},{2,18},{18,2},{3,19},{19,3},{4,20},{20... | collective-permute-start | bytes 1572872 | tf_op jit(solution)/shard_map/ppermute | solution.py:233
  56.4 3.4 %copy-start.1 = (bf16[1024,4096]{1,0:T(8,128)(2,1)S(1)}, bf16[1024,4096]{1,0:T(8,128)(2,1)}, u32[]{:S(2)}) copy-start(bf16[1024,4096]{1,0:T(8,128)(2,1)} %tokens_ref.9) | copy-start | bytes 25165828
  64.1 1.4 copy-start.3
  83.3 25.6 %collective-permute-start.15 = (bf16[2048,128]{1,0:T(8,128)(2,1)}, bf16[2048,128]{1,0:T(8,128)(2,1)}, u32[]{:S(2)}, u32[]{:S(2)}) collective-permute-start(bf16[2048,128]{1,0:T(8,128)(2,1)} %broadcast_select_fusion.refs_0_), channel_id=1, source_target_pairs={{0,2},{2,0},{4,6},{6,4},{8,10},{10,8},{12,14},{14,12},{1,3},{3,1},... | collective-permute-start | bytes 1572872 | tf_op jit(solution)/shard_map/ppermute | solution.py:230
  89.7 19.2 %collective-permute-start.13 = (bf16[2048,128]{1,0:T(8,128)(2,1)}, bf16[2048,128]{1,0:T(8,128)(2,1)}, u32[]{:S(2)}, u32[]{:S(2)}) collective-permute-start(bf16[2048,128]{1,0:T(8,128)(2,1)} %broadcast_select_fusion.refs_0_), channel_id=1, source_target_pairs={{0,16},{16,0},{1,17},{17,1},{2,18},{18,2},{3,19},{19,3},{4,20},{20... | collective-permute-start | bytes 1572872 | tf_op jit(solution)/shard_map/ppermute | solution.py:233
  90.3 0.8 copy-start.6
  91.1 22.0 %collective-permute-start.14 = (bf16[2048,128]{1,0:T(8,128)(2,1)}, bf16[2048,128]{1,0:T(8,128)(2,1)}, u32[]{:S(2)}, u32[]{:S(2)}) collective-permute-start(bf16[2048,128]{1,0:T(8,128)(2,1)} %collective-permute-done.9.refs_2_), channel_id=1, source_target_pairs={{0,16},{16,0},{1,17},{17,1},{2,18},{18,2},{3,19},{19,3},{4,20},{20... | collective-permute-start | bytes 1572872 | tf_op jit(solution)/shard_map/ppermute | solution.py:233
  92.5 0.8 copy-start.17
  93.3 50.9 %all-to-all-start.3 = ((bf16[8,32,4096]{2,1,0:T(8,128)(2,1)}), bf16[8,32,4096]{2,1,0:T(8,128)(2,1)}, u32[]{:S(2)}, u32[]{:S(2)}) async-start(bf16[8,32,4096]{2,1,0:T(8,128)(2,1)} %bitcast.37), calls=%async_computation.3 | async-start | bytes 4194304 | tf_op jit(solution)/shard_map/all_to_all | solution.py:161
  113.0 10.9 %collective-permute-start.17 = (bf16[2048,128]{1,0:T(8,128)(2,1)}, bf16[2048,128]{1,0:T(8,128)(2,1)}, u32[]{:S(2)}, u32[]{:S(2)}) collective-permute-start(bf16[2048,128]{1,0:T(8,128)(2,1)} %collective-permute-done.15.refs_2_), channel_id=1, source_target_pairs={{0,16},{16,0},{1,17},{17,1},{2,18},{18,2},{3,19},{19,3},{4,20},{20... | collective-permute-start | bytes 1572872 | tf_op jit(solution)/shard_map/ppermute | solution.py:233
  113.6 3.4 %copy-start.2 = (bf16[1024,4096]{1,0:T(8,128)(2,1)S(1)}, bf16[1024,4096]{1,0:T(8,128)(2,1)}, u32[]{:S(2)}) copy-start(bf16[1024,4096]{1,0:T(8,128)(2,1)} %tokens_ref.9) | copy-start | bytes 25165828
  117.0 1.0 copy-start.5
  118.0 1.0 copy-start.7
  123.9 5.1 %copy-start.8 = (f32[1024,512]{1,0:T(8,128)S(1)}, f32[1024,512]{1,0:T(8,128)}, u32[]{:S(2)}) copy-start(f32[1024,512]{1,0:T(8,128)} %weight_product.3) | copy-start | bytes 6291460
  129.5 7.5 %collective-permute-start.18 = (f32[1024,512]{1,0:T(8,128)S(1)}, f32[1024,512]{1,0:T(8,128)S(1)}, u32[]{:S(2)}, u32[]{:S(2)}) collective-permute-start(f32[1024,512]{1,0:T(8,128)S(1)} %fusion), channel_id=1, source_target_pairs={{0,1},{1,0},{2,3},{3,2},{4,5},{5,4},{6,7},{7,6},{8,9},{9,8},{10,11... | collective-permute-start | bytes 6291464 | tf_op jit(solution)/shard_map/ppermute | solution.py:329
  132.7 3.1 %copy-start.9 = (bf16[1024,512]{1,0:T(8,128)(2,1)S(1)}, bf16[1024,512]{1,0:T(8,128)(2,1)}, u32[]{:S(2)}) copy-start(bf16[1024,512]{1,0:T(8,128)(2,1)} %param.11) | copy-start | bytes 3145732
  132.8 2.8 %collective-permute-start.16 = (f32[256,1024]{1,0:T(8,128)S(1)}, f32[256,1024]{1,0:T(8,128)S(1)}, u32[]{:S(2)}, u32[]{:S(2)}) collective-permute-start(f32[256,1024]{1,0:T(8,128)S(1)} %hidden_product.1), channel_id=1, source_target_pairs={{0,1},{1,0},{2,3},{3,2},{4,5},{5,4},{6,7},{7,6},{8,9},{9,8},{10,11... | collective-permute-start | bytes 3145736 | tf_op jit(solution)/shard_map/ppermute | solution.py:180
  144.2 12.5 %all-to-all-start.4 = ((bf16[8,32,512]{2,1,0:T(8,128)(2,1)}), bf16[8,32,512]{2,1,0:T(8,128)(2,1)S(1)}, u32[]{:S(2)}, u32[]{:S(2)}) async-start(bf16[8,32,512]{2,1,0:T(8,128)(2,1)} %bitcast.20), calls=%async_computation.4 | async-start | bytes 524288 | tf_op jit(solution)/shard_map/all_to_all | solution.py:161

commit v7 on v6

--- a/solution.py
+++ b/solution.py
@@ -275,11 +275,11 @@
     own_across_rest = twin(own_across)
     backward_pass = work.rank_space(dot(got_b, cotangent, ((1,), (1,))))
     home_a = gradient_term(backward_pass, tokens)
-    end_far, home_a, following_across = barrier((end_far, home_a, following_across))
+    end_far, home_a, following_across, following_rest = barrier(
+        (end_far, home_a, following_across, following_rest)
+    )
     far = jnp.where(inner, mid_far, end_far)
-    got_a, home_a, following_rest, near_across_rest, own_across_rest = barrier(
-        (got_a, home_a, following_rest, near_across_rest, own_across_rest)
-    )
+    got_a, home_a = barrier((got_a, home_a))
     came_a = work.exchange(home_a)
     far_across = over(far, across)
     far_rest = twin(far)

time: 159 us -> 159 us (level)
  local copies, waits for them, and re-layouts: 16.3 us -> 14.7 us
    ppermute x7, waiting for transfers between devices: 4.17 us -> 0.02 us  [twin(): return lax.ppermute(part, 'groups', SWAP)]
    all_to_all x5, waiting for transfers between devices: 11.5 us -> 14.5 us  [exchange(): lax.all_to_all(sent.reshape(self.peers, -1, sent.shape[1]), 'dp', split_a...]
    ppermute x9, waiting for transfers between devices: 29.4 us -> 31.9 us  [over(): return lax.ppermute(part, 'dp', pairs)]
    unnamed x36 -> x34, local copies, waits for them, and re-layouts: 11.8 us -> 10.3 us
  transfers between devices with their start and end apart: 24 -> 24, of which waited for: 8 -> 9; matrix products, arithmetic and copies ran while one was open for 11% -> 11% of each run, Pallas kernels for 18% -> 18%
where the time goes in v7:
time: 159 us; the launch traced here: 158 us
  starting transfers between devices  49.6 us (31%)
  waiting for transfers between devices  48.7 us (31%)
  Pallas kernels  28.5 us (18%)
  local copies, waits for them, and re-layouts  14.7 us (9%)
  matrix products  11.9 us (7%)
  other arithmetic  3.23 us (2%)
    ppermute x9, waiting for transfers between devices, over(): return lax.ppermute(part, 'dp', pairs)  31.9 us
    ppermute x9, starting transfers between devices, over(): return lax.ppermute(part, 'dp', pairs)  21.3 us
    pallas_call x3, Pallas kernels, product(): pl.pallas_call(functools.partial(product_kernel, len(pieces)), out_shape=...  21.1 us
    all_to_all x5, starting transfers between devices, exchange(): lax.all_to_all(sent.reshape(self.peers, -1, sent.shape[1]), 'dp', split_a...  20.7 us
    all_to_all x5, waiting for transfers between devices, exchange(): lax.all_to_all(sent.reshape(self.peers, -1, sent.shape[1]), 'dp', split_a...  14.5 us
    dot_general x7, matrix products, dot(): lax.dot_general(left, right, ((contract[0], contract[1]), ((), ())), pref...  11.9 us
    unnamed x34, local copies, waits for them, and re-layouts  10.3 us
    ppermute x7, starting transfers between devices, twin(): return lax.ppermute(part, 'groups', SWAP)  6.91 us
  transfers between devices with their start and end apart: 24, of which 9 were waited for; matrix products, arithmetic and copies ran while one was open for 11% of the time, Pallas kernels for 18%

profile of v7, /device:TPU:0, one launch (start us, length us, event | category | flops | bytes accessed | tf_op | source)
XLA Modules:
  0.0 157.8 jit_solution(1086276484075577463)
XLA Ops:
  0.7 1.2 constant_dynamic-slice_fusion
  1.8 0.7 collective-permute-start.2
  2.5 5.9 %collective-permute-start.1 = (bf16[2048,128]{1,0:T(8,128)(2,1)S(1)}, bf16[2048,128]{1,0:T(8,128)(2,1)}, u32[]{:S(2)}, u32[]{:S(2)}) collective-permute-start(bf16[2048,128]{1,0:T(8,128)(2,1)S(1)} %constant_dynamic-slice_fusion), channel_id=1, source_target_pairs={{0,4},{2,6},{4,0},{6,2},{8,12},{10,14},{12,8},{14,10},{1,5},{3,7},... | collective-permute-start | bytes 1572872 | tf_op jit(solution)/shard_map/ppermute | solution.py:230
  8.4 1.5 collective-permute-start
  9.9 0.8 slice_reduce_fusion
  10.7 0.8 select_reduce_fusion.1
  12.4 3.3 %all-to-all-start = ((s32[8,1,1]{2,1,0:T(1,128)}), s32[8,1,1]{2,1,0:T(1,128)S(1)}, u32[]{:S(2)}, u32[]{:S(2)}) async-start(s32[8,1,1]{2,1,0:T(1,128)} %copy.12), calls=%async_computation | async-start | bytes 8192 | tf_op jit(solution)/shard_map/all_to_all | solution.py:161
  16.4 0.9 constant_dynamic-slice_fusion.1
  17.3 2.8 %collective-permute-done.1.refs_3_ = bf16[2048,128]{1,0:T(8,128)(2,1)} collective-permute-done((bf16[2048,128]{1,0:T(8,128)(2,1)S(1)}, bf16[2048,128]{1,0:T(8,128)(2,1)}, u32[]{:S(2)}, u32[]{:S(2)}) %collective-permute-start.1) | collective-permute-done | bytes 524320 | tf_op jit(solution)/shard_map/ppermute | solution.py:230
  20.2 0.7 collective-permute-start.5
  20.9 1.6 %collective-permute-start.4 = (bf16[2048,128]{1,0:T(8,128)(2,1)}, bf16[2048,128]{1,0:T(8,128)(2,1)}, u32[]{:S(2)}, u32[]{:S(2)}) collective-permute-start(bf16[2048,128]{1,0:T(8,128)(2,1)} %collective-permute-done.1.refs_3_), channel_id=1, source_target_pairs={{0,2},{2,0},{4,6},{6,4},{8,10},{10,8},{12,14},{14,12},{1,3},{3,1},... | collective-permute-start | bytes 1572872 | tf_op jit(solution)/shard_map/ppermute | solution.py:230
  22.5 1.5 collective-permute-start.3
  24.0 1.3 collective-permute-start.6
  25.7 1.1 convolution_convert_fusion.2
  26.7 5.7 %all-to-all-start.1 = ((bf16[8,32,512]{2,1,0:T(8,128)(2,1)}), bf16[8,32,512]{2,1,0:T(8,128)(2,1)S(1)}, u32[]{:S(2)}, u32[]{:S(2)}) async-start(bf16[8,32,512]{2,1,0:T(8,128)(2,1)} %bitcast.42), calls=%async_computation.1 | async-start | bytes 524288 | tf_op jit(solution)/shard_map/all_to_all | solution.py:161
  32.4 9.6 %collective-permute-done.6 = bf16[2048,128]{1,0:T(8,128)(2,1)S(1)} collective-permute-done((bf16[2048,128]{1,0:T(8,128)(2,1)S(1)}, bf16[2048,128]{1,0:T(8,128)(2,1)S(1)}, u32[]{:S(2)}, u32[]{:S(2)}) %collective-permute-start.6) | collective-permute-done | bytes 524320 | tf_op jit(solution)/shard_map/ppermute | solution.py:230
  42.1 2.1 %convolution_convert_fusion = bf16[256,4096]{1,0:T(8,128)(2,1)} fusion(bf16[128,4096]{1,0:T(8,128)(2,1)S(1)} %bitcast.35, s32[128]{0:T(128)S(1)} %get-tuple-element.62, s32[128]{0:T(128)S(1)} %get-tuple-element.63, s32[256]{0:T(256)S(1)} %get-tuple-element.59, s32[256]{0:T(256)S(1)} %get-tuple-element.60, s32[128]{0:T(128)S(1)} %get-tuple-element.61, ...), kind=kOutput, calls=%fused_computation | convolution fusion | flops 269680640 | bytes 3151360 | tf_op jit(solution)/shard_map/dot_general | solution.py:18
  44.3 3.7 %all-to-all-start.2 = ((bf16[8,32,4096]{2,1,0:T(8,128)(2,1)}), bf16[8,32,4096]{2,1,0:T(8,128)(2,1)S(1)}, u32[]{:S(2)}, u32[]{:S(2)}) async-start(bf16[8,32,4096]{2,1,0:T(8,128)(2,1)} %bitcast.38), calls=%async_computation.2 | async-start | bytes 4194304 | tf_op jit(solution)/shard_map/all_to_all | solution.py:161
  48.0 1.8 %fusion.11 = f32[256,1024]{1,0:T(8,128)S(1)} fusion(bf16[256,512]{1,0:T(8,128)(2,1)S(1)} %bitcast.39, bf16[1024,512]{1,0:T(8,128)(2,1)} %param.11), kind=kOutput, calls=%fused_computation.49 | convolution fusion | flops 268435456 | bytes 2359296 | tf_op jit(solution)/shard_map/dot_general | solution.py:18
  50.6 2.0 %collective-permute-start.9 = (bf16[2048,128]{1,0:T(8,128)(2,1)S(1)}, bf16[2048,128]{1,0:T(8,128)(2,1)}, u32[]{:S(2)}, u32[]{:S(2)}) collective-permute-start(bf16[2048,128]{1,0:T(8,128)(2,1)S(1)} %broadcast_select_fusion.1.refs_0_), channel_id=1, source_target_pairs={{0,2},{2,0},{4,6},{6,4},{8,10},{10,8},{12,14},{14,12},{1,3},{3,1},... | collective-permute-start | bytes 1572872 | tf_op jit(solution)/shard_map/ppermute | solution.py:230
  52.6 1.3 collective-permute-start.7
  54.0 1.6 collective-permute-start.11
  56.4 3.4 %copy-done.1 = bf16[1024,4096]{1,0:T(8,128)(2,1)S(1)} copy-done((bf16[1024,4096]{1,0:T(8,128)(2,1)S(1)}, bf16[1024,4096]{1,0:T(8,128)(2,1)}, u32[]{:S(2)}) %copy-start.1) | copy-done | bytes 8388632
  59.8 4.3 %gradient_term.1 = bf16[256,4096]{1,0:T(8,128)(2,1)S(1)} custom-call(bf16[256,1024]{1,0:T(8,128)(2,1)S(1)} %select_convert_fusion.1.space_ref, bf16[1024,4096]{1,0:T(8,128)(2,1)S(1)} %copy-done.1), custom_call_target="tpu_custom_call" | custom-call | flops 1000000 | bytes 10000 | tf_op jit(solution)/shard_map/gradient_term/pallas_call | solution.py:117
  64.1 1.3 copy-done.3
  65.5 15.2 %collective-permute-done.9.refs_2_ = bf16[2048,128]{1,0:T(8,128)(2,1)} collective-permute-done((bf16[2048,128]{1,0:T(8,128)(2,1)S(1)}, bf16[2048,128]{1,0:T(8,128)(2,1)}, u32[]{:S(2)}, u32[]{:S(2)}) %collective-permute-start.9) | collective-permute-done | bytes 524320 | tf_op jit(solution)/shard_map/ppermute | solution.py:230
  80.7 1.8 %collective-permute-done.7 = bf16[2048,128]{1,0:T(8,128)(2,1)S(1)} collective-permute-done((bf16[2048,128]{1,0:T(8,128)(2,1)S(1)}, bf16[2048,128]{1,0:T(8,128)(2,1)S(1)}, u32[]{:S(2)}, u32[]{:S(2)}) %collective-permute-start.7) | collective-permute-done | bytes 524320 | tf_op jit(solution)/shard_map/ppermute | solution.py:230
  82.4 0.9 broadcast_select_fusion.refs_0_
  83.3 6.4 %collective-permute-start.15 = (bf16[2048,128]{1,0:T(8,128)(2,1)}, bf16[2048,128]{1,0:T(8,128)(2,1)}, u32[]{:S(2)}, u32[]{:S(2)}) collective-permute-start(bf16[2048,128]{1,0:T(8,128)(2,1)} %broadcast_select_fusion.refs_0_), channel_id=1, source_target_pairs={{0,2},{2,0},{4,6},{6,4},{8,10},{10,8},{12,14},{14,12},{1,3},{3,1},... | collective-permute-start | bytes 1572872 | tf_op jit(solution)/shard_map/ppermute | solution.py:230
  90.3 1.5 collective-permute-start.14
  92.1 4.3 %all-to-all-start.3 = ((bf16[8,32,4096]{2,1,0:T(8,128)(2,1)}), bf16[8,32,4096]{2,1,0:T(8,128)(2,1)}, u32[]{:S(2)}, u32[]{:S(2)}) async-start(bf16[8,32,4096]{2,1,0:T(8,128)(2,1)} %bitcast.37), calls=%async_computation.3 | async-start | bytes 4194304 | tf_op jit(solution)/shard_map/all_to_all | solution.py:161
  96.5 11.1 %weight_product.3 = f32[1024,512]{1,0:T(8,128)} custom-call(s32[14]{0:T(128)} %stack.49.place_ref, bf16[1024,4096]{1,0:T(8,128)(2,1)} %tokens_ref.9, bf16[4096,128]{1,0:T(8,128)(2,1)} %refs_0_.1, bf16[2048,128]{1,0:T(8,128)(2,1)} %collective-permute-done.refs_1_, bf16[2048,128]{1,0:T(8,128)(2,1)} %collective-permute-done.11.refs_2_, ...), custom_call_target="tpu_custom_call" | custom-call | flops 4294967296 | bytes 8388608 | tf_op jit(solution)/shard_map/weight_product/pallas_call | solution.py:67
  107.6 2.5 %collective-permute-done.15.refs_2_ = bf16[2048,128]{1,0:T(8,128)(2,1)} collective-permute-done((bf16[2048,128]{1,0:T(8,128)(2,1)}, bf16[2048,128]{1,0:T(8,128)(2,1)}, u32[]{:S(2)}, u32[]{:S(2)}) %collective-permute-start.15) | collective-permute-done | bytes 524320 | tf_op jit(solution)/shard_map/ppermute | solution.py:230
  110.2 0.7 collective-permute-start.17
  110.9 3.4 %copy-done.2 = bf16[1024,4096]{1,0:T(8,128)(2,1)S(1)} copy-done((bf16[1024,4096]{1,0:T(8,128)(2,1)S(1)}, bf16[1024,4096]{1,0:T(8,128)(2,1)}, u32[]{:S(2)}) %copy-start.2) | copy-done | bytes 8388632
  114.2 1.0 copy-done.5
  115.3 1.0 copy-done.7
  116.3 4.8 %weight_product.4 = f32[1024,256]{1,0:T(8,128)S(1)} custom-call(s32[8]{0:T(128)S(1)} %stack.52.place_ref, bf16[1024,4096]{1,0:T(8,128)(2,1)S(1)} %copy-done.2, bf16[2048,128]{1,0:T(8,128)(2,1)S(1)} %copy-done.5, bf16[2048,128]{1,0:T(8,128)(2,1)S(1)} %copy-done.7, bf16[2048,128]{1,0:T(8,128)(2,1)} %collective-permute-done.9.refs_2_, ...), custom_call_target="tpu_custom_call" | custom-call | flops 1000000 | bytes 10000 | tf_op jit(solution)/shard_map/weight_product/pallas_call | solution.py:67
  121.2 5.1 %weight_product.5 = f32[1024,256]{1,0:T(8,128)S(1)} custom-call(s32[8]{0:T(128)S(1)} %stack.52.place_ref, bf16[1024,4096]{1,0:T(8,128)(2,1)S(1)} %copy-done.2, bf16[2048,128]{1,0:T(8,128)(2,1)} %broadcast_select_fusion.refs_0_, bf16[2048,128]{1,0:T(8,128)(2,1)} %collective-permute-done.13.refs_1_, bf16[2048,128]{1,0:T(8,128)(2,1)} %collective-permute-done.15.refs_2_, ...), custom_call_target="tpu_custom_call" | custom-call | flops 1000000 | bytes 10000 | tf_op jit(solution)/shard_map/weight_product/pallas_call | solution.py:67
  126.9 3.1 %hidden_product.1 = f32[256,1024]{1,0:T(8,128)S(1)} custom-call(bf16[256,4096]{1,0:T(8,128)(2,1)S(1)} %bitcast.36, bf16[1024,4096]{1,0:T(8,128)(2,1)S(1)} %copy-done.2), custom_call_target="tpu_custom_call" | custom-call | flops 1000000 | bytes 10000 | tf_op jit(solution)/shard_map/hidden_product/pallas_call | solution.py:94
  130.6 2.3 %collective-permute-done.16 = f32[256,1024]{1,0:T(8,128)S(1)} collective-permute-done((f32[256,1024]{1,0:T(8,128)S(1)}, f32[256,1024]{1,0:T(8,128)S(1)}, u32[]{:S(2)}, u32[]{:S(2)}) %collective-permute-start.16) | collective-permute-done | bytes 1048608 | tf_op jit(solution)/shard_map/ppermute | solution.py:180
  133.2 1.2 fusion.1
  134.3 1.5 add_convert_fusion
  135.8 8.2 %all-to-all-done.3 = bf16[8,32,4096]{2,1,0:T(8,128)(2,1)} async-done(((bf16[8,32,4096]{2,1,0:T(8,128)(2,1)}), bf16[8,32,4096]{2,1,0:T(8,128)(2,1)}, u32[]{:S(2)}, u32[]{:S(2)}) %all-to-all-start.3) | async-done | bytes 2097184 | tf_op jit(solution)/shard_map/all_to_all | solution.py:161
  144.0 3.6 %all-to-all-start.4 = ((bf16[8,32,512]{2,1,0:T(8,128)(2,1)}), bf16[8,32,512]{2,1,0:T(8,128)(2,1)S(1)}, u32[]{:S(2)}, u32[]{:S(2)}) async-start(bf16[8,32,512]{2,1,0:T(8,128)(2,1)} %bitcast.20), calls=%async_computation.4 | async-start | bytes 524288 | tf_op jit(solution)/shard_map/all_to_all | solution.py:161
  147.7 3.2 %convolution_convert_fusion.1 = bf16[128,4096]{1,0:T(8,128)(2,1)} fusion(bf16[256,4096]{1,0:T(8,128)(2,1)} %bitcast.18, s32[128]{0:T(128)S(1)} %get-tuple-element.62, s32[128]{0:T(128)S(1)} %get-tuple-element.63, s32[256]{0:T(256)S(1)} %get-tuple-element.59, s32[256]{0:T(256)S(1)} %get-tuple-element.60, s32[128]{0:T(128)S(1)} %get-tuple-element.61, ...), kind=kOutput, calls=%fused_computation.1 | convolution fusion | flops 269156352 | bytes 3151360 | tf_op jit(solution)/shard_map/dot_general | solution.py:18
  150.9 5.9 %all-to-all-done.4 = bf16[8,32,512]{2,1,0:T(8,128)(2,1)S(1)} async-done(((bf16[8,32,512]{2,1,0:T(8,128)(2,1)}), bf16[8,32,512]{2,1,0:T(8,128)(2,1)S(1)}, u32[]{:S(2)}, u32[]{:S(2)}) %all-to-all-start.4) | async-done | bytes 262176 | tf_op jit(solution)/shard_map/all_to_all | solution.py:161
  156.8 1.1 convolution_convert_fusion.3
  (73 shorter events, 6.0 us)
Async XLA Ops:
  0.6 41.5 %copy-start = (bf16[4,32,4096]{2,1,0:T(8,128)(2,1)S(1)}, bf16[4,32,4096]{2,1,0:T(8,128)(2,1)}, u32[]{:S(2)}) copy-start(bf16[4,32,4096]{2,1,0:T(8,128)(2,1)} %param.9) | copy-start | bytes 3145732
  1.8 15.5 %collective-permute-start.2 = (bf16[2048,128]{1,0:T(8,128)(2,1)S(1)}, bf16[2048,128]{1,0:T(8,128)(2,1)S(1)}, u32[]{:S(2)}, u32[]{:S(2)}) collective-permute-start(bf16[2048,128]{1,0:T(8,128)(2,1)S(1)} %constant_dynamic-slice_fusion), channel_id=1, source_target_pairs={{4,8},{6,10},{8,4},{10,6},{5,9},{7,11},{9,5},{11,7},{20,24},{22,26... | collective-permute-start | bytes 1572872 | tf_op jit(solution)/shard_map/ppermute | solution.py:230
  2.5 17.7 %collective-permute-start.1 = (bf16[2048,128]{1,0:T(8,128)(2,1)S(1)}, bf16[2048,128]{1,0:T(8,128)(2,1)}, u32[]{:S(2)}, u32[]{:S(2)}) collective-permute-start(bf16[2048,128]{1,0:T(8,128)(2,1)S(1)} %constant_dynamic-slice_fusion), channel_id=1, source_target_pairs={{0,4},{2,6},{4,0},{6,2},{8,12},{10,14},{12,8},{14,10},{1,5},{3,7},... | collective-permute-start | bytes 1572872 | tf_op jit(solution)/shard_map/ppermute | solution.py:230
  8.4 24.0 %collective-permute-start = (bf16[2048,128]{1,0:T(8,128)(2,1)S(1)}, bf16[2048,128]{1,0:T(8,128)(2,1)}, u32[]{:S(2)}, u32[]{:S(2)}) collective-permute-start(bf16[2048,128]{1,0:T(8,128)(2,1)S(1)} %constant_dynamic-slice_fusion), channel_id=1, source_target_pairs={{0,2},{2,0},{4,6},{6,4},{8,10},{10,8},{12,14},{14,12},{1,3},{3,1},... | collective-permute-start | bytes 1572872 | tf_op jit(solution)/shard_map/ppermute | solution.py:230
  12.4 12.9 %all-to-all-start = ((s32[8,1,1]{2,1,0:T(1,128)}), s32[8,1,1]{2,1,0:T(1,128)S(1)}, u32[]{:S(2)}, u32[]{:S(2)}) async-start(s32[8,1,1]{2,1,0:T(1,128)} %copy.12), calls=%async_computation | async-start | bytes 8192 | tf_op jit(solution)/shard_map/all_to_all | solution.py:161
  17.3 26.9 %copy-start.10 = (bf16[2048,128]{1,0:T(8,128)(2,1)}, bf16[2048,128]{1,0:T(8,128)(2,1)S(1)}, u32[]{:S(2)}) copy-start(bf16[2048,128]{1,0:T(8,128)(2,1)S(1)} %collective-permute-done.2) | copy-start | bytes 1572868
  20.2 21.9 %collective-permute-start.5 = (bf16[2048,128]{1,0:T(8,128)(2,1)}, bf16[2048,128]{1,0:T(8,128)(2,1)S(1)}, u32[]{:S(2)}, u32[]{:S(2)}) collective-permute-start(bf16[2048,128]{1,0:T(8,128)(2,1)} %collective-permute-done.1.refs_3_), channel_id=1, source_target_pairs={{4,8},{6,10},{8,4},{10,6},{5,9},{7,11},{9,5},{11,7},{20,24},{22,26... | collective-permute-start | bytes 1572872 | tf_op jit(solution)/shard_map/ppermute | solution.py:230
  20.9 21.2 %collective-permute-start.4 = (bf16[2048,128]{1,0:T(8,128)(2,1)}, bf16[2048,128]{1,0:T(8,128)(2,1)}, u32[]{:S(2)}, u32[]{:S(2)}) collective-permute-start(bf16[2048,128]{1,0:T(8,128)(2,1)} %collective-permute-done.1.refs_3_), channel_id=1, source_target_pairs={{0,2},{2,0},{4,6},{6,4},{8,10},{10,8},{12,14},{14,12},{1,3},{3,1},... | collective-permute-start | bytes 1572872 | tf_op jit(solution)/shard_map/ppermute | solution.py:230
  22.5 19.6 %collective-permute-start.3 = (bf16[2048,128]{1,0:T(8,128)(2,1)}, bf16[2048,128]{1,0:T(8,128)(2,1)}, u32[]{:S(2)}, u32[]{:S(2)}) collective-permute-start(bf16[2048,128]{1,0:T(8,128)(2,1)} %collective-permute-done.1.refs_3_), channel_id=1, source_target_pairs={{0,16},{16,0},{1,17},{17,1},{2,18},{18,2},{3,19},{19,3},{4,20},{20... | collective-permute-start | bytes 1572872 | tf_op jit(solution)/shard_map/ppermute | solution.py:233
  24.0 18.1 %collective-permute-start.6 = (bf16[2048,128]{1,0:T(8,128)(2,1)S(1)}, bf16[2048,128]{1,0:T(8,128)(2,1)S(1)}, u32[]{:S(2)}, u32[]{:S(2)}) collective-permute-start(bf16[2048,128]{1,0:T(8,128)(2,1)S(1)} %collective-permute-done.2), channel_id=1, source_target_pairs={{4,0},{6,2},{8,12},{10,14},{5,1},{7,3},{9,13},{11,15},{20,16},{22,... | collective-permute-start | bytes 1572872 | tf_op jit(solution)/shard_map/ppermute | solution.py:230
  26.7 17.5 %all-to-all-start.1 = ((bf16[8,32,512]{2,1,0:T(8,128)(2,1)}), bf16[8,32,512]{2,1,0:T(8,128)(2,1)S(1)}, u32[]{:S(2)}, u32[]{:S(2)}) async-start(bf16[8,32,512]{2,1,0:T(8,128)(2,1)} %bitcast.42), calls=%async_computation.1 | async-start | bytes 524288 | tf_op jit(solution)/shard_map/all_to_all | solution.py:161
  42.1 2.2 %copy-start.14 = (bf16[2048,128]{1,0:T(8,128)(2,1)}, bf16[2048,128]{1,0:T(8,128)(2,1)S(1)}, u32[]{:S(2)}) copy-start(bf16[2048,128]{1,0:T(8,128)(2,1)S(1)} %collective-permute-done.6) | copy-start | bytes 1572868
  42.1 2.2 %copy-start.12 = (bf16[2048,128]{1,0:T(8,128)(2,1)}, bf16[2048,128]{1,0:T(8,128)(2,1)S(1)}, u32[]{:S(2)}) copy-start(bf16[2048,128]{1,0:T(8,128)(2,1)S(1)} %collective-permute-done.5) | copy-start | bytes 1572868
  44.3 47.9 %all-to-all-start.2 = ((bf16[8,32,4096]{2,1,0:T(8,128)(2,1)}), bf16[8,32,4096]{2,1,0:T(8,128)(2,1)S(1)}, u32[]{:S(2)}, u32[]{:S(2)}) async-start(bf16[8,32,4096]{2,1,0:T(8,128)(2,1)} %bitcast.38), calls=%async_computation.2 | async-start | bytes 4194304 | tf_op jit(solution)/shard_map/all_to_all | solution.py:161
  48.0 6.0 %copy-start.16 = (s32[1024]{0:T(1024)S(1)}, s32[1024]{0:T(1024)}, u32[]{:S(2)}) copy-start(s32[1024]{0:T(1024)} %param.12) | copy-start | bytes 12292
  48.0 2.0 %copy-start.11 = (bf16[2048,128]{1,0:T(8,128)(2,1)S(1)}, bf16[2048,128]{1,0:T(8,128)(2,1)}, u32[]{:S(2)}) copy-start(bf16[2048,128]{1,0:T(8,128)(2,1)} %copy-done.10) | copy-start | bytes 1572868
  48.0 2.0 %copy-start.15 = (bf16[2048,128]{1,0:T(8,128)(2,1)S(1)}, bf16[2048,128]{1,0:T(8,128)(2,1)}, u32[]{:S(2)}) copy-start(bf16[2048,128]{1,0:T(8,128)(2,1)} %copy-done.14) | copy-start | bytes 1572868
  48.0 4.7 %copy-start.13 = (bf16[2048,128]{1,0:T(8,128)(2,1)S(1)}, bf16[2048,128]{1,0:T(8,128)(2,1)}, u32[]{:S(2)}) copy-start(bf16[2048,128]{1,0:T(8,128)(2,1)} %copy-done.12) | copy-start | bytes 1572868
  49.8 5.7 %collective-permute-start.8 = (f32[256,1024]{1,0:T(8,128)S(1)}, f32[256,1024]{1,0:T(8,128)S(1)}, u32[]{:S(2)}, u32[]{:S(2)}) collective-permute-start(f32[256,1024]{1,0:T(8,128)S(1)} %fusion.11), channel_id=1, source_target_pairs={{0,1},{1,0},{2,3},{3,2},{4,5},{5,4},{6,7},{7,6},{8,9},{9,8},{10,11... | collective-permute-start | bytes 3145736 | tf_op jit(solution)/shard_map/ppermute | solution.py:180
  50.0 14.1 %copy-start.4 = (bf16[2048,128]{1,0:T(8,128)(2,1)}, bf16[2048,128]{1,0:T(8,128)(2,1)S(1)}, u32[]{:S(2)}) copy-start(bf16[2048,128]{1,0:T(8,128)(2,1)S(1)} %broadcast_select_fusion.1.refs_0_) | copy-start | bytes 1572868
  50.0 15.4 %collective-permute-start.10 = (bf16[2048,128]{1,0:T(8,128)(2,1)S(1)}, bf16[2048,128]{1,0:T(8,128)(2,1)S(1)}, u32[]{:S(2)}, u32[]{:S(2)}) collective-permute-start(bf16[2048,128]{1,0:T(8,128)(2,1)S(1)} %broadcast_select_fusion.1.refs_0_), channel_id=1, source_target_pairs={{0,16},{16,0},{1,17},{17,1},{2,18},{18,2},{3,19},{19,3},{4,20},{20... | collective-permute-start | bytes 1572872 | tf_op jit(solution)/shard_map/ppermute | solution.py:233
  50.6 30.0 %collective-permute-start.9 = (bf16[2048,128]{1,0:T(8,128)(2,1)S(1)}, bf16[2048,128]{1,0:T(8,128)(2,1)}, u32[]{:S(2)}, u32[]{:S(2)}) collective-permute-start(bf16[2048,128]{1,0:T(8,128)(2,1)S(1)} %broadcast_select_fusion.1.refs_0_), channel_id=1, source_target_pairs={{0,2},{2,0},{4,6},{6,4},{8,10},{10,8},{12,14},{14,12},{1,3},{3,1},... | collective-permute-start | bytes 1572872 | tf_op jit(solution)/shard_map/ppermute | solution.py:230
  52.6 29.8 %collective-permute-start.7 = (bf16[2048,128]{1,0:T(8,128)(2,1)S(1)}, bf16[2048,128]{1,0:T(8,128)(2,1)S(1)}, u32[]{:S(2)}, u32[]{:S(2)}) collective-permute-start(bf16[2048,128]{1,0:T(8,128)(2,1)S(1)} %copy-done.13), channel_id=1, source_target_pairs={{4,0},{6,2},{8,12},{10,14},{5,1},{7,3},{9,13},{11,15},{20,16},{22,... | collective-permute-start | bytes 1572872 | tf_op jit(solution)/shard_map/ppermute | solution.py:230
  54.0 42.5 %collective-permute-start.11 = (bf16[2048,128]{1,0:T(8,128)(2,1)}, bf16[2048,128]{1,0:T(8,128)(2,1)}, u32[]{:S(2)}, u32[]{:S(2)}) collective-permute-start(bf16[2048,128]{1,0:T(8,128)(2,1)} %collective-permute-done.refs_1_), channel_id=1, source_target_pairs={{0,16},{16,0},{1,17},{17,1},{2,18},{18,2},{3,19},{19,3},{4,20},{20... | collective-permute-start | bytes 1572872 | tf_op jit(solution)/shard_map/ppermute | solution.py:233
  55.5 41.0 %collective-permute-start.12 = (bf16[2048,128]{1,0:T(8,128)(2,1)}, bf16[2048,128]{1,0:T(8,128)(2,1)}, u32[]{:S(2)}, u32[]{:S(2)}) collective-permute-start(bf16[2048,128]{1,0:T(8,128)(2,1)} %collective-permute-done.4.refs_5_), channel_id=1, source_target_pairs={{0,16},{16,0},{1,17},{17,1},{2,18},{18,2},{3,19},{19,3},{4,20},{20... | collective-permute-start | bytes 1572872 | tf_op jit(solution)/shard_map/ppermute | solution.py:233
  56.4 3.4 %copy-start.1 = (bf16[1024,4096]{1,0:T(8,128)(2,1)S(1)}, bf16[1024,4096]{1,0:T(8,128)(2,1)}, u32[]{:S(2)}) copy-start(bf16[1024,4096]{1,0:T(8,128)(2,1)} %tokens_ref.9) | copy-start | bytes 25165828
  64.1 1.4 copy-start.3
  65.5 24.8 %copy-start.6 = (bf16[2048,128]{1,0:T(8,128)(2,1)}, bf16[2048,128]{1,0:T(8,128)(2,1)S(1)}, u32[]{:S(2)}) copy-start(bf16[2048,128]{1,0:T(8,128)(2,1)S(1)} %collective-permute-done.10.refs_1_) | copy-start | bytes 1572868
  83.3 26.9 %collective-permute-start.15 = (bf16[2048,128]{1,0:T(8,128)(2,1)}, bf16[2048,128]{1,0:T(8,128)(2,1)}, u32[]{:S(2)}, u32[]{:S(2)}) collective-permute-start(bf16[2048,128]{1,0:T(8,128)(2,1)} %broadcast_select_fusion.refs_0_), channel_id=1, source_target_pairs={{0,2},{2,0},{4,6},{6,4},{8,10},{10,8},{12,14},{14,12},{1,3},{3,1},... | collective-permute-start | bytes 1572872 | tf_op jit(solution)/shard_map/ppermute | solution.py:230
  89.7 20.4 %collective-permute-start.13 = (bf16[2048,128]{1,0:T(8,128)(2,1)}, bf16[2048,128]{1,0:T(8,128)(2,1)}, u32[]{:S(2)}, u32[]{:S(2)}) collective-permute-start(bf16[2048,128]{1,0:T(8,128)(2,1)} %broadcast_select_fusion.refs_0_), channel_id=1, source_target_pairs={{0,16},{16,0},{1,17},{17,1},{2,18},{18,2},{3,19},{19,3},{4,20},{20... | collective-permute-start | bytes 1572872 | tf_op jit(solution)/shard_map/ppermute | solution.py:233
  90.3 19.9 %collective-permute-start.14 = (bf16[2048,128]{1,0:T(8,128)(2,1)}, bf16[2048,128]{1,0:T(8,128)(2,1)}, u32[]{:S(2)}, u32[]{:S(2)}) collective-permute-start(bf16[2048,128]{1,0:T(8,128)(2,1)} %collective-permute-done.9.refs_2_), channel_id=1, source_target_pairs={{0,16},{16,0},{1,17},{17,1},{2,18},{18,2},{3,19},{19,3},{4,20},{20... | collective-permute-start | bytes 1572872 | tf_op jit(solution)/shard_map/ppermute | solution.py:233
  92.1 51.9 %all-to-all-start.3 = ((bf16[8,32,4096]{2,1,0:T(8,128)(2,1)}), bf16[8,32,4096]{2,1,0:T(8,128)(2,1)}, u32[]{:S(2)}, u32[]{:S(2)}) async-start(bf16[8,32,4096]{2,1,0:T(8,128)(2,1)} %bitcast.37), calls=%async_computation.3 | async-start | bytes 4194304 | tf_op jit(solution)/shard_map/all_to_all | solution.py:161
  110.2 11.0 %collective-permute-start.17 = (bf16[2048,128]{1,0:T(8,128)(2,1)}, bf16[2048,128]{1,0:T(8,128)(2,1)}, u32[]{:S(2)}, u32[]{:S(2)}) collective-permute-start(bf16[2048,128]{1,0:T(8,128)(2,1)} %collective-permute-done.15.refs_2_), channel_id=1, source_target_pairs={{0,16},{16,0},{1,17},{17,1},{2,18},{18,2},{3,19},{19,3},{4,20},{20... | collective-permute-start | bytes 1572872 | tf_op jit(solution)/shard_map/ppermute | solution.py:233
  110.9 3.4 %copy-start.2 = (bf16[1024,4096]{1,0:T(8,128)(2,1)S(1)}, bf16[1024,4096]{1,0:T(8,128)(2,1)}, u32[]{:S(2)}) copy-start(bf16[1024,4096]{1,0:T(8,128)(2,1)} %tokens_ref.9) | copy-start | bytes 25165828
  114.2 1.0 copy-start.5
  115.3 1.0 copy-start.7
  121.2 5.1 %copy-start.8 = (f32[1024,512]{1,0:T(8,128)S(1)}, f32[1024,512]{1,0:T(8,128)}, u32[]{:S(2)}) copy-start(f32[1024,512]{1,0:T(8,128)} %weight_product.3) | copy-start | bytes 6291460
  126.8 7.5 %collective-permute-start.18 = (f32[1024,512]{1,0:T(8,128)S(1)}, f32[1024,512]{1,0:T(8,128)S(1)}, u32[]{:S(2)}, u32[]{:S(2)}) collective-permute-start(f32[1024,512]{1,0:T(8,128)S(1)} %fusion), channel_id=1, source_target_pairs={{0,1},{1,0},{2,3},{3,2},{4,5},{5,4},{6,7},{7,6},{8,9},{9,8},{10,11... | collective-permute-start | bytes 6291464 | tf_op jit(solution)/shard_map/ppermute | solution.py:329
  130.0 3.1 %copy-start.9 = (bf16[1024,512]{1,0:T(8,128)(2,1)S(1)}, bf16[1024,512]{1,0:T(8,128)(2,1)}, u32[]{:S(2)}) copy-start(bf16[1024,512]{1,0:T(8,128)(2,1)} %param.11) | copy-start | bytes 3145732
  130.0 2.8 %collective-permute-start.16 = (f32[256,1024]{1,0:T(8,128)S(1)}, f32[256,1024]{1,0:T(8,128)S(1)}, u32[]{:S(2)}, u32[]{:S(2)}) collective-permute-start(f32[256,1024]{1,0:T(8,128)S(1)} %hidden_product.1), channel_id=1, source_target_pairs={{0,1},{1,0},{2,3},{3,2},{4,5},{5,4},{6,7},{7,6},{8,9},{9,8},{10,11... | collective-permute-start | bytes 3145736 | tf_op jit(solution)/shard_map/ppermute | solution.py:180
  144.0 12.7 %all-to-all-start.4 = ((bf16[8,32,512]{2,1,0:T(8,128)(2,1)}), bf16[8,32,512]{2,1,0:T(8,128)(2,1)S(1)}, u32[]{:S(2)}, u32[]{:S(2)}) async-start(bf16[8,32,512]{2,1,0:T(8,128)(2,1)} %bitcast.20), calls=%async_computation.4 | async-start | bytes 524288 | tf_op jit(solution)/shard_map/all_to_all | solution.py:161
